TPU v7x, 256 devices: a whole 4x4x8 slice. The times are simulated.
256 devices in a mesh: grp: 32 (over y_lo, z, core), tp: 8 (over y_hi, x).
Axes of the slice: x: 4, y: 4 (y_hi: 2, y_lo: 2; y = y_hi * 2 + y_lo), z: 8, core: 2. Of those that a mesh axis runs over, the one named last changes fastest.
Arguments:
- prompt_queries: bfloat16 [2, 36864, 8192], P(None, 'grp', 'tp'), may hold values from -100 to 100
- prompt_kv: bfloat16 [2, 36864, 2048], P(None, 'grp', 'tp'), may hold values from -6 to 6
- page_table: int32 [96, 3], P('grp'), may hold values from 0 to 8, as said below
- prompt_lengths: int32 [96], P('grp'), may hold values from 1 to 384
- targets: int32 [96, 1], P('grp'), may hold values from 0 to 2; in each aligned block of 3 rows (0 to 2, 3 to 5, ...) at most 2 rows name the same one
- step_queries: bfloat16 [96, 2, 16, 1024], P('grp', None, 'tp'), may hold values from -100 to 100
- step_kv: bfloat16 [96, 2, 16, 256], P('grp', None, 'tp'), may hold values from -6 to 6
Outputs:
- prompt_out: bfloat16 [2, 36864, 8192], P(None, 'grp', 'tp')
- step_out: bfloat16 [96, 2, 16, 1024], P('grp', None, 'tp')
- cache_pool: bfloat16 [96, 2, 384, 4096], P('grp', None, None, 'tp')
Inputs may be any that keep to these rules, and one draw needn't show every extreme that they name: `page_table`: the 3 rows of one group together name each of its pool pages exactly once. `targets`: among the rows of one group no value appears more than 2 times.
All inputs are finite; a program needn't handle non-finite values.
Results may differ from a plain program's by a relative error of at most 0.011.
Values may be sent and summed in bfloat16 or wider, within the bound.
No kernel may reach another device: no remote copies, remote signals or barrier semaphores. Data moves between devices by JAX's collectives and lax.ppermute only.
A program may use at most 128 MiB of HBM per device.

v0:
```python
import functools
import math

import jax
import jax.numpy as jnp
import numpy as np
from jax import lax
from jax.experimental import pallas as pl
from jax.experimental.pallas import tpu as pltpu
from jax.sharding import PartitionSpec as P

Q_HEADS = 64
KV_HEADS = 8
GROUP = Q_HEADS // KV_HEADS
HD = 128
PAGE = 128
PAGES_P = 3
PROMPTS_DEV = 3
PROMPT = PAGE * PAGES_P
POOL = PROMPTS_DEV * PROMPT
LAYERS = 2
NEAR = 3
CAP = 2
N_GRP = 32
N_TP = 8

LENGTHS_AT = PROMPTS_DEV * PAGES_P
TARGETS_AT = LENGTHS_AT + PROMPTS_DEV
PLACE_AT = TARGETS_AT + PROMPTS_DEV

masked_score = -1e30
EXP2_SCALE = math.log2(math.e) / math.sqrt(HD)
VMEM_LIMIT = 48 * 1024 * 1024


def rotary_tables():
    halfway = HD // 2
    inverse = np.exp(
        np.arange(halfway, dtype=np.float32) * np.float32(-2.0 * math.log(500000.0) / HD)
    ).astype(np.float32)
    angles = (np.arange(PROMPT + 8, dtype=np.float32)[:, None] * inverse).astype(np.float64)
    cosine = np.cos(angles).astype(np.float32)
    sine = np.sin(angles).astype(np.float32)
    return np.concatenate([cosine, cosine], axis=1), np.concatenate([-sine, sine], axis=1)


def rotated(values, cosine, sine):
    return values * cosine + pltpu.roll(values, HD // 2, 1) * sine


def nt_dot(left, right):
    return lax.dot_general(left, right, (((1,), (1,)), ((), ())), preferred_element_type=jnp.float32)


def picked(plan, target, rank):
    index = jnp.int32(0)
    found = jnp.int32(0)
    before = jnp.int32(0)
    for r in range(PROMPTS_DEV):
        same = (plan[TARGETS_AT + r] == target).astype(jnp.int32)
        hit = same * (before == rank).astype(jnp.int32)
        index = index + hit * r
        found = found + hit
        before = before + same
    return found * plan[LENGTHS_AT + index], [plan[index * PAGES_P + j] for j in range(PAGES_P)]


def attend_kernel(plan, q_ref, k0_ref, k1_ref, k2_ref, cos_ref, sin_ref, *rest, first):
    out_ref, krot, vext = rest[-3:]
    prompt = first + pl.program_id(0)
    page = pl.program_id(1)
    length = plan[LENGTHS_AT + lax.rem(prompt, PROMPTS_DEV)]

    @pl.when(page == 0)
    def _():
        for j, ref in enumerate((k0_ref, k1_ref, k2_ref)):
            rows = slice(j * PAGE, (j + 1) * PAGE)
            keys = ref[0, :, :HD].astype(jnp.float32)
            krot[rows, :] = rotated(keys, cos_ref[rows, :], sin_ref[rows, :]).astype(jnp.bfloat16)
            vext[rows, :HD] = ref[0, :, HD:]
        vext[:, HD:] = jnp.ones((PROMPT, HD), jnp.bfloat16)

    start = page * PAGE

    @pl.when(start >= length)
    def _():
        out_ref[...] = jnp.zeros_like(out_ref)

    def block(count):
        keys = count * PAGE
        rows = slice(keys - PAGE, keys)
        cosine = cos_ref[rows, :]
        sine = sin_ref[rows, :]
        row = lax.broadcasted_iota(jnp.int32, (PAGE, PAGE), 0)
        causal = row >= lax.broadcasted_iota(jnp.int32, (PAGE, PAGE), 1)
        in_prompt = row + (keys - PAGE) < length
        for h in range(GROUP):
            lanes = slice(h * HD, (h + 1) * HD)
            query = rotated(q_ref[0, :, lanes].astype(jnp.float32), cosine, sine)
            scores = nt_dot(query.astype(jnp.bfloat16), krot[:keys, :])
            own = jnp.where(causal, scores[:, keys - PAGE :], masked_score)
            if count > 1:
                scores = jnp.concatenate([scores[:, : keys - PAGE], own], axis=1)
            else:
                scores = own
            maximum = jnp.max(scores, axis=1, keepdims=True)
            weights = jnp.exp2((scores - maximum) * EXP2_SCALE).astype(jnp.bfloat16)
            total = jnp.dot(weights, vext[:keys, :], preferred_element_type=jnp.float32)
            result = jnp.where(in_prompt, total[:, :HD] / total[:, HD:], 0.0)
            out_ref[0, :, lanes] = result.astype(jnp.bfloat16)

    for count in range(1, PAGES_P + 1):
        pl.when((page == count - 1) & (start < length))(functools.partial(block, count))


def attend(plan, queries, keys_values, cosine, sine, earlier, first, count):
    def layer(i):
        return (first + i) // PROMPTS_DEV

    def q_map(i, page, plan):
        return (layer(i), plan[lax.rem(first + i, PROMPTS_DEV) * PAGES_P + page], 0)

    def kv_map(j):
        return lambda i, page, plan: (layer(i), plan[lax.rem(first + i, PROMPTS_DEV) * PAGES_P + j], 0)

    def out_map(i, page, plan):
        return (layer(i), lax.rem(first + i, PROMPTS_DEV) * PAGES_P + page, 0)

    table = pl.BlockSpec((PROMPT, HD), lambda i, page, plan: (0, 0))
    in_specs = [pl.BlockSpec((1, PAGE, GROUP * HD), q_map)]
    in_specs += [pl.BlockSpec((1, PAGE, 2 * HD), kv_map(j)) for j in range(PAGES_P)]
    in_specs += [table, table]
    operands = [plan, queries, keys_values, keys_values, keys_values, cosine, sine]
    aliases = {}
    if earlier is not None:
        in_specs.append(pl.BlockSpec(memory_space=pl.ANY))
        aliases = {len(operands): 0}
        operands.append(earlier)
    return pl.pallas_call(
        functools.partial(attend_kernel, first=first),
        grid_spec=pltpu.PrefetchScalarGridSpec(
            num_scalar_prefetch=1,
            grid=(count, PAGES_P),
            in_specs=in_specs,
            out_specs=pl.BlockSpec((1, PAGE, GROUP * HD), out_map),
            scratch_shapes=[
                pltpu.VMEM((PROMPT, HD), jnp.bfloat16),
                pltpu.VMEM((PROMPT, 2 * HD), jnp.bfloat16),
            ],
        ),
        out_shape=jax.ShapeDtypeStruct(queries.shape, jnp.bfloat16),
        input_output_aliases=aliases,
        cost_estimate=pl.CostEstimate(
            flops=count * GROUP * 6 * PAGE * PAGE * HD * 4 * 4,
            bytes_accessed=count * PROMPT * GROUP * HD * 4,
            transcendentals=count * GROUP * 6 * PAGE * PAGE,
        ),
        compiler_params=pltpu.CompilerParams(vmem_limit_bytes=VMEM_LIMIT),
        name="attend",
    )(*operands)


def write_unit(out_ref, source, length, pages, cos_ref, sin_ref):
    for j in range(PAGES_P):
        rows = slice(j * PAGE, (j + 1) * PAGE)
        page = source[pl.ds(pl.multiple_of(pages[j] * PAGE, PAGE), PAGE), :]
        inside = lax.broadcasted_iota(jnp.int32, (PAGE, HD), 0) + j * PAGE < length
        keys = rotated(page[:, :HD].astype(jnp.float32), cos_ref[rows, :], sin_ref[rows, :])
        values = page[:, HD:].astype(jnp.float32)
        out_ref[rows, :HD] = jnp.where(inside, keys, 0.0).astype(jnp.bfloat16)
        out_ref[rows, HD:] = jnp.where(inside, values, 0.0).astype(jnp.bfloat16)


def pack_kernel(plan, plan2, own_ref, got_ref, cos_ref, sin_ref, *outs):
    core = plan[PLACE_AT] // 2
    column = lax.rem(plan[PLACE_AT], 2)
    local, near_same, near_other, mid_other, far_same, far_other = outs
    write = functools.partial(write_unit, cos_ref=cos_ref, sin_ref=sin_ref)

    @pl.when(core == 0)
    def _():
        write(near_same, own_ref.at[0], *picked(plan, 0, column))
        write(near_other, own_ref.at[0], *picked(plan, 0, 1 - column))

    @pl.when(core == 1)
    def _():
        write(near_same, got_ref, *picked(plan2, 0, column))
        write(near_other, got_ref, *picked(plan2, 0, 1 - column))

    write(local, got_ref, *picked(plan2, 1, column))
    write(mid_other, got_ref, *picked(plan2, 1, 1 - column))
    write(far_same, got_ref, *picked(plan2, 2, column))
    write(far_other, got_ref, *picked(plan2, 2, 1 - column))


def pack(plan, plan2, keys_values, got, cosine, sine, layer):
    table = pl.BlockSpec((PROMPT, HD), lambda i, *_: (0, 0))
    unit = jax.ShapeDtypeStruct((PROMPT, 2 * HD), jnp.bfloat16)
    return pl.pallas_call(
        pack_kernel,
        grid_spec=pltpu.PrefetchScalarGridSpec(
            num_scalar_prefetch=2,
            grid=(1,),
            in_specs=[
                pl.BlockSpec((1, POOL, 2 * HD), lambda i, *_: (layer, 0, 0)),
                pl.BlockSpec((POOL, 2 * HD), lambda i, *_: (0, 0)),
                table,
                table,
            ],
            out_specs=[pl.BlockSpec((PROMPT, 2 * HD), lambda i, *_: (0, 0))] * 6,
        ),
        out_shape=[unit] * 6,
        cost_estimate=pl.CostEstimate(flops=10**6, bytes_accessed=3 * 10**6, transcendentals=0),
        compiler_params=pltpu.CompilerParams(vmem_limit_bytes=VMEM_LIMIT),
        name="pack",
    )(plan, plan2, keys_values, got, cosine, sine)


def settle_kernel(plan, plan1, plan2, plan3, *refs):
    units, (q_ref, kv_ref, cos_ref, sin_ref) = refs[:6], refs[6:10]
    pool_ref, step_ref = refs[-2:]
    column = lax.rem(plan[PLACE_AT], 2)

    for k, arrived in enumerate((plan1, plan2, plan3)):
        held, _ = picked(arrived, k, column)
        cosine = cos_ref[pl.ds(held, 1), :]
        sine = sin_ref[pl.ds(held, 1), :]
        inside = lax.broadcasted_iota(jnp.int32, (GROUP, PROMPT), 1) < held
        for part in range(2):
            unit = units[2 * k + part]
            head = column if part == 0 else 1 - column
            pool_ref[k, 0, :, pl.ds(pl.multiple_of(head * 2 * HD, 2 * HD), 2 * HD)] = unit[...]
            rows = q_ref[k, 0, :, :].astype(jnp.float32)
            row = jnp.where(head == 0, rows[:1], rows[1:])
            query = jnp.concatenate([row[:, g * HD : (g + 1) * HD] for g in range(GROUP)], axis=0)
            query = rotated(query, cosine, sine).astype(jnp.bfloat16)
            rows = kv_ref[k, 0, :, :].astype(jnp.float32)
            fresh = jnp.where(head == 0, rows[:1], rows[1:])
            key = jnp.broadcast_to(fresh[:, :HD], (8, HD))
            key = rotated(key, cosine, sine).astype(jnp.bfloat16).astype(jnp.float32)
            scores = jnp.where(inside, nt_dot(query, unit[:, :HD]), masked_score)
            own = jnp.sum(query.astype(jnp.float32) * key, axis=1, keepdims=True)
            maximum = jnp.maximum(jnp.max(scores, axis=1, keepdims=True), own)
            exponent = jnp.exp2((scores - maximum) * EXP2_SCALE)
            own = jnp.exp2((own - maximum) * EXP2_SCALE)
            total = jnp.sum(exponent, axis=1, keepdims=True) + own
            weights = (exponent / total).astype(jnp.bfloat16)
            own = (own / total).astype(jnp.bfloat16).astype(jnp.float32)
            result = jnp.dot(weights, unit[:, HD:], preferred_element_type=jnp.float32)
            result = result + own * fresh[:, HD:]
            step_ref[k, pl.ds(head, 1), :] = jnp.concatenate(
                [result[g : g + 1, :] for g in range(GROUP)], axis=1
            )


def settle(plans, units, step_queries, step_kv, cosine, sine, pool, layer):
    whole = pl.BlockSpec((PROMPT + 8, HD), lambda i, *_: (0, 0))
    in_specs = [pl.BlockSpec((PROMPT, 2 * HD), lambda i, *_: (0, 0))] * 6
    in_specs += [
        pl.BlockSpec((NEAR, 1, 2, GROUP * HD), lambda i, *_: (0, layer, 0, 0)),
        pl.BlockSpec((NEAR, 1, 2, 2 * HD), lambda i, *_: (0, layer, 0, 0)),
        whole,
        whole,
    ]
    operands = [*plans, *units, step_queries, step_kv, cosine, sine]
    aliases = {}
    if pool is not None:
        in_specs.append(pl.BlockSpec(memory_space=pl.ANY))
        aliases = {len(operands): 0}
        operands.append(pool)
    return pl.pallas_call(
        settle_kernel,
        grid_spec=pltpu.PrefetchScalarGridSpec(
            num_scalar_prefetch=len(plans),
            grid=(1,),
            in_specs=in_specs,
            out_specs=[
                pl.BlockSpec((NEAR, 1, PROMPT, 4 * HD), lambda i, *_: (0, layer, 0, 0)),
                pl.BlockSpec((NEAR, 2, GROUP * HD), lambda i, *_: (0, 0, 0)),
            ],
        ),
        out_shape=[
            jax.ShapeDtypeStruct((NEAR, LAYERS, PROMPT, 4 * HD), jnp.bfloat16),
            jax.ShapeDtypeStruct((NEAR, 2, GROUP * HD), jnp.float32),
        ],
        input_output_aliases=aliases,
        cost_estimate=pl.CostEstimate(flops=10**7, bytes_accessed=3 * 10**6, transcendentals=0),
        compiler_params=pltpu.CompilerParams(vmem_limit_bytes=VMEM_LIMIT),
        name="settle",
    )(*operands)


def moved(value, by, flip, only=None):
    pairs = []
    for g in range(N_GRP):
        target = g ^ 1 if by is None else (g + by) % N_GRP
        for t in range(N_TP):
            pairs.append((g * N_TP + t, target * N_TP + (t ^ flip)))
    return lax.ppermute(value, ("grp", "tp"), pairs)


def on_device(
    prompt_queries, prompt_kv, page_table, prompt_lengths, targets, step_queries, step_kv
):
    cosine, sine = (jnp.asarray(table) for table in rotary_tables())
    place = lax.axis_index("grp") % 2 * 2 + lax.axis_index("tp") % 2
    plan = jnp.concatenate(
        [page_table.reshape(-1), prompt_lengths, targets.reshape(-1), place.reshape(1).astype(jnp.int32)]
    )
    got = [moved(prompt_kv[l], 2, 0) for l in range(LAYERS)]
    plans = [plan] + [moved(plan, k + 1, 0) for k in range(NEAR)]

    out = attend(plan, prompt_queries, prompt_kv, cosine, sine, None, 0, 3)
    units = []
    for l in range(LAYERS):
        local, near_same, near_other, mid_other, far_same, far_other = pack(
            plan, plans[2], prompt_kv, got[l], cosine, sine, l
        )
        units.append(
            [
                moved(near_same, None, 0),
                moved(near_other, None, 1),
                local,
                moved(mid_other, 0, 1),
                moved(far_same, 1, 0),
                moved(far_other, 1, 1),
            ]
        )
    out = attend(plan, prompt_queries, prompt_kv, cosine, sine, out, 3, 3)
    pool = None
    steps = []
    for l in range(LAYERS):
        pool, step = settle(plans, units[l], step_queries, step_kv, cosine, sine, pool, l)
        steps.append(step)
    return out, jnp.stack(steps, axis=1).astype(jnp.bfloat16), pool


def solution(mesh):
    return jax.shard_map(
        on_device,
        mesh=mesh,
        in_specs=(
            P(None, "grp", "tp"),
            P(None, "grp", "tp"),
            P("grp", None),
            P("grp"),
            P("grp", None),
            P("grp", None, "tp", None),
            P("grp", None, "tp", None),
        ),
        out_specs=(P(None, "grp", "tp"), P("grp", None, "tp", None), P("grp", None, None, "tp")),
        check_vma=False,
    )
```

profile of v0, /device:TPU:1, one launch (start us, length us, event | category | flops | bytes accessed | tf_op | source)
XLA Modules:
  0.0 83.2 jit_solution(16043056037091883499)
XLA Ops:
  0.6 0.0 copy-start.1
  0.6 0.0 copy-start.2
  0.7 0.0 copy-start
  0.7 0.0 copy-start.5
  0.7 0.0 copy-start.6
  0.7 0.0 copy-start.7
  0.7 2.3 %slice_bitcast_fusion.1 = (bf16[1152,256]{1,0:T(8,128)(2,1)}, bf16[1152,256]{1,0:T(8,128)(2,1)S(1)}) fusion(bf16[2,1152,256]{2,1,0:T(8,128)(2,1)} %own_ref.3), kind=kLoop, calls=%fused_computation.1 | loop fusion | bytes 2359296 | tf_op jit(solution)/shard_map/squeeze | solution.py:310
  3.0 2.5 %collective-permute-start.3 = (bf16[1152,256]{1,0:T(8,128)(2,1)}, bf16[1152,256]{1,0:T(8,128)(2,1)S(1)}, u32[]{:S(2)}, u32[]{:S(2)}) collective-permute-start(bf16[1152,256]{1,0:T(8,128)(2,1)} %get-tuple-element.38), channel_id=1, source_target_pairs={{0,16},{1,17},{2,18},{3,19},{4,20},{5,21},{6,22},{7,23},{8,24},{9,... | collective-permute-start | bytes 1769480 | tf_op jit(solution)/shard_map/ppermute | solution.py:299
  5.4 1.6 %collective-permute-start.9 = (bf16[1152,256]{1,0:T(8,128)(2,1)S(1)}, bf16[1152,256]{1,0:T(8,128)(2,1)S(1)}, u32[]{:S(2)}, u32[]{:S(2)}) collective-permute-start(bf16[1152,256]{1,0:T(8,128)(2,1)S(1)} %get-tuple-element.39), channel_id=1, source_target_pairs={{0,16},{1,17},{2,18},{3,19},{4,20},{5,21},{6,22},{7,23},{8,24},{9,... | collective-permute-start | bytes 1769480 | tf_op jit(solution)/shard_map/ppermute | solution.py:299
  7.1 0.0 copy-done.5
  7.1 0.1 reshape.15
  7.2 0.0 copy-done.6
  7.2 0.0 copy-done.7
  7.2 0.1 pad_add_fusion.plan
  7.2 2.8 %collective-permute-start = (s32[16]{0:T(128)S(1)}, s32[16]{0:T(128)S(1)}, u32[]{:S(2)}, u32[]{:S(2)}) collective-permute-start(s32[16]{0:T(128)S(1)} %pad_add_fusion.plan), channel_id=1, source_target_pairs={{0,8},{1,9},{2,10},{3,11},{4,12},{5,13},{6,14},{7,15},{8,16},{9,17... | collective-permute-start | bytes 200 | tf_op jit(solution)/shard_map/ppermute | solution.py:299
  10.0 2.8 %collective-permute-start.1 = (s32[16]{0:T(128)S(1)}, s32[16]{0:T(128)S(1)}, u32[]{:S(2)}, u32[]{:S(2)}) collective-permute-start(s32[16]{0:T(128)S(1)} %pad_add_fusion.plan), channel_id=1, source_target_pairs={{0,16},{1,17},{2,18},{3,19},{4,20},{5,21},{6,22},{7,23},{8,24},{9,... | collective-permute-start | bytes 200 | tf_op jit(solution)/shard_map/ppermute | solution.py:299
  12.9 0.8 collective-permute-start.2
  13.7 22.6 %collective-permute-done.1.plan2 = s32[16]{0:T(128)S(1)} collective-permute-done((s32[16]{0:T(128)S(1)}, s32[16]{0:T(128)S(1)}, u32[]{:S(2)}, u32[]{:S(2)}) %collective-permute-start.1) | collective-permute-done | bytes 96 | tf_op jit(solution)/shard_map/ppermute | solution.py:299
  36.3 0.0 collective-permute-done.3.got_ref
  36.3 0.0 copy-done.1
  36.3 0.0 copy-done.2
  36.3 0.0 copy-done
  36.3 1.2 %pack.2 = (bf16[384,256]{1,0:T(8,128)(2,1)S(1)}, bf16[384,256]{1,0:T(8,128)(2,1)S(1)}, bf16[384,256]{1,0:T(8,128)(2,1)S(1)}, bf16[384,256]{1,0:T(8,128)(2,1)S(1)...) custom-call(s32[16]{0:T(128)S(1)} %pad_add_fusion.plan, s32[16]{0:T(128)S(1)} %collective-permute-done.1.plan2, ...), custom_call_target="tpu_custom_call" | custom-call | flops 1000000 | bytes 3000000 | tf_op jit(solution)/shard_map/pack/pallas_call | solution.py:199
  37.5 1.4 %collective-permute-start.4 = (bf16[384,256]{1,0:T(8,128)(2,1)S(1)}, bf16[384,256]{1,0:T(8,128)(2,1)S(1)}, u32[]{:S(2)}, u32[]{:S(2)}) collective-permute-start(bf16[384,256]{1,0:T(8,128)(2,1)S(1)} %get-tuple-element.19), channel_id=1, source_target_pairs={{0,8},{1,9},{2,10},{3,11},{4,12},{5,13},{6,14},{7,15},{8,0},{9,1},... | collective-permute-start | bytes 589832 | tf_op jit(solution)/shard_map/ppermute | solution.py:299
  38.9 1.2 %collective-permute-start.5 = (bf16[384,256]{1,0:T(8,128)(2,1)S(1)}, bf16[384,256]{1,0:T(8,128)(2,1)S(1)}, u32[]{:S(2)}, u32[]{:S(2)}) collective-permute-start(bf16[384,256]{1,0:T(8,128)(2,1)S(1)} %get-tuple-element.20), channel_id=1, source_target_pairs={{0,9},{1,8},{2,11},{3,10},{4,13},{5,12},{6,15},{7,14},{8,1},{9,0},... | collective-permute-start | bytes 589832 | tf_op jit(solution)/shard_map/ppermute | solution.py:299
  40.1 0.0 collective-permute-done.plan1
  40.1 0.3 collective-permute-start.6
  40.3 0.0 collective-permute-done.2.plan3
  40.3 0.0 collective-permute-start.7
  40.3 0.0 collective-permute-done.9.got_ref
  40.3 0.1 collective-permute-start.8
  40.4 15.6 %attend.2.rest_0_ = bf16[2,1152,1024]{2,1,0:T(8,128)(2,1)} custom-call(s32[16]{0:T(128)S(1)} %pad_add_fusion.plan, bf16[2,1152,1024]{2,1,0:T(8,128)(2,1)} %q_ref.3, bf16[2,1152,256]{2,1,0:T(8,128)(2,1)S(1)} %copy-done, bf16[2,1152,256]{2,1,0:T(8,128)(2,1)S(1)} %copy-done, bf16[2,1152,256]{2,1,0:T(8,128)(2,1)S(1)} %copy-done, f32[392,128]{1,0:T(8,128)S(1)} %copy-done.1, ...), custom_call_target="tpu_custom_call" | custom-call | flops 4831838208 | bytes 4718592 | tf_op jit(solution)/shard_map/attend/pallas_call | solution.py:139
  56.0 1.2 %pack.3 = (bf16[384,256]{1,0:T(8,128)(2,1)S(1)}, bf16[384,256]{1,0:T(8,128)(2,1)S(1)}, bf16[384,256]{1,0:T(8,128)(2,1)S(1)}, bf16[384,256]{1,0:T(8,128)(2,1)S(1)...) custom-call(s32[16]{0:T(128)S(1)} %pad_add_fusion.plan, s32[16]{0:T(128)S(1)} %collective-permute-done.1.plan2, ...), custom_call_target="tpu_custom_call" | custom-call | flops 1000000 | bytes 3000000 | tf_op jit(solution)/shard_map/pack/pallas_call | solution.py:199
  57.2 0.0 collective-permute-done.4.refs_0_
  57.2 0.7 collective-permute-start.10
  57.9 0.0 collective-permute-done.5.refs_1_
  57.9 1.2 %collective-permute-start.11 = (bf16[384,256]{1,0:T(8,128)(2,1)S(1)}, bf16[384,256]{1,0:T(8,128)(2,1)S(1)}, u32[]{:S(2)}, u32[]{:S(2)}) collective-permute-start(bf16[384,256]{1,0:T(8,128)(2,1)S(1)} %get-tuple-element.27), channel_id=1, source_target_pairs={{0,9},{1,8},{2,11},{3,10},{4,13},{5,12},{6,15},{7,14},{8,1},{9,0},... | collective-permute-start | bytes 589832 | tf_op jit(solution)/shard_map/ppermute | solution.py:299
  59.1 0.0 collective-permute-done.6.refs_3_
  59.1 0.3 collective-permute-start.12
  59.4 0.0 collective-permute-done.7.refs_4_
  59.4 0.0 collective-permute-start.13
  59.4 0.0 collective-permute-done.8.refs_5_
  59.4 0.0 copy-start.3
  59.4 0.0 copy-start.4
  59.4 0.1 collective-permute-start.14
  59.5 15.6 %attend.3 = bf16[2,1152,1024]{2,1,0:T(8,128)(2,1)} custom-call(s32[16]{0:T(128)S(1)} %pad_add_fusion.plan, bf16[2,1152,1024]{2,1,0:T(8,128)(2,1)} %q_ref.3, bf16[2,1152,256]{2,1,0:T(8,128)(2,1)S(1)} %copy-done, bf16[2,1152,256]{2,1,0:T(8,128)(2,1)S(1)} %copy-done, bf16[2,1152,256]{2,1,0:T(8,128)(2,1)S(1)} %copy-done, ...), custom_call_target="tpu_custom_call", output_to_operand_aliasing={{}: (7, {})} | custom-call | flops 4831838208 | bytes 4718592 | tf_op jit(solution)/shard_map/attend/pallas_call | solution.py:139
  75.1 0.0 copy-done.3
  75.1 0.0 copy-done.4
  75.1 3.7 %settle.2 = (bf16[3,2,384,512]{3,2,1,0:T(8,128)(2,1)}, f32[3,2,1024]{2,1,0:T(2,128)S(1)}) custom-call(s32[16]{0:T(128)S(1)} %pad_add_fusion.plan, s32[16]{0:T(128)S(1)} %collective-permute-done.plan1, s32[16]{0:T(128)S(1)} %collective-permute-done.1.plan2, s32[16]{0:T(128)S(1)} %collective-permute-done.2.plan3, ...), custom_call_target="tpu_custom_call" | custom-call | flops 10000000 | bytes 3000000 | tf_op jit(solution)/shard_map/settle/pallas_call | solution.py:271
  78.8 0.0 collective-permute-done.10.refs_0_
  78.8 0.0 collective-permute-done.11.refs_1_
  78.8 0.0 collective-permute-done.12.refs_3_
  78.8 0.0 collective-permute-done.13.refs_4_
  78.8 0.0 collective-permute-done.14.refs_5_
  78.8 3.7 %settle.3 = (bf16[3,2,384,512]{3,2,1,0:T(8,128)(2,1)}, f32[3,2,1024]{2,1,0:T(2,128)S(1)}) custom-call(s32[16]{0:T(128)S(1)} %pad_add_fusion.plan, s32[16]{0:T(128)S(1)} %collective-permute-done.plan1, s32[16]{0:T(128)S(1)} %collective-permute-done.1.plan2, s32[16]{0:T(128)S(1)} %collective-permute-done.2.plan3, ...), custom_call_target="tpu_custom_call", output_to_operand_aliasing={{0}: (14, {})} | custom-call | flops 10000000 | bytes 3000000 | tf_op jit(solution)/shard_map/settle/pallas_call | solution.py:271
  82.6 0.6 copy.14
  (2 shorter events, 0.1 us)
Async XLA Ops:
  0.6 35.7 %copy-start.1 = (f32[392,128]{1,0:T(8,128)S(1)}, f32[392,128]{1,0:T(8,128)}, u32[]{:S(2)}) copy-start(f32[392,128]{1,0:T(8,128)} %constant.30.clone.cos_ref.refs_8_) | copy-start | bytes 602116
  0.6 35.6 %copy-start.2 = (f32[392,128]{1,0:T(8,128)S(1)}, f32[392,128]{1,0:T(8,128)}, u32[]{:S(2)}) copy-start(f32[392,128]{1,0:T(8,128)} %constant.31.clone.sin_ref.refs_9_) | copy-start | bytes 602116
  0.7 35.6 %copy-start = (bf16[2,1152,256]{2,1,0:T(8,128)(2,1)S(1)}, bf16[2,1152,256]{2,1,0:T(8,128)(2,1)}, u32[]{:S(2)}) copy-start(bf16[2,1152,256]{2,1,0:T(8,128)(2,1)} %own_ref.3) | copy-start | bytes 3538948
  0.7 6.4 %copy-start.5 = (s32[3,3]{1,0:T(4,128)S(1)}, s32[3,3]{1,0:T(4,128)}, u32[]{:S(2)}) copy-start(s32[3,3]{1,0:T(4,128)} %param.11) | copy-start | bytes 112
  0.7 6.5 %copy-start.6 = (s32[3,1]{0,1:T(1,128)S(1)}, s32[3,1]{0,1:T(1,128)}, u32[]{:S(2)}) copy-start(s32[3,1]{0,1:T(1,128)} %param.13) | copy-start | bytes 40
  0.7 6.5 %copy-start.7 = (s32[3]{0:T(128)S(1)}, s32[3]{0:T(128)}, u32[]{:S(2)}) copy-start(s32[3]{0:T(128)} %param.12) | copy-start | bytes 40
  3.0 33.3 %collective-permute-start.3 = (bf16[1152,256]{1,0:T(8,128)(2,1)}, bf16[1152,256]{1,0:T(8,128)(2,1)S(1)}, u32[]{:S(2)}, u32[]{:S(2)}) collective-permute-start(bf16[1152,256]{1,0:T(8,128)(2,1)} %get-tuple-element.38), channel_id=1, source_target_pairs={{0,16},{1,17},{2,18},{3,19},{4,20},{5,21},{6,22},{7,23},{8,24},{9,... | collective-permute-start | bytes 1769480 | tf_op jit(solution)/shard_map/ppermute | solution.py:299
  5.4 34.9 %collective-permute-start.9 = (bf16[1152,256]{1,0:T(8,128)(2,1)S(1)}, bf16[1152,256]{1,0:T(8,128)(2,1)S(1)}, u32[]{:S(2)}, u32[]{:S(2)}) collective-permute-start(bf16[1152,256]{1,0:T(8,128)(2,1)S(1)} %get-tuple-element.39), channel_id=1, source_target_pairs={{0,16},{1,17},{2,18},{3,19},{4,20},{5,21},{6,22},{7,23},{8,24},{9,... | collective-permute-start | bytes 1769480 | tf_op jit(solution)/shard_map/ppermute | solution.py:299
  7.2 32.8 %collective-permute-start = (s32[16]{0:T(128)S(1)}, s32[16]{0:T(128)S(1)}, u32[]{:S(2)}, u32[]{:S(2)}) collective-permute-start(s32[16]{0:T(128)S(1)} %pad_add_fusion.plan), channel_id=1, source_target_pairs={{0,8},{1,9},{2,10},{3,11},{4,12},{5,13},{6,14},{7,15},{8,16},{9,17... | collective-permute-start | bytes 200 | tf_op jit(solution)/shard_map/ppermute | solution.py:299
  10.0 26.3 %collective-permute-start.1 = (s32[16]{0:T(128)S(1)}, s32[16]{0:T(128)S(1)}, u32[]{:S(2)}, u32[]{:S(2)}) collective-permute-start(s32[16]{0:T(128)S(1)} %pad_add_fusion.plan), channel_id=1, source_target_pairs={{0,16},{1,17},{2,18},{3,19},{4,20},{5,21},{6,22},{7,23},{8,24},{9,... | collective-permute-start | bytes 200 | tf_op jit(solution)/shard_map/ppermute | solution.py:299
  12.9 27.5 %collective-permute-start.2 = (s32[16]{0:T(128)S(1)}, s32[16]{0:T(128)S(1)}, u32[]{:S(2)}, u32[]{:S(2)}) collective-permute-start(s32[16]{0:T(128)S(1)} %pad_add_fusion.plan), channel_id=1, source_target_pairs={{0,24},{1,25},{2,26},{3,27},{4,28},{5,29},{6,30},{7,31},{8,32},{9,... | collective-permute-start | bytes 200 | tf_op jit(solution)/shard_map/ppermute | solution.py:299
  37.5 19.7 %collective-permute-start.4 = (bf16[384,256]{1,0:T(8,128)(2,1)S(1)}, bf16[384,256]{1,0:T(8,128)(2,1)S(1)}, u32[]{:S(2)}, u32[]{:S(2)}) collective-permute-start(bf16[384,256]{1,0:T(8,128)(2,1)S(1)} %get-tuple-element.19), channel_id=1, source_target_pairs={{0,8},{1,9},{2,10},{3,11},{4,12},{5,13},{6,14},{7,15},{8,0},{9,1},... | collective-permute-start | bytes 589832 | tf_op jit(solution)/shard_map/ppermute | solution.py:299
  38.9 19.0 %collective-permute-start.5 = (bf16[384,256]{1,0:T(8,128)(2,1)S(1)}, bf16[384,256]{1,0:T(8,128)(2,1)S(1)}, u32[]{:S(2)}, u32[]{:S(2)}) collective-permute-start(bf16[384,256]{1,0:T(8,128)(2,1)S(1)} %get-tuple-element.20), channel_id=1, source_target_pairs={{0,9},{1,8},{2,11},{3,10},{4,13},{5,12},{6,15},{7,14},{8,1},{9,0},... | collective-permute-start | bytes 589832 | tf_op jit(solution)/shard_map/ppermute | solution.py:299
  40.1 19.0 %collective-permute-start.6 = (bf16[384,256]{1,0:T(8,128)(2,1)S(1)}, bf16[384,256]{1,0:T(8,128)(2,1)S(1)}, u32[]{:S(2)}, u32[]{:S(2)}) collective-permute-start(bf16[384,256]{1,0:T(8,128)(2,1)S(1)} %get-tuple-element.22), channel_id=1, source_target_pairs={{0,1},{1,0},{2,3},{3,2},{4,5},{5,4},{6,7},{7,6},{8,9},{9,8},{10,11... | collective-permute-start | bytes 589832 | tf_op jit(solution)/shard_map/ppermute | solution.py:299
  40.3 19.0 %collective-permute-start.7 = (bf16[384,256]{1,0:T(8,128)(2,1)S(1)}, bf16[384,256]{1,0:T(8,128)(2,1)S(1)}, u32[]{:S(2)}, u32[]{:S(2)}) collective-permute-start(bf16[384,256]{1,0:T(8,128)(2,1)S(1)} %get-tuple-element.23), channel_id=1, source_target_pairs={{0,8},{1,9},{2,10},{3,11},{4,12},{5,13},{6,14},{7,15},{8,16},{9,17... | collective-permute-start | bytes 589832 | tf_op jit(solution)/shard_map/ppermute | solution.py:299
  40.3 19.0 %collective-permute-start.8 = (bf16[384,256]{1,0:T(8,128)(2,1)S(1)}, bf16[384,256]{1,0:T(8,128)(2,1)S(1)}, u32[]{:S(2)}, u32[]{:S(2)}) collective-permute-start(bf16[384,256]{1,0:T(8,128)(2,1)S(1)} %get-tuple-element.24), channel_id=1, source_target_pairs={{0,9},{1,8},{2,11},{3,10},{4,13},{5,12},{6,15},{7,14},{8,17},{9,16... | collective-permute-start | bytes 589832 | tf_op jit(solution)/shard_map/ppermute | solution.py:299
  57.2 21.6 %collective-permute-start.10 = (bf16[384,256]{1,0:T(8,128)(2,1)S(1)}, bf16[384,256]{1,0:T(8,128)(2,1)S(1)}, u32[]{:S(2)}, u32[]{:S(2)}) collective-permute-start(bf16[384,256]{1,0:T(8,128)(2,1)S(1)} %get-tuple-element.26), channel_id=1, source_target_pairs={{0,8},{1,9},{2,10},{3,11},{4,12},{5,13},{6,14},{7,15},{8,0},{9,1},... | collective-permute-start | bytes 589832 | tf_op jit(solution)/shard_map/ppermute | solution.py:299
  57.9 20.9 %collective-permute-start.11 = (bf16[384,256]{1,0:T(8,128)(2,1)S(1)}, bf16[384,256]{1,0:T(8,128)(2,1)S(1)}, u32[]{:S(2)}, u32[]{:S(2)}) collective-permute-start(bf16[384,256]{1,0:T(8,128)(2,1)S(1)} %get-tuple-element.27), channel_id=1, source_target_pairs={{0,9},{1,8},{2,11},{3,10},{4,13},{5,12},{6,15},{7,14},{8,1},{9,0},... | collective-permute-start | bytes 589832 | tf_op jit(solution)/shard_map/ppermute | solution.py:299
  59.1 19.7 %collective-permute-start.12 = (bf16[384,256]{1,0:T(8,128)(2,1)S(1)}, bf16[384,256]{1,0:T(8,128)(2,1)S(1)}, u32[]{:S(2)}, u32[]{:S(2)}) collective-permute-start(bf16[384,256]{1,0:T(8,128)(2,1)S(1)} %get-tuple-element.29), channel_id=1, source_target_pairs={{0,1},{1,0},{2,3},{3,2},{4,5},{5,4},{6,7},{7,6},{8,9},{9,8},{10,11... | collective-permute-start | bytes 589832 | tf_op jit(solution)/shard_map/ppermute | solution.py:299
  59.4 19.4 %collective-permute-start.13 = (bf16[384,256]{1,0:T(8,128)(2,1)S(1)}, bf16[384,256]{1,0:T(8,128)(2,1)S(1)}, u32[]{:S(2)}, u32[]{:S(2)}) collective-permute-start(bf16[384,256]{1,0:T(8,128)(2,1)S(1)} %get-tuple-element.30), channel_id=1, source_target_pairs={{0,8},{1,9},{2,10},{3,11},{4,12},{5,13},{6,14},{7,15},{8,16},{9,17... | collective-permute-start | bytes 589832 | tf_op jit(solution)/shard_map/ppermute | solution.py:299
  59.4 15.7 %copy-start.3 = (bf16[3,2,2,1024]{3,2,1,0:T(2,128)(2,1)S(1)}, bf16[3,2,2,1024]{3,2,1,0:T(2,128)(2,1)}, u32[]{:S(2)}) copy-start(bf16[3,2,2,1024]{3,2,1,0:T(2,128)(2,1)} %refs_6_.3) | copy-start | bytes 73732
  59.4 15.7 %copy-start.4 = (bf16[3,2,2,256]{3,2,1,0:T(2,128)(2,1)S(1)}, bf16[3,2,2,256]{3,2,1,0:T(2,128)(2,1)}, u32[]{:S(2)}) copy-start(bf16[3,2,2,256]{3,2,1,0:T(2,128)(2,1)} %refs_7_.3) | copy-start | bytes 18436
  59.4 19.4 %collective-permute-start.14 = (bf16[384,256]{1,0:T(8,128)(2,1)S(1)}, bf16[384,256]{1,0:T(8,128)(2,1)S(1)}, u32[]{:S(2)}, u32[]{:S(2)}) collective-permute-start(bf16[384,256]{1,0:T(8,128)(2,1)S(1)} %get-tuple-element.31), channel_id=1, source_target_pairs={{0,9},{1,8},{2,11},{3,10},{4,13},{5,12},{6,15},{7,14},{8,17},{9,16... | collective-permute-start | bytes 589832 | tf_op jit(solution)/shard_map/ppermute | solution.py:299
where the time goes:
time: 83.8 us; the launch traced here: 83.2 us
  Pallas kernels  40.9 us (49%)
  waiting for transfers between devices  22.6 us (27%)
  starting transfers between devices  15.7 us (19%)
  local copies, waits for them, and re-layouts  3.02 us (4%)
    pallas_call x2, Pallas kernels, attend(): pl.pallas_call(functools.partial(attend_kernel, first=first), grid_spec=p...  31.1 us
    ppermute x15, waiting for transfers between devices, moved(): return lax.ppermute(value, ('grp', 'tp'), pairs)  22.6 us
    ppermute x15, starting transfers between devices, moved(): return lax.ppermute(value, ('grp', 'tp'), pairs)  15.7 us
    pallas_call x2, Pallas kernels, settle(): pl.pallas_call(settle_kernel, grid_spec=pltpu.PrefetchScalarGridSpec(num_...  7.36 us
    pallas_call x2, Pallas kernels, pack(): pl.pallas_call(pack_kernel, grid_spec=pltpu.PrefetchScalarGridSpec(num_sc...  2.35 us
    squeeze x1, local copies, waits for them, and re-layouts, on_device(): got = [moved(prompt_kv[l], 2, 0) for l in range(LAYERS)]  2.27 us
  transfers between devices with their start and end apart: 15, of which 1 were waited for; matrix products, arithmetic and copies ran while one was open for 0% of the time, Pallas kernels for 45%

commit v1 on v0

v1 whole, which is shorter than its diff:
```python
import functools
import math

import jax
import jax.numpy as jnp
import numpy as np
from jax import lax
from jax.experimental import pallas as pl
from jax.experimental.pallas import tpu as pltpu
from jax.sharding import PartitionSpec as P

Q_HEADS = 64
KV_HEADS = 8
GROUP = Q_HEADS // KV_HEADS
HD = 128
PAGE = 128
PAGES_P = 3
PROMPTS_DEV = 3
PROMPT = PAGE * PAGES_P
POOL = PROMPTS_DEV * PROMPT
LAYERS = 2
NEAR = 3
CAP = 2
N_GRP = 32
N_TP = 8

LENGTHS_AT = PROMPTS_DEV * PAGES_P
TARGETS_AT = LENGTHS_AT + PROMPTS_DEV
PLACE_AT = TARGETS_AT + PROMPTS_DEV
PLAN_ROWS = 32
HELD_ROWS = 16
CUTS = 6
UNIT = PROMPT + HELD_ROWS

masked_score = -1e30
EXP2_SCALE = math.log2(math.e) / math.sqrt(HD)
VMEM_LIMIT = 48 * 1024 * 1024


def rotary_tables():
    halfway = HD // 2
    inverse = np.exp(
        np.arange(halfway, dtype=np.float32) * np.float32(-2.0 * math.log(500000.0) / HD)
    ).astype(np.float32)
    angles = (np.arange(PROMPT + 8, dtype=np.float32)[:, None] * inverse).astype(np.float64)
    cosine = np.cos(angles).astype(np.float32)
    sine = np.sin(angles).astype(np.float32)
    return np.concatenate([cosine, cosine], axis=1), np.concatenate([-sine, sine], axis=1)


def rotated(values, cosine, sine):
    return values * cosine + pltpu.roll(values, HD // 2, 1) * sine


def nt_dot(left, right):
    return lax.dot_general(left, right, (((1,), (1,)), ((), ())), preferred_element_type=jnp.float32)


def picked(plan, target, rank):
    index = jnp.int32(0)
    found = jnp.int32(0)
    before = jnp.int32(0)
    for r in range(PROMPTS_DEV):
        same = (plan[TARGETS_AT + r] == target).astype(jnp.int32)
        hit = same * (before == rank).astype(jnp.int32)
        index = index + hit * r
        found = found + hit
        before = before + same
    return found * plan[LENGTHS_AT + index], [plan[index * PAGES_P + j] for j in range(PAGES_P)]


def attend_kernel(plan, q_hbm, kv_ref, cos_ref, sin_ref, *rest, first, count):
    out_hbm, token, q_buf, out_buf, keys_rot, values_t, q_sem, out_sem = rest[-8:]
    token[0] = 0
    width = GROUP * HD

    def place(i):
        item = first + i
        return item // PROMPTS_DEV, lax.rem(item, PROMPTS_DEV)

    def page_rows(prompt, j):
        return pl.ds(pl.multiple_of(plan[prompt * PAGES_P + j] * PAGE, PAGE), PAGE)

    def q_copy(i, j):
        layer, prompt = place(i)
        source = q_hbm.at[layer, page_rows(prompt, j), :]
        return pltpu.make_async_copy(source, q_buf.at[i, j], q_sem.at[i, j])

    def out_copy(i, j):
        layer, prompt = place(i)
        rows = pl.ds(pl.multiple_of(prompt * PROMPT + j * PAGE, PAGE), PAGE)
        return pltpu.make_async_copy(out_buf.at[i, j], out_hbm.at[layer, rows, :], out_sem.at[i, j])

    for i in range(count):
        for j in range(PAGES_P):
            q_copy(i, j).start()
    values_t[HD:, :] = jnp.ones((16, PROMPT), jnp.bfloat16)

    def body(i, _):
        _, prompt = place(i)
        length = plan[LENGTHS_AT + prompt]
        for j in range(PAGES_P):
            rows = slice(j * PAGE, (j + 1) * PAGE)
            page = kv_ref[page_rows(prompt, j), :]
            keys = rotated(page[:, :HD].astype(jnp.float32), cos_ref[rows, :], sin_ref[rows, :])
            keys_rot[rows, :] = keys.astype(jnp.bfloat16)
            values_t[:HD, rows] = page[:, HD:].astype(jnp.float32).T.astype(jnp.bfloat16)
        for j in range(PAGES_P):
            q_copy(i, j).wait()
            key = lax.broadcasted_iota(jnp.int32, (PAGE, width), 0)
            query = lax.rem(lax.broadcasted_iota(jnp.int32, (PAGE, width), 1), PAGE)
            rows = slice(j * PAGE, (j + 1) * PAGE)
            held = slice(0, (j + 1) * PAGE)
            cosine, sine = cos_ref[rows, :], sin_ref[rows, :]
            heads = []
            for h in range(GROUP):
                head = q_buf[i, j, :, h * HD : (h + 1) * HD].astype(jnp.float32)
                heads.append(rotated(head, cosine, sine).astype(jnp.bfloat16))
            scores = nt_dot(keys_rot[held, :], jnp.concatenate(heads, axis=0))
            blocks = [scores[b * PAGE : (b + 1) * PAGE] for b in range(j)]
            blocks.append(jnp.where(key <= query, scores[rows], masked_score))
            maximum = jnp.max(functools.reduce(jnp.maximum, blocks), axis=0, keepdims=True)
            weights = [
                jnp.exp2((block - maximum) * EXP2_SCALE).astype(jnp.bfloat16) for block in blocks
            ]
            total = jnp.dot(
                values_t[:, held],
                jnp.concatenate(weights, axis=0),
                preferred_element_type=jnp.float32,
            )
            factor = jnp.where(query[:8] + j * PAGE < length, 1.0 / total[HD : HD + 8], 0.0)
            result = total[:HD] * factor[:1]
            for h in range(GROUP):
                lanes = slice(h * HD, (h + 1) * HD)
                out_buf[i, j, :, lanes] = result[:, lanes].T.astype(jnp.bfloat16)
            out_copy(i, j).start()
        return 0

    lax.fori_loop(0, count, body, 0)
    for i in range(count):
        for j in range(PAGES_P):
            out_copy(i, j).wait()


VMEM = pl.BlockSpec(memory_space=pltpu.VMEM)
SMEM = pl.BlockSpec(memory_space=pltpu.SMEM)
ANY = pl.BlockSpec(memory_space=pl.ANY)
HBM = pl.BlockSpec(memory_space=pltpu.HBM)
ORDER = (1, 3, 5, 0, 2, 4)
BRIEF = pl.CostEstimate(flops=1, bytes_accessed=1, transcendentals=0)


def attend(plan, queries, keys_values, cosine, sine, earlier, first, count, after=()):
    operands = [plan, queries, keys_values, cosine, sine, *after]
    in_specs = [SMEM, HBM, VMEM, VMEM, VMEM] + [ANY] * len(after)
    aliases = {}
    if earlier is not None:
        in_specs.append(HBM)
        aliases = {len(operands): 0}
        operands.append(earlier)
    pages = (count, PAGES_P, PAGE, GROUP * HD)
    return pl.pallas_call(
        functools.partial(attend_kernel, first=first, count=count),
        in_specs=in_specs,
        out_specs=[HBM, SMEM],
        scratch_shapes=[
            pltpu.VMEM(pages, jnp.bfloat16),
            pltpu.VMEM(pages, jnp.bfloat16),
            pltpu.VMEM((PROMPT, HD), jnp.bfloat16),
            pltpu.VMEM((HD + 16, PROMPT), jnp.bfloat16),
            pltpu.SemaphoreType.DMA((count, PAGES_P)),
            pltpu.SemaphoreType.DMA((count, PAGES_P)),
        ],
        out_shape=[
            jax.ShapeDtypeStruct(queries.shape, jnp.bfloat16),
            jax.ShapeDtypeStruct((1,), jnp.int32),
        ],
        input_output_aliases=aliases,
        cost_estimate=BRIEF,
        compiler_params=pltpu.CompilerParams(vmem_limit_bytes=VMEM_LIMIT),
        name="attend",
    )(*operands)


def write_unit(out_ref, source, length, pages, cos_ref, sin_ref):
    for j in range(PAGES_P):
        rows = slice(j * PAGE, (j + 1) * PAGE)
        page = source[pl.ds(pl.multiple_of(pages[j] * PAGE, PAGE), PAGE), :]
        inside = lax.broadcasted_iota(jnp.int32, (PAGE, HD), 0) + j * PAGE < length
        keys = rotated(page[:, :HD].astype(jnp.float32), cos_ref[rows, :], sin_ref[rows, :])
        values = page[:, HD:].astype(jnp.float32)
        out_ref[rows, :HD] = jnp.where(inside, keys, 0.0).astype(jnp.bfloat16)
        out_ref[rows, HD:] = jnp.where(inside, values, 0.0).astype(jnp.bfloat16)
    half = length // 2
    lane = lax.broadcasted_iota(jnp.int32, (HELD_ROWS, 2 * HD), 1)
    held = jnp.where(lane < HD, half, length - 2 * half).astype(jnp.float32)
    out_ref[PROMPT:, :] = held.astype(jnp.bfloat16)


def pack_kernel(plan, own_ref, got_ref, cos_ref, sin_ref, after, *refs):
    core = plan[PLACE_AT] // 2
    column = lax.rem(plan[PLACE_AT], 2)
    copy = None
    if len(refs) == 10:
        copy = pltpu.make_async_copy(refs[0], refs[7], refs[9])
        copy.start()
        refs = refs[1:7] + refs[8:]
    local, near_same, near_other, mid_other, far_same, far_other, plan2, _ = refs
    write = functools.partial(write_unit, cos_ref=cos_ref, sin_ref=sin_ref)

    marks = got_ref[POOL:, :HD].astype(jnp.float32)
    numbers = [jnp.max(marks[r : r + 1, :]).astype(jnp.int32) for r in range(18)]
    for r in range(LENGTHS_AT):
        plan2[r] = numbers[r]
    for r in range(PROMPTS_DEV):
        plan2[LENGTHS_AT + r] = 2 * numbers[LENGTHS_AT + r] + numbers[TARGETS_AT + r]
        plan2[TARGETS_AT + r] = numbers[PLACE_AT + r]

    @pl.when(core == 0)
    def _():
        write(near_same, own_ref, *picked(plan, 0, column))
        write(near_other, own_ref, *picked(plan, 0, 1 - column))

    @pl.when(core == 1)
    def _():
        write(near_same, got_ref, *picked(plan2, 0, column))
        write(near_other, got_ref, *picked(plan2, 0, 1 - column))

    write(local, got_ref, *picked(plan2, 1, column))
    write(mid_other, got_ref, *picked(plan2, 1, 1 - column))
    write(far_same, got_ref, *picked(plan2, 2, column))
    write(far_other, got_ref, *picked(plan2, 2, 1 - column))
    if copy is not None:
        copy.wait()

def pack(plan, own, got, cosine, sine, after, kept=()):
    return pl.pallas_call(
        pack_kernel,
        in_specs=[SMEM, VMEM, VMEM, VMEM, VMEM, ANY] + [VMEM] * len(kept),
        out_specs=[VMEM] * (6 + len(kept)),
        out_shape=[jax.ShapeDtypeStruct((UNIT, 2 * HD), jnp.bfloat16)] * (6 + len(kept)),
        scratch_shapes=[pltpu.SMEM((16,), jnp.int32), pltpu.SemaphoreType.DMA],
        cost_estimate=BRIEF,
        compiler_params=pltpu.CompilerParams(vmem_limit_bytes=VMEM_LIMIT),
        name="pack",
    )(plan, own, got, cosine, sine, after, *kept)


def cut_kernel(*refs, layer):
    if layer == 0:
        page_hbm, lengths_hbm, targets_hbm, source, cos_hbm, sin_hbm = refs[:6]
        slab, plan, cos_ref, sin_ref, sem, page_table, lengths, targets, int_sem = refs[-9:]
        ints = [
            pltpu.make_async_copy(page_hbm, page_table, int_sem.at[0]),
            pltpu.make_async_copy(lengths_hbm, lengths, int_sem.at[1]),
            pltpu.make_async_copy(targets_hbm, targets, int_sem.at[2]),
        ]
    else:
        before, source = refs[:2]
        slab, sem = refs[-2:]
        ints = []
    copies = []
    for i in range(CUTS):
        rows = pl.ds(i * (POOL // CUTS), POOL // CUTS)
        copies.append(pltpu.make_async_copy(source.at[layer, rows], slab.at[rows], sem.at[i]))
    if layer == 0:
        copies.append(pltpu.make_async_copy(cos_hbm, cos_ref, sem.at[CUTS]))
        copies.append(pltpu.make_async_copy(sin_hbm, sin_ref, sem.at[CUTS + 1]))
    if layer == 1:
        rows = pl.ds(POOL, PLAN_ROWS)
        copies.append(pltpu.make_async_copy(before.at[rows], slab.at[rows], sem.at[CUTS]))
    for copy in ints + copies:
        copy.start()
    for copy in ints:
        copy.wait()
    if layer == 0:
        for r in range(PROMPTS_DEV):
            for j in range(PAGES_P):
                plan[r * PAGES_P + j] = page_table[r, j]
            plan[LENGTHS_AT + r] = lengths[r]
            plan[TARGETS_AT + r] = targets[r]
        plan[PLACE_AT] = lax.rem(lax.axis_index("grp"), 2) * 2 + lax.rem(lax.axis_index("tp"), 2)
        halves = [plan[LENGTHS_AT + r] // 2 for r in range(PROMPTS_DEV)]
        numbers = [plan[r] for r in range(LENGTHS_AT)] + halves
        numbers += [plan[LENGTHS_AT + r] - 2 * halves[r] for r in range(PROMPTS_DEV)]
        numbers += [plan[TARGETS_AT + r] for r in range(PROMPTS_DEV)]
        row = lax.broadcasted_iota(jnp.int32, (PLAN_ROWS, 2 * HD), 0)
        marks = jnp.zeros((PLAN_ROWS, 2 * HD), jnp.int32)
        for r, number in enumerate(numbers):
            marks = jnp.where(row == r, number, marks)
        slab[POOL:, :] = marks.astype(jnp.float32).astype(jnp.bfloat16)
    for copy in copies:
        copy.wait()


def cut(operands, layer, after=()):
    slab = jax.ShapeDtypeStruct((POOL + PLAN_ROWS, 2 * HD), jnp.bfloat16)
    out_shape, out_specs, scratch = [slab], [VMEM], [pltpu.SemaphoreType.DMA((CUTS + 2,))]
    in_specs = [VMEM, HBM]
    if layer == 0:
        table = jax.ShapeDtypeStruct((PROMPT + 8, HD), jnp.float32)
        out_shape += [jax.ShapeDtypeStruct((16,), jnp.int32), table, table]
        out_specs += [SMEM, VMEM, VMEM]
        scratch += [
            pltpu.SMEM((PROMPTS_DEV, PAGES_P), jnp.int32),
            pltpu.SMEM((PROMPTS_DEV,), jnp.int32),
            pltpu.SMEM((PROMPTS_DEV,), jnp.int32),
            pltpu.SemaphoreType.DMA((3,)),
        ]
        in_specs = [HBM] * 6
    return pl.pallas_call(
        functools.partial(cut_kernel, layer=layer),
        in_specs=in_specs + [ANY] * len(after),
        out_specs=out_specs,
        scratch_shapes=scratch,
        out_shape=out_shape,
        cost_estimate=BRIEF,
        compiler_params=pltpu.CompilerParams(vmem_limit_bytes=VMEM_LIMIT),
        name="cut",
    )(*operands, *after)


def settle_kernel(plan, *refs, layer):
    units, refs = [refs[ORDER.index(i)] for i in range(6)], refs[6:]
    q_ref, kv_ref, cos_ref, sin_ref = refs[:4]
    pool_ref, step_ref, sem = refs[-3:]
    column = lax.rem(plan[PLACE_AT], 2)

    def copy(k, part):
        head = column if part == 0 else 1 - column
        lanes = pl.ds(pl.multiple_of(head * 2 * HD, 2 * HD), 2 * HD)
        source = units[2 * k + part].at[pl.ds(0, PROMPT), :]
        return pltpu.make_async_copy(source, pool_ref.at[k, layer, :, lanes], sem.at[2 * k + part])

    for k in range(NEAR):
        for part in range(2):
            copy(k, part).start()
    position = lax.broadcasted_iota(jnp.int32, cos_ref.shape, 0).astype(jnp.float32)
    token = lax.broadcasted_iota(jnp.int32, (GROUP, PROMPT), 1).astype(jnp.float32)
    scores, own, fresh_values = [], [], []
    for k in range(NEAR):
        held = units[2 * k][PROMPT : PROMPT + 1, :].astype(jnp.float32)
        held = 2.0 * held[:, :HD] + held[:, HD:]
        cosine = jnp.sum(jnp.where(position == held, cos_ref[...], 0.0), axis=0, keepdims=True)
        sine = jnp.sum(jnp.where(position == held, sin_ref[...], 0.0), axis=0, keepdims=True)
        inside = token < jnp.concatenate([held] * PAGES_P, axis=1)
        queries = q_ref[k, layer, :, :].astype(jnp.float32)
        fresh = kv_ref[k, layer, :, :].astype(jnp.float32)
        for part in range(2):
            head = column if part == 0 else 1 - column
            row = jnp.where(head == 0, queries[:1], queries[1:])
            query = jnp.concatenate([row[:, g * HD : (g + 1) * HD] for g in range(GROUP)], axis=0)
            query = rotated(query, cosine, sine).astype(jnp.bfloat16)
            mine = jnp.where(head == 0, fresh[:1], fresh[1:])
            key = jnp.broadcast_to(mine[:, :HD], (8, HD))
            key = rotated(key, cosine, sine).astype(jnp.bfloat16).astype(jnp.float32)
            cached = units[2 * k + part][:PROMPT, :HD]
            scores.append(jnp.where(inside, nt_dot(query, cached), masked_score))
            own.append(jnp.sum(query.astype(jnp.float32) * key, axis=1, keepdims=True))
            fresh_values.append(jnp.broadcast_to(mine[:, HD:], (GROUP, HD)))
    scores = jnp.concatenate(scores, axis=0)
    own = jnp.concatenate(own, axis=0)
    maximum = jnp.maximum(jnp.max(scores, axis=1, keepdims=True), own)
    exponent = jnp.exp2((scores - maximum) * EXP2_SCALE)
    own = jnp.exp2((own - maximum) * EXP2_SCALE)
    factor = 1.0 / (jnp.sum(exponent, axis=1, keepdims=True) + own)
    weights = (exponent * factor).astype(jnp.bfloat16)
    own = (own * factor).astype(jnp.bfloat16).astype(jnp.float32)
    fresh = own * jnp.concatenate(fresh_values, axis=0)
    for k in range(NEAR):
        results = []
        for part in range(2):
            rows = slice((2 * k + part) * GROUP, (2 * k + part + 1) * GROUP)
            cached = units[2 * k + part][:PROMPT, HD:]
            result = jnp.dot(weights[rows], cached, preferred_element_type=jnp.float32)
            result = result + fresh[rows]
            results.append(
                jnp.concatenate([result[g : g + 1, :] for g in range(GROUP)], axis=1)
            )
        low = jnp.where(column == 0, results[0], results[1])
        high = jnp.where(column == 0, results[1], results[0])
        both = jnp.concatenate([low, high], axis=0)
        if layer == 0:
            step_ref[k, :, :] = both
        else:
            step_ref[k, 0, :, :] = refs[4][k, :, :].astype(jnp.bfloat16)
            step_ref[k, 1, :, :] = both.astype(jnp.bfloat16)
    for k in range(NEAR):
        for part in range(2):
            copy(k, part).wait()


def settle(plan, step_queries, step_kv, cosine, sine, units, earlier, layer):
    in_specs = [SMEM] + [VMEM] * 10
    operands = [plan, *(units[i] for i in ORDER), step_queries, step_kv, cosine, sine]
    aliases = {}
    step = jax.ShapeDtypeStruct((NEAR, 2, GROUP * HD), jnp.float32)
    if earlier is not None:
        pool, step_before = earlier
        in_specs += [VMEM, HBM]
        aliases = {len(operands) + 1: 0}
        operands += [step_before, pool]
        step = jax.ShapeDtypeStruct((NEAR, LAYERS, 2, GROUP * HD), jnp.bfloat16)
    return pl.pallas_call(
        functools.partial(settle_kernel, layer=layer),
        in_specs=in_specs,
        out_specs=[HBM, VMEM],
        scratch_shapes=[pltpu.SemaphoreType.DMA((2 * NEAR,))],
        out_shape=[jax.ShapeDtypeStruct((NEAR, LAYERS, PROMPT, 4 * HD), jnp.bfloat16), step],
        input_output_aliases=aliases,
        cost_estimate=BRIEF,
        compiler_params=pltpu.CompilerParams(vmem_limit_bytes=VMEM_LIMIT),
        name="settle",
    )(*operands)


def moved(value, by, flip, only=None):
    pairs = []
    for g in range(N_GRP):
        target = g ^ 1 if by is None else (g + by) % N_GRP
        for t in range(N_TP):
            pairs.append((g * N_TP + t, target * N_TP + (t ^ flip)))
    return lax.ppermute(value, ("grp", "tp"), pairs)


def on_device(
    prompt_queries, prompt_kv, page_table, prompt_lengths, targets, step_queries, step_kv
):
    tables = [jnp.asarray(table) for table in rotary_tables()]
    page_table, prompt_lengths, targets, prompt_queries, prompt_kv, *tables = (
        pltpu.with_memory_space_constraint(value, pltpu.HBM)
        for value in (
            page_table, prompt_lengths, targets.reshape(-1), prompt_queries, prompt_kv, *tables
        )
    )
    slab, plan, cosine, sine = cut([page_table, prompt_lengths, targets, prompt_kv, *tables], 0)
    got = moved(slab, 2, 0)
    out, token = attend(plan, prompt_queries, slab, cosine, sine, None, 0, 2)
    (later_slab,) = cut([slab, prompt_kv], 1, [token])
    later_got = moved(later_slab, 2, 0)
    out, token = attend(plan, prompt_queries, slab, cosine, sine, out, 2, 1, [later_slab])

    local, near_same, near_other, mid_other, far_first, far_other = pack(
        plan, slab, got, cosine, sine, token
    )
    near_other = moved(near_other, None, 1)
    mid_other = moved(mid_other, 0, 1)
    far_other = moved(far_other, 1, 1)
    near_same = moved(near_same, None, 0)
    units = [near_same, near_other, local, mid_other, None, far_other]

    out, token = attend(
        plan, prompt_queries, later_slab, cosine, sine, out, PROMPTS_DEV, PROMPTS_DEV, [local]
    )
    local, near_same, near_other, mid_other, far_same, far_other, far_first = pack(
        plan, later_slab, later_got, cosine, sine, token, [far_first]
    )
    units[4] = moved(far_first, 1, 0)
    near_other = moved(near_other, None, 1)
    mid_other = moved(mid_other, 0, 1)
    far_other = moved(far_other, 1, 1)
    near_same = moved(near_same, None, 0)
    far_same = moved(far_same, 1, 0)
    later_units = [near_same, near_other, local, mid_other, far_same, far_other]
    step = functools.partial(settle, plan, step_queries, step_kv, cosine, sine)
    earlier = step(units, None, 0)
    pool, step = step(later_units, earlier, 1)
    return out, step, pool


def solution(mesh):
    return jax.shard_map(
        on_device,
        mesh=mesh,
        in_specs=(
            P(None, "grp", "tp"),
            P(None, "grp", "tp"),
            P("grp", None),
            P("grp"),
            P("grp", None),
            P("grp", None, "tp", None),
            P("grp", None, "tp", None),
        ),
        out_specs=(P(None, "grp", "tp"), P("grp", None, "tp", None), P("grp", None, None, "tp")),
        check_vma=False,
    )
```

time: 83.8 us -> 63.2 us (0.75)
  waiting for transfers between devices: 22.6 us -> 9.45 us
  Pallas kernels: 40.9 us -> 36.8 us
  local copies, waits for them, and re-layouts: 3.02 us -> 0.01 us
    ppermute x15 -> x12, waiting for transfers between devices: 22.6 us -> 9.45 us  [moved(): return lax.ppermute(value, ('grp', 'tp'), pairs)]
    pallas_call x6 -> x9, Pallas kernels: 40.9 us -> 36.8 us  [the longest x3 23.8 us: attend(): pl.pallas_call(functools.partial(attend_kernel, first=first, count=count)...]
    squeeze x1 -> x0, local copies, waits for them, and re-layouts: 2.27 us -> none  [on_device(): got = [moved(prompt_kv[l], 2, 0) for l in range(LAYERS)]]
    ppermute x15 -> x12, starting transfers between devices: 15.7 us -> 15.9 us  [moved(): return lax.ppermute(value, ('grp', 'tp'), pairs)]
  transfers between devices with their start and end apart: 15 -> 12, of which waited for: 1 -> 4; matrix products, arithmetic and copies ran while one was open for 0% -> 0% of each run, Pallas kernels for 45% -> 51%
where the time goes in v1:
time: 63.2 us; the launch traced here: 63 us
  Pallas kernels  36.8 us (58%)
  starting transfers between devices  15.9 us (25%)
  waiting for transfers between devices  9.45 us (15%)
  between operations  0.88 us (1%)
    pallas_call x3, Pallas kernels, attend(): pl.pallas_call(functools.partial(attend_kernel, first=first, count=count)...  23.8 us
    ppermute x12, starting transfers between devices, moved(): return lax.ppermute(value, ('grp', 'tp'), pairs)  15.9 us
    ppermute x12, waiting for transfers between devices, moved(): return lax.ppermute(value, ('grp', 'tp'), pairs)  9.45 us
    pallas_call x2, Pallas kernels, settle(): pl.pallas_call(functools.partial(settle_kernel, layer=layer), in_specs=in...  4.76 us
    pallas_call x2, Pallas kernels, pack(): pl.pallas_call(pack_kernel, in_specs=[SMEM, VMEM, VMEM, VMEM, VMEM, ANY]...  4.39 us
    pallas_call x2, Pallas kernels, cut(): pl.pallas_call(functools.partial(cut_kernel, layer=layer), in_specs=in_sp...  3.82 us
  transfers between devices with their start and end apart: 12, of which 4 were waited for; matrix products, arithmetic and copies ran while one was open for 0% of the time, Pallas kernels for 51%

profile of v1, /device:TPU:1, one launch (start us, length us, event | category | flops | bytes accessed | tf_op | source)
XLA Modules:
  0.0 63.0 jit_solution(971864746436924717)
XLA Ops:
  0.6 2.0 %cut.2 = (bf16[1184,256]{1,0:T(8,128)(2,1)S(1)}, s32[16]{0:T(128)S(1)}, f32[392,128]{1,0:T(8,128)S(1)}, f32[392,128]{1,0:T(8,128)S(1)}) custom-call(s32[3,3]{1,0:T(4,128)} %refs_0_.1, s32[3]{0:T(128)} %refs_1_.2, s32[3]{0:T(128)} %bitcast.1, bf16[2,1152,256]{2,1,0:T(8,128)(2,1)} %refs_1_.3, f32[392,128]{1,0:T(8,128)} %constant.4.clone.refs_4_, ...), custom_call_target="tpu_custom_call" | custom-call | flops 1 | bytes 1 | tf_op jit(solution)/shard_map/cut/pallas_call | solution.py:311
  2.6 2.5 %collective-permute-start = (bf16[1184,256]{1,0:T(8,128)(2,1)S(1)}, bf16[1184,256]{1,0:T(8,128)(2,1)S(1)}, u32[]{:S(2)}, u32[]{:S(2)}) collective-permute-start(bf16[1184,256]{1,0:T(8,128)(2,1)S(1)} %get-tuple-element.31.kv_ref.refs_0_.own_ref), channel_id=1, source_target_pairs={{0,16},{1,17},{2,18},{3,19},{4,20},{5,21},{6,22},{7,23},{8,24},{9,... | collective-permute-start | bytes 1818632 | tf_op jit(solution)/shard_map/ppermute | solution.py:423
  5.2 7.9 %attend.3 = (bf16[2,1152,1024]{2,1,0:T(8,128)(2,1)}, s32[1]{0:T(128)}) custom-call(s32[16]{0:T(128)S(1)} %get-tuple-element.30.plan, bf16[2,1152,1024]{2,1,0:T(8,128)(2,1)} %q_hbm.5, bf16[1184,256]{1,0:T(8,128)(2,1)S(1)} %get-tuple-element.31.kv_ref.refs_0_.own_ref, f32[392,128]{1,0:T(8,128)S(1)} %get-tuple-element.32.cos_ref.refs_8_, ...), custom_call_target="tpu_custom_call" | custom-call | flops 1 | bytes 1 | tf_op jit(solution)/shard_map/attend/pallas_call | solution.py:162
  13.1 1.8 %cut.3.rest_0_.kv_ref.own_ref = bf16[1184,256]{1,0:T(8,128)(2,1)S(1)} custom-call(bf16[1184,256]{1,0:T(8,128)(2,1)S(1)} %get-tuple-element.31.kv_ref.refs_0_.own_ref, bf16[2,1152,256]{2,1,0:T(8,128)(2,1)} %refs_1_.3, s32[1]{0:T(128)} %get-tuple-element.34.refs_2_), custom_call_target="tpu_custom_call" | custom-call | flops 1 | bytes 1 | tf_op jit(solution)/shard_map/cut/pallas_call | solution.py:311
  14.9 1.7 %collective-permute-start.1 = (bf16[1184,256]{1,0:T(8,128)(2,1)S(1)}, bf16[1184,256]{1,0:T(8,128)(2,1)S(1)}, u32[]{:S(2)}, u32[]{:S(2)}) collective-permute-start(bf16[1184,256]{1,0:T(8,128)(2,1)S(1)} %cut.3.rest_0_.kv_ref.own_ref), channel_id=1, source_target_pairs={{0,16},{1,17},{2,18},{3,19},{4,20},{5,21},{6,22},{7,23},{8,24},{9,... | collective-permute-start | bytes 1818632 | tf_op jit(solution)/shard_map/ppermute | solution.py:423
  16.7 5.3 %attend.4 = (bf16[2,1152,1024]{2,1,0:T(8,128)(2,1)}, s32[1]{0:T(128)}) custom-call(s32[16]{0:T(128)S(1)} %get-tuple-element.30.plan, bf16[2,1152,1024]{2,1,0:T(8,128)(2,1)} %q_hbm.5, bf16[1184,256]{1,0:T(8,128)(2,1)S(1)} %get-tuple-element.31.kv_ref.refs_0_.own_ref, ...), custom_call_target="tpu_custom_call", output_to_operand_aliasing={{0}: (6, {})} | custom-call | flops 1 | bytes 1 | tf_op jit(solution)/shard_map/attend/pallas_call | solution.py:162
  21.9 1.6 %collective-permute-done.got_ref = bf16[1184,256]{1,0:T(8,128)(2,1)S(1)} collective-permute-done((bf16[1184,256]{1,0:T(8,128)(2,1)S(1)}, bf16[1184,256]{1,0:T(8,128)(2,1)S(1)}, u32[]{:S(2)}, u32[]{:S(2)}) %collective-permute-start) | collective-permute-done | bytes 606240 | tf_op jit(solution)/shard_map/ppermute | solution.py:423
  23.5 2.0 %pack.2 = (bf16[400,256]{1,0:T(8,128)(2,1)S(1)}, bf16[400,256]{1,0:T(8,128)(2,1)S(1)}, bf16[400,256]{1,0:T(8,128)(2,1)S(1)}, bf16[400,256]{1,0:T(8,128)(2,1)S(1)...) custom-call(s32[16]{0:T(128)S(1)} %get-tuple-element.30.plan, ...), custom_call_target="tpu_custom_call" | custom-call | flops 1 | bytes 1 | tf_op jit(solution)/shard_map/pack/pallas_call | solution.py:237
  25.5 3.2 %collective-permute-start.7 = (bf16[400,256]{1,0:T(8,128)(2,1)S(1)}, bf16[400,256]{1,0:T(8,128)(2,1)S(1)}, u32[]{:S(2)}, u32[]{:S(2)}) collective-permute-start(bf16[400,256]{1,0:T(8,128)(2,1)S(1)} %get-tuple-element.48), channel_id=1, source_target_pairs={{0,9},{1,8},{2,11},{3,10},{4,13},{5,12},{6,15},{7,14},{8,1},{9,0},... | collective-permute-start | bytes 614408 | tf_op jit(solution)/shard_map/ppermute | solution.py:423
  28.7 0.3 collective-permute-start.8
  29.0 0.0 collective-permute-start.9
  29.0 1.6 %collective-permute-start.10 = (bf16[400,256]{1,0:T(8,128)(2,1)S(1)}, bf16[400,256]{1,0:T(8,128)(2,1)S(1)}, u32[]{:S(2)}, u32[]{:S(2)}) collective-permute-start(bf16[400,256]{1,0:T(8,128)(2,1)S(1)} %get-tuple-element.51), channel_id=1, source_target_pairs={{0,8},{1,9},{2,10},{3,11},{4,12},{5,13},{6,14},{7,15},{8,0},{9,1},... | collective-permute-start | bytes 614408 | tf_op jit(solution)/shard_map/ppermute | solution.py:423
  30.6 0.0 copy-start
  30.6 0.0 copy-start.1
  30.6 10.6 %attend.5 = (bf16[2,1152,1024]{2,1,0:T(8,128)(2,1)}, s32[1]{0:T(128)}) custom-call(s32[16]{0:T(128)S(1)} %get-tuple-element.30.plan, bf16[2,1152,1024]{2,1,0:T(8,128)(2,1)} %q_hbm.5, bf16[1184,256]{1,0:T(8,128)(2,1)S(1)} %cut.3.rest_0_.kv_ref.own_ref, f32[392,128]{1,0:T(8,128)S(1)} %get-tuple-element.32.cos_ref.refs_8_, ...), custom_call_target="tpu_custom_call", output_to_operand_aliasing={{0}: (6, {})} | custom-call | flops 1 | bytes 1 | tf_op jit(solution)/shard_map/attend/pallas_call | solution.py:162
  41.2 0.0 collective-permute-done.1.got_ref
  41.2 2.4 %pack.3 = (bf16[400,256]{1,0:T(8,128)(2,1)S(1)}, bf16[400,256]{1,0:T(8,128)(2,1)S(1)}, bf16[400,256]{1,0:T(8,128)(2,1)S(1)}, bf16[400,256]{1,0:T(8,128)(2,1)S(1)...) custom-call(s32[16]{0:T(128)S(1)} %get-tuple-element.30.plan, ...), custom_call_target="tpu_custom_call" | custom-call | flops 1 | bytes 1 | tf_op jit(solution)/shard_map/pack/pallas_call | solution.py:237
  43.7 1.3 %collective-permute-start.11 = (bf16[400,256]{1,0:T(8,128)(2,1)S(1)}, bf16[400,256]{1,0:T(8,128)(2,1)S(1)}, u32[]{:S(2)}, u32[]{:S(2)}) collective-permute-start(bf16[400,256]{1,0:T(8,128)(2,1)S(1)} %get-tuple-element.52), channel_id=1, source_target_pairs={{0,8},{1,9},{2,10},{3,11},{4,12},{5,13},{6,14},{7,15},{8,16},{9,17... | collective-permute-start | bytes 614408 | tf_op jit(solution)/shard_map/ppermute | solution.py:423
  45.0 0.0 collective-permute-done.7.refs_0_
  45.0 0.0 collective-permute-start.2
  45.0 0.0 collective-permute-done.8.refs_1_
  45.0 1.0 %collective-permute-start.3 = (bf16[400,256]{1,0:T(8,128)(2,1)S(1)}, bf16[400,256]{1,0:T(8,128)(2,1)S(1)}, u32[]{:S(2)}, u32[]{:S(2)}) collective-permute-start(bf16[400,256]{1,0:T(8,128)(2,1)S(1)} %get-tuple-element.43), channel_id=1, source_target_pairs={{0,1},{1,0},{2,3},{3,2},{4,5},{5,4},{6,7},{7,6},{8,9},{9,8},{10,11... | collective-permute-start | bytes 614408 | tf_op jit(solution)/shard_map/ppermute | solution.py:423
  46.0 0.0 collective-permute-done.9.refs_2_
  46.0 2.4 %collective-permute-start.4 = (bf16[400,256]{1,0:T(8,128)(2,1)S(1)}, bf16[400,256]{1,0:T(8,128)(2,1)S(1)}, u32[]{:S(2)}, u32[]{:S(2)}) collective-permute-start(bf16[400,256]{1,0:T(8,128)(2,1)S(1)} %get-tuple-element.44), channel_id=1, source_target_pairs={{0,9},{1,8},{2,11},{3,10},{4,13},{5,12},{6,15},{7,14},{8,17},{9,16... | collective-permute-start | bytes 614408 | tf_op jit(solution)/shard_map/ppermute | solution.py:423
  48.4 0.0 collective-permute-done.10.refs_3_
  48.4 0.0 collective-permute-start.5
  48.4 0.0 collective-permute-done.11.refs_5_
  48.4 1.7 %collective-permute-start.6 = (bf16[400,256]{1,0:T(8,128)(2,1)S(1)}, bf16[400,256]{1,0:T(8,128)(2,1)S(1)}, u32[]{:S(2)}, u32[]{:S(2)}) collective-permute-start(bf16[400,256]{1,0:T(8,128)(2,1)S(1)} %get-tuple-element.47), channel_id=1, source_target_pairs={{0,8},{1,9},{2,10},{3,11},{4,12},{5,13},{6,14},{7,15},{8,16},{9,17... | collective-permute-start | bytes 614408 | tf_op jit(solution)/shard_map/ppermute | solution.py:423
  50.2 0.0 copy-done
  50.2 0.0 copy-done.1
  50.2 2.0 %settle.2 = (bf16[3,2,384,512]{3,2,1,0:T(8,128)(2,1)}, f32[3,2,1024]{2,1,0:T(2,128)S(1)}) custom-call(s32[16]{0:T(128)S(1)} %get-tuple-element.30.plan, bf16[400,256]{1,0:T(8,128)(2,1)S(1)} %collective-permute-done.7.refs_0_, bf16[400,256]{1,0:T(8,128)(2,1)S(1)} %collective-permute-done.8.refs_1_, bf16[400,256]{1,0:T(8,128)(2,1)S(1)} %collective-permute-done.9.refs_2_, ...), custom_call_target="tpu_custom_call" | custom-call | flops 1 | bytes 1 | tf_op jit(solution)/shard_map/settle/pallas_call | solution.py:404
  52.2 0.2 collective-permute-done.2.refs_0_
  52.4 4.7 %collective-permute-done.3.refs_1_ = bf16[400,256]{1,0:T(8,128)(2,1)S(1)} collective-permute-done((bf16[400,256]{1,0:T(8,128)(2,1)S(1)}, bf16[400,256]{1,0:T(8,128)(2,1)S(1)}, u32[]{:S(2)}, u32[]{:S(2)}) %collective-permute-start.3) | collective-permute-done | bytes 204832 | tf_op jit(solution)/shard_map/ppermute | solution.py:423
  57.1 3.0 %collective-permute-done.4.refs_2_ = bf16[400,256]{1,0:T(8,128)(2,1)S(1)} collective-permute-done((bf16[400,256]{1,0:T(8,128)(2,1)S(1)}, bf16[400,256]{1,0:T(8,128)(2,1)S(1)}, u32[]{:S(2)}, u32[]{:S(2)}) %collective-permute-start.4) | collective-permute-done | bytes 204832 | tf_op jit(solution)/shard_map/ppermute | solution.py:423
  60.1 0.0 collective-permute-done.5.refs_3_
  60.1 0.0 collective-permute-done.6.refs_5_
  60.1 2.7 %settle.3 = (bf16[3,2,384,512]{3,2,1,0:T(8,128)(2,1)}, bf16[3,2,2,1024]{3,2,1,0:T(2,128)(2,1)}) custom-call(s32[16]{0:T(128)S(1)} %get-tuple-element.30.plan, bf16[400,256]{1,0:T(8,128)(2,1)S(1)} %collective-permute-done.2.refs_0_, bf16[400,256]{1,0:T(8,128)(2,1)S(1)} %collective-permute-done.3.refs_1_, ...), custom_call_target="tpu_custom_call", output_to_operand_aliasing={{0}: (12, {})} | custom-call | flops 1 | bytes 1 | tf_op jit(solution)/shard_map/settle/pallas_call | solution.py:404
Async XLA Ops:
  2.6 20.9 %collective-permute-start = (bf16[1184,256]{1,0:T(8,128)(2,1)S(1)}, bf16[1184,256]{1,0:T(8,128)(2,1)S(1)}, u32[]{:S(2)}, u32[]{:S(2)}) collective-permute-start(bf16[1184,256]{1,0:T(8,128)(2,1)S(1)} %get-tuple-element.31.kv_ref.refs_0_.own_ref), channel_id=1, source_target_pairs={{0,16},{1,17},{2,18},{3,19},{4,20},{5,21},{6,22},{7,23},{8,24},{9,... | collective-permute-start | bytes 1818632 | tf_op jit(solution)/shard_map/ppermute | solution.py:423
  14.9 26.3 %collective-permute-start.1 = (bf16[1184,256]{1,0:T(8,128)(2,1)S(1)}, bf16[1184,256]{1,0:T(8,128)(2,1)S(1)}, u32[]{:S(2)}, u32[]{:S(2)}) collective-permute-start(bf16[1184,256]{1,0:T(8,128)(2,1)S(1)} %cut.3.rest_0_.kv_ref.own_ref), channel_id=1, source_target_pairs={{0,16},{1,17},{2,18},{3,19},{4,20},{5,21},{6,22},{7,23},{8,24},{9,... | collective-permute-start | bytes 1818632 | tf_op jit(solution)/shard_map/ppermute | solution.py:423
  25.5 19.5 %collective-permute-start.7 = (bf16[400,256]{1,0:T(8,128)(2,1)S(1)}, bf16[400,256]{1,0:T(8,128)(2,1)S(1)}, u32[]{:S(2)}, u32[]{:S(2)}) collective-permute-start(bf16[400,256]{1,0:T(8,128)(2,1)S(1)} %get-tuple-element.48), channel_id=1, source_target_pairs={{0,9},{1,8},{2,11},{3,10},{4,13},{5,12},{6,15},{7,14},{8,1},{9,0},... | collective-permute-start | bytes 614408 | tf_op jit(solution)/shard_map/ppermute | solution.py:423
  28.7 16.3 %collective-permute-start.8 = (bf16[400,256]{1,0:T(8,128)(2,1)S(1)}, bf16[400,256]{1,0:T(8,128)(2,1)S(1)}, u32[]{:S(2)}, u32[]{:S(2)}) collective-permute-start(bf16[400,256]{1,0:T(8,128)(2,1)S(1)} %get-tuple-element.49), channel_id=1, source_target_pairs={{0,1},{1,0},{2,3},{3,2},{4,5},{5,4},{6,7},{7,6},{8,9},{9,8},{10,11... | collective-permute-start | bytes 614408 | tf_op jit(solution)/shard_map/ppermute | solution.py:423
  29.0 17.1 %collective-permute-start.9 = (bf16[400,256]{1,0:T(8,128)(2,1)S(1)}, bf16[400,256]{1,0:T(8,128)(2,1)S(1)}, u32[]{:S(2)}, u32[]{:S(2)}) collective-permute-start(bf16[400,256]{1,0:T(8,128)(2,1)S(1)} %get-tuple-element.50), channel_id=1, source_target_pairs={{0,9},{1,8},{2,11},{3,10},{4,13},{5,12},{6,15},{7,14},{8,17},{9,16... | collective-permute-start | bytes 614408 | tf_op jit(solution)/shard_map/ppermute | solution.py:423
  29.0 19.5 %collective-permute-start.10 = (bf16[400,256]{1,0:T(8,128)(2,1)S(1)}, bf16[400,256]{1,0:T(8,128)(2,1)S(1)}, u32[]{:S(2)}, u32[]{:S(2)}) collective-permute-start(bf16[400,256]{1,0:T(8,128)(2,1)S(1)} %get-tuple-element.51), channel_id=1, source_target_pairs={{0,8},{1,9},{2,10},{3,11},{4,12},{5,13},{6,14},{7,15},{8,0},{9,1},... | collective-permute-start | bytes 614408 | tf_op jit(solution)/shard_map/ppermute | solution.py:423
  30.6 19.6 %copy-start = (bf16[3,2,2,1024]{3,2,1,0:T(2,128)(2,1)S(1)}, bf16[3,2,2,1024]{3,2,1,0:T(2,128)(2,1)}, u32[]{:S(2)}) copy-start(bf16[3,2,2,1024]{3,2,1,0:T(2,128)(2,1)} %refs_6_.3) | copy-start | bytes 73732
  30.6 19.6 %copy-start.1 = (bf16[3,2,2,256]{3,2,1,0:T(2,128)(2,1)S(1)}, bf16[3,2,2,256]{3,2,1,0:T(2,128)(2,1)}, u32[]{:S(2)}) copy-start(bf16[3,2,2,256]{3,2,1,0:T(2,128)(2,1)} %refs_7_.3) | copy-start | bytes 18436
  43.7 4.8 %collective-permute-start.11 = (bf16[400,256]{1,0:T(8,128)(2,1)S(1)}, bf16[400,256]{1,0:T(8,128)(2,1)S(1)}, u32[]{:S(2)}, u32[]{:S(2)}) collective-permute-start(bf16[400,256]{1,0:T(8,128)(2,1)S(1)} %get-tuple-element.52), channel_id=1, source_target_pairs={{0,8},{1,9},{2,10},{3,11},{4,12},{5,13},{6,14},{7,15},{8,16},{9,17... | collective-permute-start | bytes 614408 | tf_op jit(solution)/shard_map/ppermute | solution.py:423
  45.0 7.4 %collective-permute-start.2 = (bf16[400,256]{1,0:T(8,128)(2,1)S(1)}, bf16[400,256]{1,0:T(8,128)(2,1)S(1)}, u32[]{:S(2)}, u32[]{:S(2)}) collective-permute-start(bf16[400,256]{1,0:T(8,128)(2,1)S(1)} %get-tuple-element.42), channel_id=1, source_target_pairs={{0,9},{1,8},{2,11},{3,10},{4,13},{5,12},{6,15},{7,14},{8,1},{9,0},... | collective-permute-start | bytes 614408 | tf_op jit(solution)/shard_map/ppermute | solution.py:423
  45.0 12.1 %collective-permute-start.3 = (bf16[400,256]{1,0:T(8,128)(2,1)S(1)}, bf16[400,256]{1,0:T(8,128)(2,1)S(1)}, u32[]{:S(2)}, u32[]{:S(2)}) collective-permute-start(bf16[400,256]{1,0:T(8,128)(2,1)S(1)} %get-tuple-element.43), channel_id=1, source_target_pairs={{0,1},{1,0},{2,3},{3,2},{4,5},{5,4},{6,7},{7,6},{8,9},{9,8},{10,11... | collective-permute-start | bytes 614408 | tf_op jit(solution)/shard_map/ppermute | solution.py:423
  46.0 14.0 %collective-permute-start.4 = (bf16[400,256]{1,0:T(8,128)(2,1)S(1)}, bf16[400,256]{1,0:T(8,128)(2,1)S(1)}, u32[]{:S(2)}, u32[]{:S(2)}) collective-permute-start(bf16[400,256]{1,0:T(8,128)(2,1)S(1)} %get-tuple-element.44), channel_id=1, source_target_pairs={{0,9},{1,8},{2,11},{3,10},{4,13},{5,12},{6,15},{7,14},{8,17},{9,16... | collective-permute-start | bytes 614408 | tf_op jit(solution)/shard_map/ppermute | solution.py:423
  48.4 11.6 %collective-permute-start.5 = (bf16[400,256]{1,0:T(8,128)(2,1)S(1)}, bf16[400,256]{1,0:T(8,128)(2,1)S(1)}, u32[]{:S(2)}, u32[]{:S(2)}) collective-permute-start(bf16[400,256]{1,0:T(8,128)(2,1)S(1)} %get-tuple-element.45), channel_id=1, source_target_pairs={{0,8},{1,9},{2,10},{3,11},{4,12},{5,13},{6,14},{7,15},{8,0},{9,1},... | collective-permute-start | bytes 614408 | tf_op jit(solution)/shard_map/ppermute | solution.py:423
  48.4 11.6 %collective-permute-start.6 = (bf16[400,256]{1,0:T(8,128)(2,1)S(1)}, bf16[400,256]{1,0:T(8,128)(2,1)S(1)}, u32[]{:S(2)}, u32[]{:S(2)}) collective-permute-start(bf16[400,256]{1,0:T(8,128)(2,1)S(1)} %get-tuple-element.47), channel_id=1, source_target_pairs={{0,8},{1,9},{2,10},{3,11},{4,12},{5,13},{6,14},{7,15},{8,16},{9,17... | collective-permute-start | bytes 614408 | tf_op jit(solution)/shard_map/ppermute | solution.py:423

commit v2 on v1

--- a/solution.py
+++ b/solution.py
@@ -69,9 +69,24 @@
     return found * plan[LENGTHS_AT + index], [plan[index * PAGES_P + j] for j in range(PAGES_P)]
 
 
-def attend_kernel(plan, q_hbm, kv_ref, cos_ref, sin_ref, *rest, first, count):
-    out_hbm, token, q_buf, out_buf, keys_rot, values_t, q_sem, out_sem = rest[-8:]
-    token[0] = 0
+def slab_copies_of(pool, layer, slab, sem):
+    copies = []
+    for i in range(CUTS):
+        rows = pl.ds(i * (POOL // CUTS), POOL // CUTS)
+        copies.append(pltpu.make_async_copy(pool.at[layer, rows], slab.at[rows], sem.at[i]))
+    return copies
+
+
+def attend_kernel(plan, q_hbm, *refs, first, count, supply):
+    kv_ref, cos_ref, sin_ref = refs[:3]
+    out_hbm, mark, q_buf, out_buf, keys_rot, values_t, q_sem, out_sem, slab_sem = refs[-9:]
+    slab_copies = []
+    if supply:
+        slab_copies = slab_copies_of(refs[3], 1, mark, slab_sem)
+        rows = pl.ds(POOL, PLAN_ROWS)
+        slab_copies.append(pltpu.make_async_copy(kv_ref.at[rows], mark.at[rows], slab_sem.at[CUTS]))
+    else:
+        mark[0] = 0
     width = GROUP * HD
 
     def place(i):
@@ -94,14 +109,16 @@
     for i in range(count):
         for j in range(PAGES_P):
             q_copy(i, j).start()
+    for copy in slab_copies:
+        copy.start()
     values_t[HD:, :] = jnp.ones((16, PROMPT), jnp.bfloat16)
 
-    def body(i, _):
+    def body(source, i, _):
         _, prompt = place(i)
         length = plan[LENGTHS_AT + prompt]
         for j in range(PAGES_P):
             rows = slice(j * PAGE, (j + 1) * PAGE)
-            page = kv_ref[page_rows(prompt, j), :]
+            page = source[page_rows(prompt, j), :]
             keys = rotated(page[:, :HD].astype(jnp.float32), cos_ref[rows, :], sin_ref[rows, :])
             keys_rot[rows, :] = keys.astype(jnp.bfloat16)
             values_t[:HD, rows] = page[:, HD:].astype(jnp.float32).T.astype(jnp.bfloat16)
@@ -136,7 +153,12 @@
             out_copy(i, j).start()
         return 0
 
-    lax.fori_loop(0, count, body, 0)
+    before = min(count, PROMPTS_DEV) if supply else count
+    lax.fori_loop(0, before, functools.partial(body, kv_ref), 0)
+    for copy in slab_copies:
+        copy.wait()
+    if before < count:
+        lax.fori_loop(before, count, functools.partial(body, mark), 0)
     for i in range(count):
         for j in range(PAGES_P):
             out_copy(i, j).wait()
@@ -150,9 +172,16 @@
 BRIEF = pl.CostEstimate(flops=1, bytes_accessed=1, transcendentals=0)
 
 
-def attend(plan, queries, keys_values, cosine, sine, earlier, first, count, after=()):
-    operands = [plan, queries, keys_values, cosine, sine, *after]
-    in_specs = [SMEM, HBM, VMEM, VMEM, VMEM] + [ANY] * len(after)
+def attend(plan, queries, slab, cosine, sine, first, count, supply=None, earlier=None, after=()):
+    operands = [plan, queries, slab, cosine, sine]
+    in_specs = [SMEM, HBM, VMEM, VMEM, VMEM]
+    mark = jax.ShapeDtypeStruct((1,), jnp.int32)
+    if supply is not None:
+        operands.append(supply)
+        in_specs.append(HBM)
+        mark = jax.ShapeDtypeStruct(slab.shape, slab.dtype)
+    operands += after
+    in_specs += [ANY] * len(after)
     aliases = {}
     if earlier is not None:
         in_specs.append(HBM)
@@ -160,9 +189,9 @@
         operands.append(earlier)
     pages = (count, PAGES_P, PAGE, GROUP * HD)
     return pl.pallas_call(
-        functools.partial(attend_kernel, first=first, count=count),
+        functools.partial(attend_kernel, first=first, count=count, supply=supply is not None),
         in_specs=in_specs,
-        out_specs=[HBM, SMEM],
+        out_specs=[HBM, SMEM if supply is None else VMEM],
         scratch_shapes=[
             pltpu.VMEM(pages, jnp.bfloat16),
             pltpu.VMEM(pages, jnp.bfloat16),
@@ -170,11 +199,9 @@
             pltpu.VMEM((HD + 16, PROMPT), jnp.bfloat16),
             pltpu.SemaphoreType.DMA((count, PAGES_P)),
             pltpu.SemaphoreType.DMA((count, PAGES_P)),
+            pltpu.SemaphoreType.DMA((CUTS + 1,)),
         ],
-        out_shape=[
-            jax.ShapeDtypeStruct(queries.shape, jnp.bfloat16),
-            jax.ShapeDtypeStruct((1,), jnp.int32),
-        ],
+        out_shape=[jax.ShapeDtypeStruct(queries.shape, jnp.bfloat16), mark],
         input_output_aliases=aliases,
         cost_estimate=BRIEF,
         compiler_params=pltpu.CompilerParams(vmem_limit_bytes=VMEM_LIMIT),
@@ -246,78 +273,63 @@
     )(plan, own, got, cosine, sine, after, *kept)
 
 
-def cut_kernel(*refs, layer):
-    if layer == 0:
-        page_hbm, lengths_hbm, targets_hbm, source, cos_hbm, sin_hbm = refs[:6]
-        slab, plan, cos_ref, sin_ref, sem, page_table, lengths, targets, int_sem = refs[-9:]
-        ints = [
-            pltpu.make_async_copy(page_hbm, page_table, int_sem.at[0]),
-            pltpu.make_async_copy(lengths_hbm, lengths, int_sem.at[1]),
-            pltpu.make_async_copy(targets_hbm, targets, int_sem.at[2]),
-        ]
-    else:
-        before, source = refs[:2]
-        slab, sem = refs[-2:]
-        ints = []
-    copies = []
-    for i in range(CUTS):
-        rows = pl.ds(i * (POOL // CUTS), POOL // CUTS)
-        copies.append(pltpu.make_async_copy(source.at[layer, rows], slab.at[rows], sem.at[i]))
-    if layer == 0:
-        copies.append(pltpu.make_async_copy(cos_hbm, cos_ref, sem.at[CUTS]))
-        copies.append(pltpu.make_async_copy(sin_hbm, sin_ref, sem.at[CUTS + 1]))
-    if layer == 1:
-        rows = pl.ds(POOL, PLAN_ROWS)
-        copies.append(pltpu.make_async_copy(before.at[rows], slab.at[rows], sem.at[CUTS]))
+def cut_kernel(*refs):
+    page_hbm, lengths_hbm, targets_hbm, source, cos_hbm, sin_hbm = refs[:6]
+    slab, plan, cos_ref, sin_ref, sem, page_table, lengths, targets, int_sem = refs[6:]
+    ints = [
+        pltpu.make_async_copy(page_hbm, page_table, int_sem.at[0]),
+        pltpu.make_async_copy(lengths_hbm, lengths, int_sem.at[1]),
+        pltpu.make_async_copy(targets_hbm, targets, int_sem.at[2]),
+    ]
+    copies = slab_copies_of(source, 0, slab, sem)
+    copies.append(pltpu.make_async_copy(cos_hbm, cos_ref, sem.at[CUTS]))
+    copies.append(pltpu.make_async_copy(sin_hbm, sin_ref, sem.at[CUTS + 1]))
     for copy in ints + copies:
         copy.start()
     for copy in ints:
         copy.wait()
-    if layer == 0:
-        for r in range(PROMPTS_DEV):
-            for j in range(PAGES_P):
-                plan[r * PAGES_P + j] = page_table[r, j]
-            plan[LENGTHS_AT + r] = lengths[r]
-            plan[TARGETS_AT + r] = targets[r]
-        plan[PLACE_AT] = lax.rem(lax.axis_index("grp"), 2) * 2 + lax.rem(lax.axis_index("tp"), 2)
-        halves = [plan[LENGTHS_AT + r] // 2 for r in range(PROMPTS_DEV)]
-        numbers = [plan[r] for r in range(LENGTHS_AT)] + halves
-        numbers += [plan[LENGTHS_AT + r] - 2 * halves[r] for r in range(PROMPTS_DEV)]
-        numbers += [plan[TARGETS_AT + r] for r in range(PROMPTS_DEV)]
-        row = lax.broadcasted_iota(jnp.int32, (PLAN_ROWS, 2 * HD), 0)
-        marks = jnp.zeros((PLAN_ROWS, 2 * HD), jnp.int32)
-        for r, number in enumerate(numbers):
-            marks = jnp.where(row == r, number, marks)
-        slab[POOL:, :] = marks.astype(jnp.float32).astype(jnp.bfloat16)
+    for r in range(PROMPTS_DEV):
+        for j in range(PAGES_P):
+            plan[r * PAGES_P + j] = page_table[r, j]
+        plan[LENGTHS_AT + r] = lengths[r]
+        plan[TARGETS_AT + r] = targets[r]
+    plan[PLACE_AT] = lax.rem(lax.axis_index("grp"), 2) * 2 + lax.rem(lax.axis_index("tp"), 2)
+    halves = [plan[LENGTHS_AT + r] // 2 for r in range(PROMPTS_DEV)]
+    numbers = [plan[r] for r in range(LENGTHS_AT)] + halves
+    numbers += [plan[LENGTHS_AT + r] - 2 * halves[r] for r in range(PROMPTS_DEV)]
+    numbers += [plan[TARGETS_AT + r] for r in range(PROMPTS_DEV)]
+    row = lax.broadcasted_iota(jnp.int32, (PLAN_ROWS, 2 * HD), 0)
+    marks = jnp.zeros((PLAN_ROWS, 2 * HD), jnp.int32)
+    for r, number in enumerate(numbers):
+        marks = jnp.where(row == r, number, marks)
+    slab[POOL:, :] = marks.astype(jnp.float32).astype(jnp.bfloat16)
     for copy in copies:
         copy.wait()
 
 
-def cut(operands, layer, after=()):
-    slab = jax.ShapeDtypeStruct((POOL + PLAN_ROWS, 2 * HD), jnp.bfloat16)
-    out_shape, out_specs, scratch = [slab], [VMEM], [pltpu.SemaphoreType.DMA((CUTS + 2,))]
-    in_specs = [VMEM, HBM]
-    if layer == 0:
-        table = jax.ShapeDtypeStruct((PROMPT + 8, HD), jnp.float32)
-        out_shape += [jax.ShapeDtypeStruct((16,), jnp.int32), table, table]
-        out_specs += [SMEM, VMEM, VMEM]
-        scratch += [
+def cut(*operands):
+    table = jax.ShapeDtypeStruct((PROMPT + 8, HD), jnp.float32)
+    return pl.pallas_call(
+        cut_kernel,
+        in_specs=[HBM] * 6,
+        out_specs=[VMEM, SMEM, VMEM, VMEM],
+        scratch_shapes=[
+            pltpu.SemaphoreType.DMA((CUTS + 2,)),
             pltpu.SMEM((PROMPTS_DEV, PAGES_P), jnp.int32),
             pltpu.SMEM((PROMPTS_DEV,), jnp.int32),
             pltpu.SMEM((PROMPTS_DEV,), jnp.int32),
             pltpu.SemaphoreType.DMA((3,)),
-        ]
-        in_specs = [HBM] * 6
-    return pl.pallas_call(
-        functools.partial(cut_kernel, layer=layer),
-        in_specs=in_specs + [ANY] * len(after),
-        out_specs=out_specs,
-        scratch_shapes=scratch,
-        out_shape=out_shape,
+        ],
+        out_shape=[
+            jax.ShapeDtypeStruct((POOL + PLAN_ROWS, 2 * HD), jnp.bfloat16),
+            jax.ShapeDtypeStruct((16,), jnp.int32),
+            table,
+            table,
+        ],
         cost_estimate=BRIEF,
         compiler_params=pltpu.CompilerParams(vmem_limit_bytes=VMEM_LIMIT),
         name="cut",
-    )(*operands, *after)
+    )(*operands)
 
 
 def settle_kernel(plan, *refs, layer):
@@ -339,7 +351,7 @@
     token = lax.broadcasted_iota(jnp.int32, (GROUP, PROMPT), 1).astype(jnp.float32)
     scores, own, fresh_values = [], [], []
     for k in range(NEAR):
-        held = units[2 * k][PROMPT : PROMPT + 1, :].astype(jnp.float32)
+        held = units[max(1, 2 * k)][PROMPT : PROMPT + 1, :].astype(jnp.float32)
         held = 2.0 * held[:, :HD] + held[:, HD:]
         cosine = jnp.sum(jnp.where(position == held, cos_ref[...], 0.0), axis=0, keepdims=True)
         sine = jnp.sum(jnp.where(position == held, sin_ref[...], 0.0), axis=0, keepdims=True)
@@ -433,29 +445,26 @@
             page_table, prompt_lengths, targets.reshape(-1), prompt_queries, prompt_kv, *tables
         )
     )
-    slab, plan, cosine, sine = cut([page_table, prompt_lengths, targets, prompt_kv, *tables], 0)
+    slab, plan, cosine, sine = cut(page_table, prompt_lengths, targets, prompt_kv, *tables)
     got = moved(slab, 2, 0)
-    out, token = attend(plan, prompt_queries, slab, cosine, sine, None, 0, 2)
-    (later_slab,) = cut([slab, prompt_kv], 1, [token])
+    attention = functools.partial(attend, plan, prompt_queries)
+    out, later_slab = attention(slab, cosine, sine, 0, 4, prompt_kv)
     later_got = moved(later_slab, 2, 0)
-    out, token = attend(plan, prompt_queries, slab, cosine, sine, out, 2, 1, [later_slab])
-
-    local, near_same, near_other, mid_other, far_first, far_other = pack(
-        plan, slab, got, cosine, sine, token
+
+    local, near_first, near_other, mid_other, far_same, far_other = pack(
+        plan, slab, got, cosine, sine, later_slab
     )
     near_other = moved(near_other, None, 1)
     mid_other = moved(mid_other, 0, 1)
     far_other = moved(far_other, 1, 1)
-    near_same = moved(near_same, None, 0)
-    units = [near_same, near_other, local, mid_other, None, far_other]
-
-    out, token = attend(
-        plan, prompt_queries, later_slab, cosine, sine, out, PROMPTS_DEV, PROMPTS_DEV, [local]
+    far_same = moved(far_same, 1, 0)
+    units = [None, near_other, local, mid_other, far_same, far_other]
+
+    out, mark = attention(later_slab, cosine, sine, 4, 2, None, out, [local])
+    local, near_same, near_other, mid_other, far_same, far_other, near_first = pack(
+        plan, later_slab, later_got, cosine, sine, mark, [near_first]
     )
-    local, near_same, near_other, mid_other, far_same, far_other, far_first = pack(
-        plan, later_slab, later_got, cosine, sine, token, [far_first]
-    )
-    units[4] = moved(far_first, 1, 0)
+    units[0] = moved(near_first, None, 0)
     near_other = moved(near_other, None, 1)
     mid_other = moved(mid_other, 0, 1)
     far_other = moved(far_other, 1, 1)

time: 63.2 us -> 59.6 us (0.943)
  Pallas kernels: 36.8 us -> 31.3 us
  waiting for transfers between devices: 9.45 us -> 13.9 us
  starting transfers between devices: 15.9 us -> 13.4 us
    pallas_call x5 -> x3, Pallas kernels: 27.6 us -> 22.8 us  [the longest x2 20.8 us: attend(): pl.pallas_call(functools.partial(attend_kernel, first=first, count=count,...]
    ppermute x12, waiting for transfers between devices: 9.45 us -> 13.9 us  [moved(): return lax.ppermute(value, ('grp', 'tp'), pairs)]
    ppermute x12, starting transfers between devices: 15.9 us -> 13.4 us  [moved(): return lax.ppermute(value, ('grp', 'tp'), pairs)]
    pallas_call x2, Pallas kernels: 4.39 us -> 3.73 us  [pack(): pl.pallas_call(pack_kernel, in_specs=[SMEM, VMEM, VMEM, VMEM, VMEM, ANY]...]
  transfers between devices with their start and end apart: 12 -> 12, of which waited for: 4 -> 5; matrix products, arithmetic and copies ran while one was open for 0% -> 0% of each run, Pallas kernels for 51% -> 45%
where the time goes in v2:
time: 59.6 us; the launch traced here: 59.5 us
  Pallas kernels  31.3 us (53%)
  waiting for transfers between devices  13.9 us (23%)
  starting transfers between devices  13.4 us (22%)
  between operations  0.86 us (1%)
    pallas_call x2, Pallas kernels, attend(): pl.pallas_call(functools.partial(attend_kernel, first=first, count=count,...  20.8 us
    ppermute x12, waiting for transfers between devices, moved(): return lax.ppermute(value, ('grp', 'tp'), pairs)  13.9 us
    ppermute x12, starting transfers between devices, moved(): return lax.ppermute(value, ('grp', 'tp'), pairs)  13.4 us
    pallas_call x2, Pallas kernels, settle(): pl.pallas_call(functools.partial(settle_kernel, layer=layer), in_specs=in...  4.75 us
    pallas_call x2, Pallas kernels, pack(): pl.pallas_call(pack_kernel, in_specs=[SMEM, VMEM, VMEM, VMEM, VMEM, ANY]...  3.73 us
    pallas_call x1, Pallas kernels, cut(): pl.pallas_call(cut_kernel, in_specs=[HBM] * 6, out_specs=[VMEM, SMEM, VME...  1.97 us
  transfers between devices with their start and end apart: 12, of which 5 were waited for; matrix products, arithmetic and copies ran while one was open for 0% of the time, Pallas kernels for 45%

profile of v2, /device:TPU:1, one launch (start us, length us, event | category | flops | bytes accessed | tf_op | source)
XLA Modules:
  0.0 59.5 jit_solution(17794105812542939378)
XLA Ops:
  0.6 2.0 %cut.1 = (bf16[1184,256]{1,0:T(8,128)(2,1)S(1)}, s32[16]{0:T(128)S(1)}, f32[392,128]{1,0:T(8,128)S(1)}, f32[392,128]{1,0:T(8,128)S(1)}) custom-call(s32[3,3]{1,0:T(4,128)} %refs_0_.1, s32[3]{0:T(128)} %refs_1_.1, s32[3]{0:T(128)} %bitcast.1, bf16[2,1152,256]{2,1,0:T(8,128)(2,1)} %refs_3_.3, f32[392,128]{1,0:T(8,128)} %constant.4.clone.refs_4_, ...), custom_call_target="tpu_custom_call" | custom-call | flops 1 | bytes 1 | tf_op jit(solution)/shard_map/cut/pallas_call | solution.py:312
  2.6 2.5 %collective-permute-start = (bf16[1184,256]{1,0:T(8,128)(2,1)S(1)}, bf16[1184,256]{1,0:T(8,128)(2,1)S(1)}, u32[]{:S(2)}, u32[]{:S(2)}) collective-permute-start(bf16[1184,256]{1,0:T(8,128)(2,1)S(1)} %get-tuple-element.29.refs_0_.own_ref), channel_id=1, source_target_pairs={{0,16},{1,17},{2,18},{3,19},{4,20},{5,21},{6,22},{7,23},{8,24},{9,... | collective-permute-start | bytes 1818632 | tf_op jit(solution)/shard_map/ppermute | solution.py:435
  5.2 12.8 %attend.2 = (bf16[2,1152,1024]{2,1,0:T(8,128)(2,1)}, bf16[1184,256]{1,0:T(8,128)(2,1)S(1)}) custom-call(s32[16]{0:T(128)S(1)} %get-tuple-element.28.plan, bf16[2,1152,1024]{2,1,0:T(8,128)(2,1)} %q_hbm.3, bf16[1184,256]{1,0:T(8,128)(2,1)S(1)} %get-tuple-element.29.refs_0_.own_ref, f32[392,128]{1,0:T(8,128)S(1)} %get-tuple-element.30.refs_1_.cos_ref.refs_8_, ...), custom_call_target="tpu_custom_call" | custom-call | flops 1 | bytes 1 | tf_op jit(solution)/shard_map/attend/pallas_call | solution.py:191
  18.0 1.7 %collective-permute-start.1 = (bf16[1184,256]{1,0:T(8,128)(2,1)S(1)}, bf16[1184,256]{1,0:T(8,128)(2,1)S(1)}, u32[]{:S(2)}, u32[]{:S(2)}) collective-permute-start(bf16[1184,256]{1,0:T(8,128)(2,1)S(1)} %get-tuple-element.32.after.refs_0_.own_ref), channel_id=1, source_target_pairs={{0,16},{1,17},{2,18},{3,19},{4,20},{5,21},{6,22},{7,23},{8,24},{9,... | collective-permute-start | bytes 1818632 | tf_op jit(solution)/shard_map/ppermute | solution.py:435
  19.7 3.8 %collective-permute-done.got_ref = bf16[1184,256]{1,0:T(8,128)(2,1)S(1)} collective-permute-done((bf16[1184,256]{1,0:T(8,128)(2,1)S(1)}, bf16[1184,256]{1,0:T(8,128)(2,1)S(1)}, u32[]{:S(2)}, u32[]{:S(2)}) %collective-permute-start) | collective-permute-done | bytes 606240 | tf_op jit(solution)/shard_map/ppermute | solution.py:435
  23.5 1.3 %pack.2 = (bf16[400,256]{1,0:T(8,128)(2,1)S(1)}, bf16[400,256]{1,0:T(8,128)(2,1)S(1)}, bf16[400,256]{1,0:T(8,128)(2,1)S(1)}, bf16[400,256]{1,0:T(8,128)(2,1)S(1)...) custom-call(s32[16]{0:T(128)S(1)} %get-tuple-element.28.plan, ...), custom_call_target="tpu_custom_call" | custom-call | flops 1 | bytes 1 | tf_op jit(solution)/shard_map/pack/pallas_call | solution.py:264
  24.8 2.4 %collective-permute-start.7 = (bf16[400,256]{1,0:T(8,128)(2,1)S(1)}, bf16[400,256]{1,0:T(8,128)(2,1)S(1)}, u32[]{:S(2)}, u32[]{:S(2)}) collective-permute-start(bf16[400,256]{1,0:T(8,128)(2,1)S(1)} %get-tuple-element.44), channel_id=1, source_target_pairs={{0,9},{1,8},{2,11},{3,10},{4,13},{5,12},{6,15},{7,14},{8,1},{9,0},... | collective-permute-start | bytes 614408 | tf_op jit(solution)/shard_map/ppermute | solution.py:435
  27.2 0.3 collective-permute-start.8
  27.5 0.0 collective-permute-start.9
  27.5 0.0 collective-permute-start.11
  27.5 0.0 copy-start
  27.5 0.0 copy-start.1
  27.5 8.0 %attend.3 = (bf16[2,1152,1024]{2,1,0:T(8,128)(2,1)}, s32[1]{0:T(128)}) custom-call(s32[16]{0:T(128)S(1)} %get-tuple-element.28.plan, bf16[2,1152,1024]{2,1,0:T(8,128)(2,1)} %q_hbm.3, bf16[1184,256]{1,0:T(8,128)(2,1)S(1)} %get-tuple-element.32.after.refs_0_.own_ref, ...), custom_call_target="tpu_custom_call", output_to_operand_aliasing={{0}: (6, {})} | custom-call | flops 1 | bytes 1 | tf_op jit(solution)/shard_map/attend/pallas_call | solution.py:191
  35.5 1.0 %collective-permute-done.1.got_ref = bf16[1184,256]{1,0:T(8,128)(2,1)S(1)} collective-permute-done((bf16[1184,256]{1,0:T(8,128)(2,1)S(1)}, bf16[1184,256]{1,0:T(8,128)(2,1)S(1)}, u32[]{:S(2)}, u32[]{:S(2)}) %collective-permute-start.1) | collective-permute-done | bytes 606240 | tf_op jit(solution)/shard_map/ppermute | solution.py:435
  36.5 2.4 %pack.3 = (bf16[400,256]{1,0:T(8,128)(2,1)S(1)}, bf16[400,256]{1,0:T(8,128)(2,1)S(1)}, bf16[400,256]{1,0:T(8,128)(2,1)S(1)}, bf16[400,256]{1,0:T(8,128)(2,1)S(1)...) custom-call(s32[16]{0:T(128)S(1)} %get-tuple-element.28.plan, ...), custom_call_target="tpu_custom_call" | custom-call | flops 1 | bytes 1 | tf_op jit(solution)/shard_map/pack/pallas_call | solution.py:264
  39.0 2.1 %collective-permute-start.10 = (bf16[400,256]{1,0:T(8,128)(2,1)S(1)}, bf16[400,256]{1,0:T(8,128)(2,1)S(1)}, u32[]{:S(2)}, u32[]{:S(2)}) collective-permute-start(bf16[400,256]{1,0:T(8,128)(2,1)S(1)} %get-tuple-element.47), channel_id=1, source_target_pairs={{0,8},{1,9},{2,10},{3,11},{4,12},{5,13},{6,14},{7,15},{8,0},{9,1},... | collective-permute-start | bytes 614408 | tf_op jit(solution)/shard_map/ppermute | solution.py:435
  41.0 0.0 collective-permute-done.7.refs_0_
  41.0 1.2 %collective-permute-start.2 = (bf16[400,256]{1,0:T(8,128)(2,1)S(1)}, bf16[400,256]{1,0:T(8,128)(2,1)S(1)}, u32[]{:S(2)}, u32[]{:S(2)}) collective-permute-start(bf16[400,256]{1,0:T(8,128)(2,1)S(1)} %get-tuple-element.38), channel_id=1, source_target_pairs={{0,9},{1,8},{2,11},{3,10},{4,13},{5,12},{6,15},{7,14},{8,1},{9,0},... | collective-permute-start | bytes 614408 | tf_op jit(solution)/shard_map/ppermute | solution.py:435
  42.3 0.0 collective-permute-done.8.refs_1_
  42.3 0.2 collective-permute-start.3
  42.5 0.0 collective-permute-done.9.refs_2_
  42.5 0.3 collective-permute-start.4
  42.8 0.0 collective-permute-done.11.refs_5_
  42.8 1.3 %collective-permute-start.5 = (bf16[400,256]{1,0:T(8,128)(2,1)S(1)}, bf16[400,256]{1,0:T(8,128)(2,1)S(1)}, u32[]{:S(2)}, u32[]{:S(2)}) collective-permute-start(bf16[400,256]{1,0:T(8,128)(2,1)S(1)} %get-tuple-element.41), channel_id=1, source_target_pairs={{0,8},{1,9},{2,10},{3,11},{4,12},{5,13},{6,14},{7,15},{8,0},{9,1},... | collective-permute-start | bytes 614408 | tf_op jit(solution)/shard_map/ppermute | solution.py:435
  44.1 0.0 collective-permute-done.10.refs_3_
  44.1 1.3 %collective-permute-start.6 = (bf16[400,256]{1,0:T(8,128)(2,1)S(1)}, bf16[400,256]{1,0:T(8,128)(2,1)S(1)}, u32[]{:S(2)}, u32[]{:S(2)}) collective-permute-start(bf16[400,256]{1,0:T(8,128)(2,1)S(1)} %get-tuple-element.43), channel_id=1, source_target_pairs={{0,8},{1,9},{2,10},{3,11},{4,12},{5,13},{6,14},{7,15},{8,16},{9,17... | collective-permute-start | bytes 614408 | tf_op jit(solution)/shard_map/ppermute | solution.py:435
  45.5 0.0 copy-done
  45.5 0.0 copy-done.1
  45.5 2.0 %settle.2 = (bf16[3,2,384,512]{3,2,1,0:T(8,128)(2,1)}, f32[3,2,1024]{2,1,0:T(2,128)S(1)}) custom-call(s32[16]{0:T(128)S(1)} %get-tuple-element.28.plan, bf16[400,256]{1,0:T(8,128)(2,1)S(1)} %collective-permute-done.7.refs_0_, bf16[400,256]{1,0:T(8,128)(2,1)S(1)} %collective-permute-done.8.refs_1_, bf16[400,256]{1,0:T(8,128)(2,1)S(1)} %collective-permute-done.9.refs_2_, ...), custom_call_target="tpu_custom_call" | custom-call | flops 1 | bytes 1 | tf_op jit(solution)/shard_map/settle/pallas_call | solution.py:416
  47.5 3.4 %collective-permute-done.2.refs_0_ = bf16[400,256]{1,0:T(8,128)(2,1)S(1)} collective-permute-done((bf16[400,256]{1,0:T(8,128)(2,1)S(1)}, bf16[400,256]{1,0:T(8,128)(2,1)S(1)}, u32[]{:S(2)}, u32[]{:S(2)}) %collective-permute-start.2) | collective-permute-done | bytes 204832 | tf_op jit(solution)/shard_map/ppermute | solution.py:435
  50.9 3.3 %collective-permute-done.3.refs_1_ = bf16[400,256]{1,0:T(8,128)(2,1)S(1)} collective-permute-done((bf16[400,256]{1,0:T(8,128)(2,1)S(1)}, bf16[400,256]{1,0:T(8,128)(2,1)S(1)}, u32[]{:S(2)}, u32[]{:S(2)}) %collective-permute-start.3) | collective-permute-done | bytes 204832 | tf_op jit(solution)/shard_map/ppermute | solution.py:435
  54.2 2.5 %collective-permute-done.4.refs_2_ = bf16[400,256]{1,0:T(8,128)(2,1)S(1)} collective-permute-done((bf16[400,256]{1,0:T(8,128)(2,1)S(1)}, bf16[400,256]{1,0:T(8,128)(2,1)S(1)}, u32[]{:S(2)}, u32[]{:S(2)}) %collective-permute-start.4) | collective-permute-done | bytes 204832 | tf_op jit(solution)/shard_map/ppermute | solution.py:435
  56.6 0.0 collective-permute-done.5.refs_3_
  56.6 0.0 collective-permute-done.6.refs_5_
  56.6 2.7 %settle.3 = (bf16[3,2,384,512]{3,2,1,0:T(8,128)(2,1)}, bf16[3,2,2,1024]{3,2,1,0:T(2,128)(2,1)}) custom-call(s32[16]{0:T(128)S(1)} %get-tuple-element.28.plan, bf16[400,256]{1,0:T(8,128)(2,1)S(1)} %collective-permute-done.2.refs_0_, bf16[400,256]{1,0:T(8,128)(2,1)S(1)} %collective-permute-done.3.refs_1_, ...), custom_call_target="tpu_custom_call", output_to_operand_aliasing={{0}: (12, {})} | custom-call | flops 1 | bytes 1 | tf_op jit(solution)/shard_map/settle/pallas_call | solution.py:416
Async XLA Ops:
  2.6 20.9 %collective-permute-start = (bf16[1184,256]{1,0:T(8,128)(2,1)S(1)}, bf16[1184,256]{1,0:T(8,128)(2,1)S(1)}, u32[]{:S(2)}, u32[]{:S(2)}) collective-permute-start(bf16[1184,256]{1,0:T(8,128)(2,1)S(1)} %get-tuple-element.29.refs_0_.own_ref), channel_id=1, source_target_pairs={{0,16},{1,17},{2,18},{3,19},{4,20},{5,21},{6,22},{7,23},{8,24},{9,... | collective-permute-start | bytes 1818632 | tf_op jit(solution)/shard_map/ppermute | solution.py:435
  18.0 18.5 %collective-permute-start.1 = (bf16[1184,256]{1,0:T(8,128)(2,1)S(1)}, bf16[1184,256]{1,0:T(8,128)(2,1)S(1)}, u32[]{:S(2)}, u32[]{:S(2)}) collective-permute-start(bf16[1184,256]{1,0:T(8,128)(2,1)S(1)} %get-tuple-element.32.after.refs_0_.own_ref), channel_id=1, source_target_pairs={{0,16},{1,17},{2,18},{3,19},{4,20},{5,21},{6,22},{7,23},{8,24},{9,... | collective-permute-start | bytes 1818632 | tf_op jit(solution)/shard_map/ppermute | solution.py:435
  24.8 16.2 %collective-permute-start.7 = (bf16[400,256]{1,0:T(8,128)(2,1)S(1)}, bf16[400,256]{1,0:T(8,128)(2,1)S(1)}, u32[]{:S(2)}, u32[]{:S(2)}) collective-permute-start(bf16[400,256]{1,0:T(8,128)(2,1)S(1)} %get-tuple-element.44), channel_id=1, source_target_pairs={{0,9},{1,8},{2,11},{3,10},{4,13},{5,12},{6,15},{7,14},{8,1},{9,0},... | collective-permute-start | bytes 614408 | tf_op jit(solution)/shard_map/ppermute | solution.py:435
  27.2 15.0 %collective-permute-start.8 = (bf16[400,256]{1,0:T(8,128)(2,1)S(1)}, bf16[400,256]{1,0:T(8,128)(2,1)S(1)}, u32[]{:S(2)}, u32[]{:S(2)}) collective-permute-start(bf16[400,256]{1,0:T(8,128)(2,1)S(1)} %get-tuple-element.45), channel_id=1, source_target_pairs={{0,1},{1,0},{2,3},{3,2},{4,5},{5,4},{6,7},{7,6},{8,9},{9,8},{10,11... | collective-permute-start | bytes 614408 | tf_op jit(solution)/shard_map/ppermute | solution.py:435
  27.5 15.0 %collective-permute-start.9 = (bf16[400,256]{1,0:T(8,128)(2,1)S(1)}, bf16[400,256]{1,0:T(8,128)(2,1)S(1)}, u32[]{:S(2)}, u32[]{:S(2)}) collective-permute-start(bf16[400,256]{1,0:T(8,128)(2,1)S(1)} %get-tuple-element.46), channel_id=1, source_target_pairs={{0,9},{1,8},{2,11},{3,10},{4,13},{5,12},{6,15},{7,14},{8,17},{9,16... | collective-permute-start | bytes 614408 | tf_op jit(solution)/shard_map/ppermute | solution.py:435
  27.5 15.3 %collective-permute-start.11 = (bf16[400,256]{1,0:T(8,128)(2,1)S(1)}, bf16[400,256]{1,0:T(8,128)(2,1)S(1)}, u32[]{:S(2)}, u32[]{:S(2)}) collective-permute-start(bf16[400,256]{1,0:T(8,128)(2,1)S(1)} %get-tuple-element.48), channel_id=1, source_target_pairs={{0,8},{1,9},{2,10},{3,11},{4,12},{5,13},{6,14},{7,15},{8,16},{9,17... | collective-permute-start | bytes 614408 | tf_op jit(solution)/shard_map/ppermute | solution.py:435
  27.5 18.0 %copy-start = (bf16[3,2,2,1024]{3,2,1,0:T(2,128)(2,1)S(1)}, bf16[3,2,2,1024]{3,2,1,0:T(2,128)(2,1)}, u32[]{:S(2)}) copy-start(bf16[3,2,2,1024]{3,2,1,0:T(2,128)(2,1)} %refs_6_.3) | copy-start | bytes 73732
  27.5 18.0 %copy-start.1 = (bf16[3,2,2,256]{3,2,1,0:T(2,128)(2,1)S(1)}, bf16[3,2,2,256]{3,2,1,0:T(2,128)(2,1)}, u32[]{:S(2)}) copy-start(bf16[3,2,2,256]{3,2,1,0:T(2,128)(2,1)} %refs_7_.3) | copy-start | bytes 18436
  39.0 5.2 %collective-permute-start.10 = (bf16[400,256]{1,0:T(8,128)(2,1)S(1)}, bf16[400,256]{1,0:T(8,128)(2,1)S(1)}, u32[]{:S(2)}, u32[]{:S(2)}) collective-permute-start(bf16[400,256]{1,0:T(8,128)(2,1)S(1)} %get-tuple-element.47), channel_id=1, source_target_pairs={{0,8},{1,9},{2,10},{3,11},{4,12},{5,13},{6,14},{7,15},{8,0},{9,1},... | collective-permute-start | bytes 614408 | tf_op jit(solution)/shard_map/ppermute | solution.py:435
  41.0 9.8 %collective-permute-start.2 = (bf16[400,256]{1,0:T(8,128)(2,1)S(1)}, bf16[400,256]{1,0:T(8,128)(2,1)S(1)}, u32[]{:S(2)}, u32[]{:S(2)}) collective-permute-start(bf16[400,256]{1,0:T(8,128)(2,1)S(1)} %get-tuple-element.38), channel_id=1, source_target_pairs={{0,9},{1,8},{2,11},{3,10},{4,13},{5,12},{6,15},{7,14},{8,1},{9,0},... | collective-permute-start | bytes 614408 | tf_op jit(solution)/shard_map/ppermute | solution.py:435
  42.3 11.9 %collective-permute-start.3 = (bf16[400,256]{1,0:T(8,128)(2,1)S(1)}, bf16[400,256]{1,0:T(8,128)(2,1)S(1)}, u32[]{:S(2)}, u32[]{:S(2)}) collective-permute-start(bf16[400,256]{1,0:T(8,128)(2,1)S(1)} %get-tuple-element.39), channel_id=1, source_target_pairs={{0,1},{1,0},{2,3},{3,2},{4,5},{5,4},{6,7},{7,6},{8,9},{9,8},{10,11... | collective-permute-start | bytes 614408 | tf_op jit(solution)/shard_map/ppermute | solution.py:435
  42.5 14.1 %collective-permute-start.4 = (bf16[400,256]{1,0:T(8,128)(2,1)S(1)}, bf16[400,256]{1,0:T(8,128)(2,1)S(1)}, u32[]{:S(2)}, u32[]{:S(2)}) collective-permute-start(bf16[400,256]{1,0:T(8,128)(2,1)S(1)} %get-tuple-element.40), channel_id=1, source_target_pairs={{0,9},{1,8},{2,11},{3,10},{4,13},{5,12},{6,15},{7,14},{8,17},{9,16... | collective-permute-start | bytes 614408 | tf_op jit(solution)/shard_map/ppermute | solution.py:435
  42.8 13.8 %collective-permute-start.5 = (bf16[400,256]{1,0:T(8,128)(2,1)S(1)}, bf16[400,256]{1,0:T(8,128)(2,1)S(1)}, u32[]{:S(2)}, u32[]{:S(2)}) collective-permute-start(bf16[400,256]{1,0:T(8,128)(2,1)S(1)} %get-tuple-element.41), channel_id=1, source_target_pairs={{0,8},{1,9},{2,10},{3,11},{4,12},{5,13},{6,14},{7,15},{8,0},{9,1},... | collective-permute-start | bytes 614408 | tf_op jit(solution)/shard_map/ppermute | solution.py:435
  44.1 12.5 %collective-permute-start.6 = (bf16[400,256]{1,0:T(8,128)(2,1)S(1)}, bf16[400,256]{1,0:T(8,128)(2,1)S(1)}, u32[]{:S(2)}, u32[]{:S(2)}) collective-permute-start(bf16[400,256]{1,0:T(8,128)(2,1)S(1)} %get-tuple-element.43), channel_id=1, source_target_pairs={{0,8},{1,9},{2,10},{3,11},{4,12},{5,13},{6,14},{7,15},{8,16},{9,17... | collective-permute-start | bytes 614408 | tf_op jit(solution)/shard_map/ppermute | solution.py:435

commit v3 on v2

--- a/solution.py
+++ b/solution.py
@@ -168,7 +168,7 @@
 SMEM = pl.BlockSpec(memory_space=pltpu.SMEM)
 ANY = pl.BlockSpec(memory_space=pl.ANY)
 HBM = pl.BlockSpec(memory_space=pltpu.HBM)
-ORDER = (1, 3, 5, 0, 2, 4)
+ORDER = (5, 1, 3, 0, 2, 4)
 BRIEF = pl.CostEstimate(flops=1, bytes_accessed=1, transcendentals=0)
 
 
@@ -332,11 +332,11 @@
     )(*operands)
 
 
-def settle_kernel(plan, *refs, layer):
+def settle_kernel(*refs, layer):
     units, refs = [refs[ORDER.index(i)] for i in range(6)], refs[6:]
     q_ref, kv_ref, cos_ref, sin_ref = refs[:4]
     pool_ref, step_ref, sem = refs[-3:]
-    column = lax.rem(plan[PLACE_AT], 2)
+    column = lax.rem(lax.axis_index("tp"), 2)
 
     def copy(k, part):
         head = column if part == 0 else 1 - column
@@ -402,9 +402,9 @@
             copy(k, part).wait()
 
 
-def settle(plan, step_queries, step_kv, cosine, sine, units, earlier, layer):
-    in_specs = [SMEM] + [VMEM] * 10
-    operands = [plan, *(units[i] for i in ORDER), step_queries, step_kv, cosine, sine]
+def settle(step_queries, step_kv, cosine, sine, units, earlier, layer):
+    in_specs = [VMEM] * 10
+    operands = [*(units[i] for i in ORDER), step_queries, step_kv, cosine, sine]
     aliases = {}
     step = jax.ShapeDtypeStruct((NEAR, 2, GROUP * HD), jnp.float32)
     if earlier is not None:
@@ -454,9 +454,9 @@
     local, near_first, near_other, mid_other, far_same, far_other = pack(
         plan, slab, got, cosine, sine, later_slab
     )
+    far_other = moved(far_other, 1, 1)
     near_other = moved(near_other, None, 1)
     mid_other = moved(mid_other, 0, 1)
-    far_other = moved(far_other, 1, 1)
     far_same = moved(far_same, 1, 0)
     units = [None, near_other, local, mid_other, far_same, far_other]
 
@@ -465,13 +465,13 @@
         plan, later_slab, later_got, cosine, sine, mark, [near_first]
     )
     units[0] = moved(near_first, None, 0)
+    far_other = moved(far_other, 1, 1)
     near_other = moved(near_other, None, 1)
     mid_other = moved(mid_other, 0, 1)
-    far_other = moved(far_other, 1, 1)
     near_same = moved(near_same, None, 0)
     far_same = moved(far_same, 1, 0)
     later_units = [near_same, near_other, local, mid_other, far_same, far_other]
-    step = functools.partial(settle, plan, step_queries, step_kv, cosine, sine)
+    step = functools.partial(settle, step_queries, step_kv, cosine, sine)
     earlier = step(units, None, 0)
     pool, step = step(later_units, earlier, 1)
     return out, step, pool

time: 59.6 us -> 58.9 us (0.988)
  starting transfers between devices: 13.4 us -> 14.8 us
  waiting for transfers between devices: 13.9 us -> 12.6 us
  Pallas kernels: 31.3 us -> 30.3 us
    ppermute x12, starting transfers between devices: 13.4 us -> 14.8 us  [moved(): return lax.ppermute(value, ('grp', 'tp'), pairs)]
    ppermute x12, waiting for transfers between devices: 13.9 us -> 12.6 us  [moved(): return lax.ppermute(value, ('grp', 'tp'), pairs)]
    pallas_call x2, Pallas kernels: 4.75 us -> 3.71 us  [settle(): pl.pallas_call(functools.partial(settle_kernel, layer=layer), in_specs=in...]
  transfers between devices with their start and end apart: 12 -> 12, of which waited for: 5 -> 4; matrix products, arithmetic and copies ran while one was open for 0% -> 0% of each run, Pallas kernels for 45% -> 45%
where the time goes in v3:
time: 58.9 us; the launch traced here: 58.6 us
  Pallas kernels  30.3 us (51%)
  starting transfers between devices  14.8 us (25%)
  waiting for transfers between devices  12.6 us (21%)
  between operations  0.87 us (1%)
    pallas_call x2, Pallas kernels, attend(): pl.pallas_call(functools.partial(attend_kernel, first=first, count=count,...  20.8 us
    ppermute x12, starting transfers between devices, moved(): return lax.ppermute(value, ('grp', 'tp'), pairs)  14.8 us
    ppermute x12, waiting for transfers between devices, moved(): return lax.ppermute(value, ('grp', 'tp'), pairs)  12.6 us
    pallas_call x2, Pallas kernels, pack(): pl.pallas_call(pack_kernel, in_specs=[SMEM, VMEM, VMEM, VMEM, VMEM, ANY]...  3.74 us
    pallas_call x2, Pallas kernels, settle(): pl.pallas_call(functools.partial(settle_kernel, layer=layer), in_specs=in...  3.71 us
    pallas_call x1, Pallas kernels, cut(): pl.pallas_call(cut_kernel, in_specs=[HBM] * 6, out_specs=[VMEM, SMEM, VME...  1.97 us
  transfers between devices with their start and end apart: 12, of which 4 were waited for; matrix products, arithmetic and copies ran while one was open for 0% of the time, Pallas kernels for 45%

profile of v3, /device:TPU:1, one launch (start us, length us, event | category | flops | bytes accessed | tf_op | source)
XLA Modules:
  0.0 58.6 jit_solution(10380317807474795451)
XLA Ops:
  0.6 2.0 %cut.1 = (bf16[1184,256]{1,0:T(8,128)(2,1)S(1)}, s32[16]{0:T(128)S(1)}, f32[392,128]{1,0:T(8,128)S(1)}, f32[392,128]{1,0:T(8,128)S(1)}) custom-call(s32[3,3]{1,0:T(4,128)} %refs_0_.1, s32[3]{0:T(128)} %refs_1_.1, s32[3]{0:T(128)} %bitcast.1, bf16[2,1152,256]{2,1,0:T(8,128)(2,1)} %refs_3_.3, f32[392,128]{1,0:T(8,128)} %constant.4.clone.refs_4_, ...), custom_call_target="tpu_custom_call" | custom-call | flops 1 | bytes 1 | tf_op jit(solution)/shard_map/cut/pallas_call | solution.py:312
  2.6 2.5 %collective-permute-start = (bf16[1184,256]{1,0:T(8,128)(2,1)S(1)}, bf16[1184,256]{1,0:T(8,128)(2,1)S(1)}, u32[]{:S(2)}, u32[]{:S(2)}) collective-permute-start(bf16[1184,256]{1,0:T(8,128)(2,1)S(1)} %get-tuple-element.29.refs_0_.own_ref), channel_id=1, source_target_pairs={{0,16},{1,17},{2,18},{3,19},{4,20},{5,21},{6,22},{7,23},{8,24},{9,... | collective-permute-start | bytes 1818632 | tf_op jit(solution)/shard_map/ppermute | solution.py:435
  5.2 12.8 %attend.2 = (bf16[2,1152,1024]{2,1,0:T(8,128)(2,1)}, bf16[1184,256]{1,0:T(8,128)(2,1)S(1)}) custom-call(s32[16]{0:T(128)S(1)} %get-tuple-element.28.plan, bf16[2,1152,1024]{2,1,0:T(8,128)(2,1)} %q_hbm.3, bf16[1184,256]{1,0:T(8,128)(2,1)S(1)} %get-tuple-element.29.refs_0_.own_ref, f32[392,128]{1,0:T(8,128)S(1)} %get-tuple-element.30.refs_1_.cos_ref.refs_8_, ...), custom_call_target="tpu_custom_call" | custom-call | flops 1 | bytes 1 | tf_op jit(solution)/shard_map/attend/pallas_call | solution.py:191
  18.0 1.7 %collective-permute-start.1 = (bf16[1184,256]{1,0:T(8,128)(2,1)S(1)}, bf16[1184,256]{1,0:T(8,128)(2,1)S(1)}, u32[]{:S(2)}, u32[]{:S(2)}) collective-permute-start(bf16[1184,256]{1,0:T(8,128)(2,1)S(1)} %get-tuple-element.32.after.refs_0_.own_ref), channel_id=1, source_target_pairs={{0,16},{1,17},{2,18},{3,19},{4,20},{5,21},{6,22},{7,23},{8,24},{9,... | collective-permute-start | bytes 1818632 | tf_op jit(solution)/shard_map/ppermute | solution.py:435
  19.7 3.8 %collective-permute-done.got_ref = bf16[1184,256]{1,0:T(8,128)(2,1)S(1)} collective-permute-done((bf16[1184,256]{1,0:T(8,128)(2,1)S(1)}, bf16[1184,256]{1,0:T(8,128)(2,1)S(1)}, u32[]{:S(2)}, u32[]{:S(2)}) %collective-permute-start) | collective-permute-done | bytes 606240 | tf_op jit(solution)/shard_map/ppermute | solution.py:435
  23.5 1.3 %pack.2 = (bf16[400,256]{1,0:T(8,128)(2,1)S(1)}, bf16[400,256]{1,0:T(8,128)(2,1)S(1)}, bf16[400,256]{1,0:T(8,128)(2,1)S(1)}, bf16[400,256]{1,0:T(8,128)(2,1)S(1)...) custom-call(s32[16]{0:T(128)S(1)} %get-tuple-element.28.plan, ...), custom_call_target="tpu_custom_call" | custom-call | flops 1 | bytes 1 | tf_op jit(solution)/shard_map/pack/pallas_call | solution.py:264
  24.8 0.1 collective-permute-start.7
  24.9 2.4 %collective-permute-start.8 = (bf16[400,256]{1,0:T(8,128)(2,1)S(1)}, bf16[400,256]{1,0:T(8,128)(2,1)S(1)}, u32[]{:S(2)}, u32[]{:S(2)}) collective-permute-start(bf16[400,256]{1,0:T(8,128)(2,1)S(1)} %get-tuple-element.45), channel_id=1, source_target_pairs={{0,9},{1,8},{2,11},{3,10},{4,13},{5,12},{6,15},{7,14},{8,1},{9,0},... | collective-permute-start | bytes 614408 | tf_op jit(solution)/shard_map/ppermute | solution.py:435
  27.3 0.5 collective-permute-start.9
  27.9 1.8 %collective-permute-start.11 = (bf16[400,256]{1,0:T(8,128)(2,1)S(1)}, bf16[400,256]{1,0:T(8,128)(2,1)S(1)}, u32[]{:S(2)}, u32[]{:S(2)}) collective-permute-start(bf16[400,256]{1,0:T(8,128)(2,1)S(1)} %get-tuple-element.48), channel_id=1, source_target_pairs={{0,8},{1,9},{2,10},{3,11},{4,12},{5,13},{6,14},{7,15},{8,16},{9,17... | collective-permute-start | bytes 614408 | tf_op jit(solution)/shard_map/ppermute | solution.py:435
  29.7 0.0 copy-start
  29.7 0.0 copy-start.1
  29.7 8.0 %attend.3 = (bf16[2,1152,1024]{2,1,0:T(8,128)(2,1)}, s32[1]{0:T(128)}) custom-call(s32[16]{0:T(128)S(1)} %get-tuple-element.28.plan, bf16[2,1152,1024]{2,1,0:T(8,128)(2,1)} %q_hbm.3, bf16[1184,256]{1,0:T(8,128)(2,1)S(1)} %get-tuple-element.32.after.refs_0_.own_ref, ...), custom_call_target="tpu_custom_call", output_to_operand_aliasing={{0}: (6, {})} | custom-call | flops 1 | bytes 1 | tf_op jit(solution)/shard_map/attend/pallas_call | solution.py:191
  37.7 0.0 collective-permute-done.1.got_ref
  37.7 2.4 %pack.3 = (bf16[400,256]{1,0:T(8,128)(2,1)S(1)}, bf16[400,256]{1,0:T(8,128)(2,1)S(1)}, bf16[400,256]{1,0:T(8,128)(2,1)S(1)}, bf16[400,256]{1,0:T(8,128)(2,1)S(1)...) custom-call(s32[16]{0:T(128)S(1)} %get-tuple-element.28.plan, ...), custom_call_target="tpu_custom_call" | custom-call | flops 1 | bytes 1 | tf_op jit(solution)/shard_map/pack/pallas_call | solution.py:264
  40.1 0.9 %collective-permute-start.10 = (bf16[400,256]{1,0:T(8,128)(2,1)S(1)}, bf16[400,256]{1,0:T(8,128)(2,1)S(1)}, u32[]{:S(2)}, u32[]{:S(2)}) collective-permute-start(bf16[400,256]{1,0:T(8,128)(2,1)S(1)} %get-tuple-element.47), channel_id=1, source_target_pairs={{0,8},{1,9},{2,10},{3,11},{4,12},{5,13},{6,14},{7,15},{8,0},{9,1},... | collective-permute-start | bytes 614408 | tf_op jit(solution)/shard_map/ppermute | solution.py:435
  41.0 0.0 collective-permute-done.7.refs_0_
  41.0 0.3 collective-permute-start.2
  41.3 0.0 collective-permute-done.8.refs_1_
  41.3 1.5 %collective-permute-start.3 = (bf16[400,256]{1,0:T(8,128)(2,1)S(1)}, bf16[400,256]{1,0:T(8,128)(2,1)S(1)}, u32[]{:S(2)}, u32[]{:S(2)}) collective-permute-start(bf16[400,256]{1,0:T(8,128)(2,1)S(1)} %get-tuple-element.39), channel_id=1, source_target_pairs={{0,9},{1,8},{2,11},{3,10},{4,13},{5,12},{6,15},{7,14},{8,1},{9,0},... | collective-permute-start | bytes 614408 | tf_op jit(solution)/shard_map/ppermute | solution.py:435
  42.8 0.0 collective-permute-done.9.refs_2_
  42.8 1.2 %collective-permute-start.4 = (bf16[400,256]{1,0:T(8,128)(2,1)S(1)}, bf16[400,256]{1,0:T(8,128)(2,1)S(1)}, u32[]{:S(2)}, u32[]{:S(2)}) collective-permute-start(bf16[400,256]{1,0:T(8,128)(2,1)S(1)} %get-tuple-element.40), channel_id=1, source_target_pairs={{0,1},{1,0},{2,3},{3,2},{4,5},{5,4},{6,7},{7,6},{8,9},{9,8},{10,11... | collective-permute-start | bytes 614408 | tf_op jit(solution)/shard_map/ppermute | solution.py:435
  44.0 0.0 collective-permute-done.11.refs_5_
  44.0 0.0 collective-permute-start.5
  44.0 0.0 collective-permute-done.10.refs_3_
  44.0 1.8 %collective-permute-start.6 = (bf16[400,256]{1,0:T(8,128)(2,1)S(1)}, bf16[400,256]{1,0:T(8,128)(2,1)S(1)}, u32[]{:S(2)}, u32[]{:S(2)}) collective-permute-start(bf16[400,256]{1,0:T(8,128)(2,1)S(1)} %get-tuple-element.43), channel_id=1, source_target_pairs={{0,8},{1,9},{2,10},{3,11},{4,12},{5,13},{6,14},{7,15},{8,16},{9,17... | collective-permute-start | bytes 614408 | tf_op jit(solution)/shard_map/ppermute | solution.py:435
  45.8 0.0 copy-done
  45.9 0.0 copy-done.1
  45.9 1.5 %settle.2 = (bf16[3,2,384,512]{3,2,1,0:T(8,128)(2,1)}, f32[3,2,1024]{2,1,0:T(2,128)S(1)}) custom-call(bf16[400,256]{1,0:T(8,128)(2,1)S(1)} %collective-permute-done.7.refs_0_, bf16[400,256]{1,0:T(8,128)(2,1)S(1)} %collective-permute-done.8.refs_1_, bf16[400,256]{1,0:T(8,128)(2,1)S(1)} %collective-permute-done.9.refs_2_, ...), custom_call_target="tpu_custom_call" | custom-call | flops 1 | bytes 1 | tf_op jit(solution)/shard_map/settle/pallas_call | solution.py:416
  47.4 2.6 %collective-permute-done.2.refs_0_ = bf16[400,256]{1,0:T(8,128)(2,1)S(1)} collective-permute-done((bf16[400,256]{1,0:T(8,128)(2,1)S(1)}, bf16[400,256]{1,0:T(8,128)(2,1)S(1)}, u32[]{:S(2)}, u32[]{:S(2)}) %collective-permute-start.2) | collective-permute-done | bytes 204832 | tf_op jit(solution)/shard_map/ppermute | solution.py:435
  50.0 4.1 %collective-permute-done.3.refs_1_ = bf16[400,256]{1,0:T(8,128)(2,1)S(1)} collective-permute-done((bf16[400,256]{1,0:T(8,128)(2,1)S(1)}, bf16[400,256]{1,0:T(8,128)(2,1)S(1)}, u32[]{:S(2)}, u32[]{:S(2)}) %collective-permute-start.3) | collective-permute-done | bytes 204832 | tf_op jit(solution)/shard_map/ppermute | solution.py:435
  54.1 2.1 %collective-permute-done.4.refs_2_ = bf16[400,256]{1,0:T(8,128)(2,1)S(1)} collective-permute-done((bf16[400,256]{1,0:T(8,128)(2,1)S(1)}, bf16[400,256]{1,0:T(8,128)(2,1)S(1)}, u32[]{:S(2)}, u32[]{:S(2)}) %collective-permute-start.4) | collective-permute-done | bytes 204832 | tf_op jit(solution)/shard_map/ppermute | solution.py:435
  56.2 0.0 collective-permute-done.5.refs_3_
  56.2 0.0 collective-permute-done.6.refs_5_
  56.2 2.2 %settle.3 = (bf16[3,2,384,512]{3,2,1,0:T(8,128)(2,1)}, bf16[3,2,2,1024]{3,2,1,0:T(2,128)(2,1)}) custom-call(bf16[400,256]{1,0:T(8,128)(2,1)S(1)} %collective-permute-done.2.refs_0_, bf16[400,256]{1,0:T(8,128)(2,1)S(1)} %collective-permute-done.3.refs_1_, bf16[400,256]{1,0:T(8,128)(2,1)S(1)} %collective-permute-done.4.refs_2_, ...), custom_call_target="tpu_custom_call", output_to_operand_aliasing={{0}: (11, {})} | custom-call | flops 1 | bytes 1 | tf_op jit(solution)/shard_map/settle/pallas_call | solution.py:416
Async XLA Ops:
  2.6 20.9 %collective-permute-start = (bf16[1184,256]{1,0:T(8,128)(2,1)S(1)}, bf16[1184,256]{1,0:T(8,128)(2,1)S(1)}, u32[]{:S(2)}, u32[]{:S(2)}) collective-permute-start(bf16[1184,256]{1,0:T(8,128)(2,1)S(1)} %get-tuple-element.29.refs_0_.own_ref), channel_id=1, source_target_pairs={{0,16},{1,17},{2,18},{3,19},{4,20},{5,21},{6,22},{7,23},{8,24},{9,... | collective-permute-start | bytes 1818632 | tf_op jit(solution)/shard_map/ppermute | solution.py:435
  18.0 19.7 %collective-permute-start.1 = (bf16[1184,256]{1,0:T(8,128)(2,1)S(1)}, bf16[1184,256]{1,0:T(8,128)(2,1)S(1)}, u32[]{:S(2)}, u32[]{:S(2)}) collective-permute-start(bf16[1184,256]{1,0:T(8,128)(2,1)S(1)} %get-tuple-element.32.after.refs_0_.own_ref), channel_id=1, source_target_pairs={{0,16},{1,17},{2,18},{3,19},{4,20},{5,21},{6,22},{7,23},{8,24},{9,... | collective-permute-start | bytes 1818632 | tf_op jit(solution)/shard_map/ppermute | solution.py:435
  24.8 16.2 %collective-permute-start.7 = (bf16[400,256]{1,0:T(8,128)(2,1)S(1)}, bf16[400,256]{1,0:T(8,128)(2,1)S(1)}, u32[]{:S(2)}, u32[]{:S(2)}) collective-permute-start(bf16[400,256]{1,0:T(8,128)(2,1)S(1)} %get-tuple-element.44), channel_id=1, source_target_pairs={{0,9},{1,8},{2,11},{3,10},{4,13},{5,12},{6,15},{7,14},{8,17},{9,16... | collective-permute-start | bytes 614408 | tf_op jit(solution)/shard_map/ppermute | solution.py:435
  24.9 16.4 %collective-permute-start.8 = (bf16[400,256]{1,0:T(8,128)(2,1)S(1)}, bf16[400,256]{1,0:T(8,128)(2,1)S(1)}, u32[]{:S(2)}, u32[]{:S(2)}) collective-permute-start(bf16[400,256]{1,0:T(8,128)(2,1)S(1)} %get-tuple-element.45), channel_id=1, source_target_pairs={{0,9},{1,8},{2,11},{3,10},{4,13},{5,12},{6,15},{7,14},{8,1},{9,0},... | collective-permute-start | bytes 614408 | tf_op jit(solution)/shard_map/ppermute | solution.py:435
  27.3 15.5 %collective-permute-start.9 = (bf16[400,256]{1,0:T(8,128)(2,1)S(1)}, bf16[400,256]{1,0:T(8,128)(2,1)S(1)}, u32[]{:S(2)}, u32[]{:S(2)}) collective-permute-start(bf16[400,256]{1,0:T(8,128)(2,1)S(1)} %get-tuple-element.46), channel_id=1, source_target_pairs={{0,1},{1,0},{2,3},{3,2},{4,5},{5,4},{6,7},{7,6},{8,9},{9,8},{10,11... | collective-permute-start | bytes 614408 | tf_op jit(solution)/shard_map/ppermute | solution.py:435
  27.9 16.1 %collective-permute-start.11 = (bf16[400,256]{1,0:T(8,128)(2,1)S(1)}, bf16[400,256]{1,0:T(8,128)(2,1)S(1)}, u32[]{:S(2)}, u32[]{:S(2)}) collective-permute-start(bf16[400,256]{1,0:T(8,128)(2,1)S(1)} %get-tuple-element.48), channel_id=1, source_target_pairs={{0,8},{1,9},{2,10},{3,11},{4,12},{5,13},{6,14},{7,15},{8,16},{9,17... | collective-permute-start | bytes 614408 | tf_op jit(solution)/shard_map/ppermute | solution.py:435
  29.7 16.2 %copy-start = (bf16[3,2,2,1024]{3,2,1,0:T(2,128)(2,1)S(1)}, bf16[3,2,2,1024]{3,2,1,0:T(2,128)(2,1)}, u32[]{:S(2)}) copy-start(bf16[3,2,2,1024]{3,2,1,0:T(2,128)(2,1)} %refs_6_.3) | copy-start | bytes 73732
  29.7 16.2 %copy-start.1 = (bf16[3,2,2,256]{3,2,1,0:T(2,128)(2,1)S(1)}, bf16[3,2,2,256]{3,2,1,0:T(2,128)(2,1)}, u32[]{:S(2)}) copy-start(bf16[3,2,2,256]{3,2,1,0:T(2,128)(2,1)} %refs_7_.3) | copy-start | bytes 18436
  40.1 3.9 %collective-permute-start.10 = (bf16[400,256]{1,0:T(8,128)(2,1)S(1)}, bf16[400,256]{1,0:T(8,128)(2,1)S(1)}, u32[]{:S(2)}, u32[]{:S(2)}) collective-permute-start(bf16[400,256]{1,0:T(8,128)(2,1)S(1)} %get-tuple-element.47), channel_id=1, source_target_pairs={{0,8},{1,9},{2,10},{3,11},{4,12},{5,13},{6,14},{7,15},{8,0},{9,1},... | collective-permute-start | bytes 614408 | tf_op jit(solution)/shard_map/ppermute | solution.py:435
  41.0 8.9 %collective-permute-start.2 = (bf16[400,256]{1,0:T(8,128)(2,1)S(1)}, bf16[400,256]{1,0:T(8,128)(2,1)S(1)}, u32[]{:S(2)}, u32[]{:S(2)}) collective-permute-start(bf16[400,256]{1,0:T(8,128)(2,1)S(1)} %get-tuple-element.38), channel_id=1, source_target_pairs={{0,9},{1,8},{2,11},{3,10},{4,13},{5,12},{6,15},{7,14},{8,17},{9,16... | collective-permute-start | bytes 614408 | tf_op jit(solution)/shard_map/ppermute | solution.py:435
  41.3 12.7 %collective-permute-start.3 = (bf16[400,256]{1,0:T(8,128)(2,1)S(1)}, bf16[400,256]{1,0:T(8,128)(2,1)S(1)}, u32[]{:S(2)}, u32[]{:S(2)}) collective-permute-start(bf16[400,256]{1,0:T(8,128)(2,1)S(1)} %get-tuple-element.39), channel_id=1, source_target_pairs={{0,9},{1,8},{2,11},{3,10},{4,13},{5,12},{6,15},{7,14},{8,1},{9,0},... | collective-permute-start | bytes 614408 | tf_op jit(solution)/shard_map/ppermute | solution.py:435
  42.8 13.4 %collective-permute-start.4 = (bf16[400,256]{1,0:T(8,128)(2,1)S(1)}, bf16[400,256]{1,0:T(8,128)(2,1)S(1)}, u32[]{:S(2)}, u32[]{:S(2)}) collective-permute-start(bf16[400,256]{1,0:T(8,128)(2,1)S(1)} %get-tuple-element.40), channel_id=1, source_target_pairs={{0,1},{1,0},{2,3},{3,2},{4,5},{5,4},{6,7},{7,6},{8,9},{9,8},{10,11... | collective-permute-start | bytes 614408 | tf_op jit(solution)/shard_map/ppermute | solution.py:435
  44.0 12.2 %collective-permute-start.5 = (bf16[400,256]{1,0:T(8,128)(2,1)S(1)}, bf16[400,256]{1,0:T(8,128)(2,1)S(1)}, u32[]{:S(2)}, u32[]{:S(2)}) collective-permute-start(bf16[400,256]{1,0:T(8,128)(2,1)S(1)} %get-tuple-element.41), channel_id=1, source_target_pairs={{0,8},{1,9},{2,10},{3,11},{4,12},{5,13},{6,14},{7,15},{8,0},{9,1},... | collective-permute-start | bytes 614408 | tf_op jit(solution)/shard_map/ppermute | solution.py:435
  44.0 12.2 %collective-permute-start.6 = (bf16[400,256]{1,0:T(8,128)(2,1)S(1)}, bf16[400,256]{1,0:T(8,128)(2,1)S(1)}, u32[]{:S(2)}, u32[]{:S(2)}) collective-permute-start(bf16[400,256]{1,0:T(8,128)(2,1)S(1)} %get-tuple-element.43), channel_id=1, source_target_pairs={{0,8},{1,9},{2,10},{3,11},{4,12},{5,13},{6,14},{7,15},{8,16},{9,17... | collective-permute-start | bytes 614408 | tf_op jit(solution)/shard_map/ppermute | solution.py:435

commit v4 on v3

--- a/solution.py
+++ b/solution.py
@@ -86,7 +86,7 @@
         rows = pl.ds(POOL, PLAN_ROWS)
         slab_copies.append(pltpu.make_async_copy(kv_ref.at[rows], mark.at[rows], slab_sem.at[CUTS]))
     else:
-        mark[0] = 0
+        mark[...] = jnp.zeros_like(mark)
     width = GROUP * HD
 
     def place(i):
@@ -175,7 +175,7 @@
 def attend(plan, queries, slab, cosine, sine, first, count, supply=None, earlier=None, after=()):
     operands = [plan, queries, slab, cosine, sine]
     in_specs = [SMEM, HBM, VMEM, VMEM, VMEM]
-    mark = jax.ShapeDtypeStruct((1,), jnp.int32)
+    mark = jax.ShapeDtypeStruct((8, HD), jnp.int32)
     if supply is not None:
         operands.append(supply)
         in_specs.append(HBM)
@@ -191,7 +191,7 @@
     return pl.pallas_call(
         functools.partial(attend_kernel, first=first, count=count, supply=supply is not None),
         in_specs=in_specs,
-        out_specs=[HBM, SMEM if supply is None else VMEM],
+        out_specs=[HBM, VMEM],
         scratch_shapes=[
             pltpu.VMEM(pages, jnp.bfloat16),
             pltpu.VMEM(pages, jnp.bfloat16),
@@ -224,9 +224,13 @@
     out_ref[PROMPT:, :] = held.astype(jnp.bfloat16)
 
 
-def pack_kernel(plan, own_ref, got_ref, cos_ref, sin_ref, after, *refs):
-    core = plan[PLACE_AT] // 2
-    column = lax.rem(plan[PLACE_AT], 2)
+def pack_kernel(plan_any, own_ref, got_ref, cos_ref, sin_ref, after, *refs):
+    plan, plan_sem = refs[-2:]
+    refs = refs[:-2]
+    plan_copy = pltpu.make_async_copy(plan_any, plan, plan_sem)
+    plan_copy.start()
+    core = lax.rem(lax.axis_index("grp"), 2)
+    column = lax.rem(lax.axis_index("tp"), 2)
     copy = None
     if len(refs) == 10:
         copy = pltpu.make_async_copy(refs[0], refs[7], refs[9])
@@ -243,6 +247,12 @@
         plan2[LENGTHS_AT + r] = 2 * numbers[LENGTHS_AT + r] + numbers[TARGETS_AT + r]
         plan2[TARGETS_AT + r] = numbers[PLACE_AT + r]
 
+    write(local, got_ref, *picked(plan2, 1, column))
+    write(mid_other, got_ref, *picked(plan2, 1, 1 - column))
+    write(far_same, got_ref, *picked(plan2, 2, column))
+    write(far_other, got_ref, *picked(plan2, 2, 1 - column))
+    plan_copy.wait()
+
     @pl.when(core == 0)
     def _():
         write(near_same, own_ref, *picked(plan, 0, column))
@@ -253,20 +263,21 @@
         write(near_same, got_ref, *picked(plan2, 0, column))
         write(near_other, got_ref, *picked(plan2, 0, 1 - column))
 
-    write(local, got_ref, *picked(plan2, 1, column))
-    write(mid_other, got_ref, *picked(plan2, 1, 1 - column))
-    write(far_same, got_ref, *picked(plan2, 2, column))
-    write(far_other, got_ref, *picked(plan2, 2, 1 - column))
     if copy is not None:
         copy.wait()
 
 def pack(plan, own, got, cosine, sine, after, kept=()):
     return pl.pallas_call(
         pack_kernel,
-        in_specs=[SMEM, VMEM, VMEM, VMEM, VMEM, ANY] + [VMEM] * len(kept),
+        in_specs=[ANY, VMEM, VMEM, VMEM, VMEM, ANY] + [VMEM] * len(kept),
         out_specs=[VMEM] * (6 + len(kept)),
         out_shape=[jax.ShapeDtypeStruct((UNIT, 2 * HD), jnp.bfloat16)] * (6 + len(kept)),
-        scratch_shapes=[pltpu.SMEM((16,), jnp.int32), pltpu.SemaphoreType.DMA],
+        scratch_shapes=[
+            pltpu.SMEM((16,), jnp.int32),
+            pltpu.SemaphoreType.DMA,
+            pltpu.SMEM((16,), jnp.int32),
+            pltpu.SemaphoreType.DMA,
+        ],
         cost_estimate=BRIEF,
         compiler_params=pltpu.CompilerParams(vmem_limit_bytes=VMEM_LIMIT),
         name="pack",

time: 58.9 us -> 58 us (0.985)
  Pallas kernels: 30.3 us -> 28.1 us
  waiting for transfers between devices: 12.6 us -> 14.1 us
    pallas_call x2, Pallas kernels: 3.74 us -> 2.11 us  [pack(): pl.pallas_call(pack_kernel, in_specs=[ANY, VMEM, VMEM, VMEM, VMEM, ANY] +...]
    ppermute x12, waiting for transfers between devices: 12.6 us -> 14.1 us  [moved(): return lax.ppermute(value, ('grp', 'tp'), pairs)]
  transfers between devices with their start and end apart: 12 -> 12, of which waited for: 4 -> 4; matrix products, arithmetic and copies ran while one was open for 0% -> 0% of each run, Pallas kernels for 45% -> 41%
where the time goes in v4:
time: 58 us; the launch traced here: 57.9 us
  Pallas kernels  28.1 us (48%)
  starting transfers between devices  14.8 us (26%)
  waiting for transfers between devices  14.1 us (24%)
  between operations  0.87 us (2%)
    pallas_call x2, Pallas kernels, attend(): pl.pallas_call(functools.partial(attend_kernel, first=first, count=count,...  20.3 us
    ppermute x12, starting transfers between devices, moved(): return lax.ppermute(value, ('grp', 'tp'), pairs)  14.8 us
    ppermute x12, waiting for transfers between devices, moved(): return lax.ppermute(value, ('grp', 'tp'), pairs)  14.1 us
    pallas_call x2, Pallas kernels, settle(): pl.pallas_call(functools.partial(settle_kernel, layer=layer), in_specs=in...  3.71 us
    pallas_call x2, Pallas kernels, pack(): pl.pallas_call(pack_kernel, in_specs=[ANY, VMEM, VMEM, VMEM, VMEM, ANY] +...  2.11 us
    pallas_call x1, Pallas kernels, cut(): pl.pallas_call(cut_kernel, in_specs=[HBM] * 6, out_specs=[VMEM, SMEM, VME...  1.97 us
  transfers between devices with their start and end apart: 12, of which 4 were waited for; matrix products, arithmetic and copies ran while one was open for 0% of the time, Pallas kernels for 41%

profile of v4, /device:TPU:1, one launch (start us, length us, event | category | flops | bytes accessed | tf_op | source)
XLA Modules:
  0.0 57.9 jit_solution(14890121982170105040)
XLA Ops:
  0.6 2.0 %cut.1 = (bf16[1184,256]{1,0:T(8,128)(2,1)S(1)}, s32[16]{0:T(128)S(1)}, f32[392,128]{1,0:T(8,128)S(1)}, f32[392,128]{1,0:T(8,128)S(1)}) custom-call(s32[3,3]{1,0:T(4,128)} %refs_0_.1, s32[3]{0:T(128)} %refs_1_.1, s32[3]{0:T(128)} %bitcast.1, bf16[2,1152,256]{2,1,0:T(8,128)(2,1)} %refs_3_.3, f32[392,128]{1,0:T(8,128)} %constant.4.clone.refs_4_, ...), custom_call_target="tpu_custom_call" | custom-call | flops 1 | bytes 1 | tf_op jit(solution)/shard_map/cut/pallas_call | solution.py:323
  2.6 2.5 %collective-permute-start = (bf16[1184,256]{1,0:T(8,128)(2,1)S(1)}, bf16[1184,256]{1,0:T(8,128)(2,1)S(1)}, u32[]{:S(2)}, u32[]{:S(2)}) collective-permute-start(bf16[1184,256]{1,0:T(8,128)(2,1)S(1)} %get-tuple-element.29.refs_0_.own_ref), channel_id=1, source_target_pairs={{0,16},{1,17},{2,18},{3,19},{4,20},{5,21},{6,22},{7,23},{8,24},{9,... | collective-permute-start | bytes 1818632 | tf_op jit(solution)/shard_map/ppermute | solution.py:446
  5.2 12.8 %attend.2 = (bf16[2,1152,1024]{2,1,0:T(8,128)(2,1)}, bf16[1184,256]{1,0:T(8,128)(2,1)S(1)}) custom-call(s32[16]{0:T(128)S(1)} %get-tuple-element.28.plan.plan_any, bf16[2,1152,1024]{2,1,0:T(8,128)(2,1)} %q_hbm.3, bf16[1184,256]{1,0:T(8,128)(2,1)S(1)} %get-tuple-element.29.refs_0_.own_ref, f32[392,128]{1,0:T(8,128)S(1)} %get-tuple-element.30.refs_1_.cos_ref.refs_8_, ...), custom_call_target="tpu_custom_call" | custom-call | flops 1 | bytes 1 | tf_op jit(solution)/shard_map/attend/pallas_call | solution.py:191
  18.0 1.7 %collective-permute-start.1 = (bf16[1184,256]{1,0:T(8,128)(2,1)S(1)}, bf16[1184,256]{1,0:T(8,128)(2,1)S(1)}, u32[]{:S(2)}, u32[]{:S(2)}) collective-permute-start(bf16[1184,256]{1,0:T(8,128)(2,1)S(1)} %get-tuple-element.32.after.refs_0_.own_ref), channel_id=1, source_target_pairs={{0,16},{1,17},{2,18},{3,19},{4,20},{5,21},{6,22},{7,23},{8,24},{9,... | collective-permute-start | bytes 1818632 | tf_op jit(solution)/shard_map/ppermute | solution.py:446
  19.7 3.8 %collective-permute-done.got_ref = bf16[1184,256]{1,0:T(8,128)(2,1)S(1)} collective-permute-done((bf16[1184,256]{1,0:T(8,128)(2,1)S(1)}, bf16[1184,256]{1,0:T(8,128)(2,1)S(1)}, u32[]{:S(2)}, u32[]{:S(2)}) %collective-permute-start) | collective-permute-done | bytes 606240 | tf_op jit(solution)/shard_map/ppermute | solution.py:446
  23.5 1.0 %pack.2 = (bf16[400,256]{1,0:T(8,128)(2,1)S(1)}, bf16[400,256]{1,0:T(8,128)(2,1)S(1)}, bf16[400,256]{1,0:T(8,128)(2,1)S(1)}, bf16[400,256]{1,0:T(8,128)(2,1)S(1)...) custom-call(s32[16]{0:T(128)S(1)} %get-tuple-element.28.plan.plan_any, ...), custom_call_target="tpu_custom_call" | custom-call | flops 1 | bytes 1 | tf_op jit(solution)/shard_map/pack/pallas_call | solution.py:270
  24.5 0.1 collective-permute-start.7
  24.6 2.4 %collective-permute-start.8 = (bf16[400,256]{1,0:T(8,128)(2,1)S(1)}, bf16[400,256]{1,0:T(8,128)(2,1)S(1)}, u32[]{:S(2)}, u32[]{:S(2)}) collective-permute-start(bf16[400,256]{1,0:T(8,128)(2,1)S(1)} %get-tuple-element.45), channel_id=1, source_target_pairs={{0,9},{1,8},{2,11},{3,10},{4,13},{5,12},{6,15},{7,14},{8,1},{9,0},... | collective-permute-start | bytes 614408 | tf_op jit(solution)/shard_map/ppermute | solution.py:446
  27.0 0.5 collective-permute-start.9
  27.6 1.8 %collective-permute-start.11 = (bf16[400,256]{1,0:T(8,128)(2,1)S(1)}, bf16[400,256]{1,0:T(8,128)(2,1)S(1)}, u32[]{:S(2)}, u32[]{:S(2)}) collective-permute-start(bf16[400,256]{1,0:T(8,128)(2,1)S(1)} %get-tuple-element.48), channel_id=1, source_target_pairs={{0,8},{1,9},{2,10},{3,11},{4,12},{5,13},{6,14},{7,15},{8,16},{9,17... | collective-permute-start | bytes 614408 | tf_op jit(solution)/shard_map/ppermute | solution.py:446
  29.4 0.0 copy-start
  29.4 0.0 copy-start.1
  29.4 7.5 %attend.3 = (bf16[2,1152,1024]{2,1,0:T(8,128)(2,1)}, s32[8,128]{1,0:T(8,128)S(1)}) custom-call(s32[16]{0:T(128)S(1)} %get-tuple-element.28.plan.plan_any, bf16[2,1152,1024]{2,1,0:T(8,128)(2,1)} %q_hbm.3, bf16[1184,256]{1,0:T(8,128)(2,1)S(1)} %get-tuple-element.32.after.refs_0_.own_ref, ...), custom_call_target="tpu_custom_call", output_to_operand_aliasing={{0}: (6, {})} | custom-call | flops 1 | bytes 1 | tf_op jit(solution)/shard_map/attend/pallas_call | solution.py:191
  36.9 0.0 collective-permute-done.1.got_ref
  36.9 1.1 %pack.3 = (bf16[400,256]{1,0:T(8,128)(2,1)S(1)}, bf16[400,256]{1,0:T(8,128)(2,1)S(1)}, bf16[400,256]{1,0:T(8,128)(2,1)S(1)}, bf16[400,256]{1,0:T(8,128)(2,1)S(1)...) custom-call(s32[16]{0:T(128)S(1)} %get-tuple-element.28.plan.plan_any, ...), custom_call_target="tpu_custom_call" | custom-call | flops 1 | bytes 1 | tf_op jit(solution)/shard_map/pack/pallas_call | solution.py:270
  38.0 1.7 %collective-permute-start.10 = (bf16[400,256]{1,0:T(8,128)(2,1)S(1)}, bf16[400,256]{1,0:T(8,128)(2,1)S(1)}, u32[]{:S(2)}, u32[]{:S(2)}) collective-permute-start(bf16[400,256]{1,0:T(8,128)(2,1)S(1)} %get-tuple-element.47), channel_id=1, source_target_pairs={{0,8},{1,9},{2,10},{3,11},{4,12},{5,13},{6,14},{7,15},{8,0},{9,1},... | collective-permute-start | bytes 614408 | tf_op jit(solution)/shard_map/ppermute | solution.py:446
  39.7 0.0 collective-permute-done.7.refs_0_
  39.7 0.0 collective-permute-start.2
  39.7 0.0 collective-permute-done.8.refs_1_
  39.7 1.7 %collective-permute-start.3 = (bf16[400,256]{1,0:T(8,128)(2,1)S(1)}, bf16[400,256]{1,0:T(8,128)(2,1)S(1)}, u32[]{:S(2)}, u32[]{:S(2)}) collective-permute-start(bf16[400,256]{1,0:T(8,128)(2,1)S(1)} %get-tuple-element.39), channel_id=1, source_target_pairs={{0,9},{1,8},{2,11},{3,10},{4,13},{5,12},{6,15},{7,14},{8,1},{9,0},... | collective-permute-start | bytes 614408 | tf_op jit(solution)/shard_map/ppermute | solution.py:446
  41.4 0.0 collective-permute-done.9.refs_2_
  41.4 1.9 %collective-permute-start.4 = (bf16[400,256]{1,0:T(8,128)(2,1)S(1)}, bf16[400,256]{1,0:T(8,128)(2,1)S(1)}, u32[]{:S(2)}, u32[]{:S(2)}) collective-permute-start(bf16[400,256]{1,0:T(8,128)(2,1)S(1)} %get-tuple-element.40), channel_id=1, source_target_pairs={{0,1},{1,0},{2,3},{3,2},{4,5},{5,4},{6,7},{7,6},{8,9},{9,8},{10,11... | collective-permute-start | bytes 614408 | tf_op jit(solution)/shard_map/ppermute | solution.py:446
  43.3 0.0 collective-permute-done.11.refs_5_
  43.3 0.0 collective-permute-start.5
  43.3 0.0 collective-permute-done.10.refs_3_
  43.3 0.4 collective-permute-start.6
  43.7 0.0 copy-done
  43.7 0.0 copy-done.1
  43.7 1.5 %settle.2 = (bf16[3,2,384,512]{3,2,1,0:T(8,128)(2,1)}, f32[3,2,1024]{2,1,0:T(2,128)S(1)}) custom-call(bf16[400,256]{1,0:T(8,128)(2,1)S(1)} %collective-permute-done.7.refs_0_, bf16[400,256]{1,0:T(8,128)(2,1)S(1)} %collective-permute-done.8.refs_1_, bf16[400,256]{1,0:T(8,128)(2,1)S(1)} %collective-permute-done.9.refs_2_, ...), custom_call_target="tpu_custom_call" | custom-call | flops 1 | bytes 1 | tf_op jit(solution)/shard_map/settle/pallas_call | solution.py:427
  45.3 0.4 collective-permute-done.2.refs_0_
  45.7 6.3 %collective-permute-done.3.refs_1_ = bf16[400,256]{1,0:T(8,128)(2,1)S(1)} collective-permute-done((bf16[400,256]{1,0:T(8,128)(2,1)S(1)}, bf16[400,256]{1,0:T(8,128)(2,1)S(1)}, u32[]{:S(2)}, u32[]{:S(2)}) %collective-permute-start.3) | collective-permute-done | bytes 204832 | tf_op jit(solution)/shard_map/ppermute | solution.py:446
  52.0 3.6 %collective-permute-done.4.refs_2_ = bf16[400,256]{1,0:T(8,128)(2,1)S(1)} collective-permute-done((bf16[400,256]{1,0:T(8,128)(2,1)S(1)}, bf16[400,256]{1,0:T(8,128)(2,1)S(1)}, u32[]{:S(2)}, u32[]{:S(2)}) %collective-permute-start.4) | collective-permute-done | bytes 204832 | tf_op jit(solution)/shard_map/ppermute | solution.py:446
  55.6 0.0 collective-permute-done.5.refs_3_
  55.6 0.0 collective-permute-done.6.refs_5_
  55.6 2.2 %settle.3 = (bf16[3,2,384,512]{3,2,1,0:T(8,128)(2,1)}, bf16[3,2,2,1024]{3,2,1,0:T(2,128)(2,1)}) custom-call(bf16[400,256]{1,0:T(8,128)(2,1)S(1)} %collective-permute-done.2.refs_0_, bf16[400,256]{1,0:T(8,128)(2,1)S(1)} %collective-permute-done.3.refs_1_, bf16[400,256]{1,0:T(8,128)(2,1)S(1)} %collective-permute-done.4.refs_2_, ...), custom_call_target="tpu_custom_call", output_to_operand_aliasing={{0}: (11, {})} | custom-call | flops 1 | bytes 1 | tf_op jit(solution)/shard_map/settle/pallas_call | solution.py:427
Async XLA Ops:
  2.6 20.9 %collective-permute-start = (bf16[1184,256]{1,0:T(8,128)(2,1)S(1)}, bf16[1184,256]{1,0:T(8,128)(2,1)S(1)}, u32[]{:S(2)}, u32[]{:S(2)}) collective-permute-start(bf16[1184,256]{1,0:T(8,128)(2,1)S(1)} %get-tuple-element.29.refs_0_.own_ref), channel_id=1, source_target_pairs={{0,16},{1,17},{2,18},{3,19},{4,20},{5,21},{6,22},{7,23},{8,24},{9,... | collective-permute-start | bytes 1818632 | tf_op jit(solution)/shard_map/ppermute | solution.py:446
  18.0 18.9 %collective-permute-start.1 = (bf16[1184,256]{1,0:T(8,128)(2,1)S(1)}, bf16[1184,256]{1,0:T(8,128)(2,1)S(1)}, u32[]{:S(2)}, u32[]{:S(2)}) collective-permute-start(bf16[1184,256]{1,0:T(8,128)(2,1)S(1)} %get-tuple-element.32.after.refs_0_.own_ref), channel_id=1, source_target_pairs={{0,16},{1,17},{2,18},{3,19},{4,20},{5,21},{6,22},{7,23},{8,24},{9,... | collective-permute-start | bytes 1818632 | tf_op jit(solution)/shard_map/ppermute | solution.py:446
  24.5 15.1 %collective-permute-start.7 = (bf16[400,256]{1,0:T(8,128)(2,1)S(1)}, bf16[400,256]{1,0:T(8,128)(2,1)S(1)}, u32[]{:S(2)}, u32[]{:S(2)}) collective-permute-start(bf16[400,256]{1,0:T(8,128)(2,1)S(1)} %get-tuple-element.44), channel_id=1, source_target_pairs={{0,9},{1,8},{2,11},{3,10},{4,13},{5,12},{6,15},{7,14},{8,17},{9,16... | collective-permute-start | bytes 614408 | tf_op jit(solution)/shard_map/ppermute | solution.py:446
  24.6 15.1 %collective-permute-start.8 = (bf16[400,256]{1,0:T(8,128)(2,1)S(1)}, bf16[400,256]{1,0:T(8,128)(2,1)S(1)}, u32[]{:S(2)}, u32[]{:S(2)}) collective-permute-start(bf16[400,256]{1,0:T(8,128)(2,1)S(1)} %get-tuple-element.45), channel_id=1, source_target_pairs={{0,9},{1,8},{2,11},{3,10},{4,13},{5,12},{6,15},{7,14},{8,1},{9,0},... | collective-permute-start | bytes 614408 | tf_op jit(solution)/shard_map/ppermute | solution.py:446
  27.0 14.4 %collective-permute-start.9 = (bf16[400,256]{1,0:T(8,128)(2,1)S(1)}, bf16[400,256]{1,0:T(8,128)(2,1)S(1)}, u32[]{:S(2)}, u32[]{:S(2)}) collective-permute-start(bf16[400,256]{1,0:T(8,128)(2,1)S(1)} %get-tuple-element.46), channel_id=1, source_target_pairs={{0,1},{1,0},{2,3},{3,2},{4,5},{5,4},{6,7},{7,6},{8,9},{9,8},{10,11... | collective-permute-start | bytes 614408 | tf_op jit(solution)/shard_map/ppermute | solution.py:446
  27.6 15.7 %collective-permute-start.11 = (bf16[400,256]{1,0:T(8,128)(2,1)S(1)}, bf16[400,256]{1,0:T(8,128)(2,1)S(1)}, u32[]{:S(2)}, u32[]{:S(2)}) collective-permute-start(bf16[400,256]{1,0:T(8,128)(2,1)S(1)} %get-tuple-element.48), channel_id=1, source_target_pairs={{0,8},{1,9},{2,10},{3,11},{4,12},{5,13},{6,14},{7,15},{8,16},{9,17... | collective-permute-start | bytes 614408 | tf_op jit(solution)/shard_map/ppermute | solution.py:446
  29.4 14.4 %copy-start = (bf16[3,2,2,1024]{3,2,1,0:T(2,128)(2,1)S(1)}, bf16[3,2,2,1024]{3,2,1,0:T(2,128)(2,1)}, u32[]{:S(2)}) copy-start(bf16[3,2,2,1024]{3,2,1,0:T(2,128)(2,1)} %refs_6_.3) | copy-start | bytes 73732
  29.4 14.4 %copy-start.1 = (bf16[3,2,2,256]{3,2,1,0:T(2,128)(2,1)S(1)}, bf16[3,2,2,256]{3,2,1,0:T(2,128)(2,1)}, u32[]{:S(2)}) copy-start(bf16[3,2,2,256]{3,2,1,0:T(2,128)(2,1)} %refs_7_.3) | copy-start | bytes 18436
  38.0 5.3 %collective-permute-start.10 = (bf16[400,256]{1,0:T(8,128)(2,1)S(1)}, bf16[400,256]{1,0:T(8,128)(2,1)S(1)}, u32[]{:S(2)}, u32[]{:S(2)}) collective-permute-start(bf16[400,256]{1,0:T(8,128)(2,1)S(1)} %get-tuple-element.47), channel_id=1, source_target_pairs={{0,8},{1,9},{2,10},{3,11},{4,12},{5,13},{6,14},{7,15},{8,0},{9,1},... | collective-permute-start | bytes 614408 | tf_op jit(solution)/shard_map/ppermute | solution.py:446
  39.7 6.0 %collective-permute-start.2 = (bf16[400,256]{1,0:T(8,128)(2,1)S(1)}, bf16[400,256]{1,0:T(8,128)(2,1)S(1)}, u32[]{:S(2)}, u32[]{:S(2)}) collective-permute-start(bf16[400,256]{1,0:T(8,128)(2,1)S(1)} %get-tuple-element.38), channel_id=1, source_target_pairs={{0,9},{1,8},{2,11},{3,10},{4,13},{5,12},{6,15},{7,14},{8,17},{9,16... | collective-permute-start | bytes 614408 | tf_op jit(solution)/shard_map/ppermute | solution.py:446
  39.7 12.3 %collective-permute-start.3 = (bf16[400,256]{1,0:T(8,128)(2,1)S(1)}, bf16[400,256]{1,0:T(8,128)(2,1)S(1)}, u32[]{:S(2)}, u32[]{:S(2)}) collective-permute-start(bf16[400,256]{1,0:T(8,128)(2,1)S(1)} %get-tuple-element.39), channel_id=1, source_target_pairs={{0,9},{1,8},{2,11},{3,10},{4,13},{5,12},{6,15},{7,14},{8,1},{9,0},... | collective-permute-start | bytes 614408 | tf_op jit(solution)/shard_map/ppermute | solution.py:446
  41.4 14.1 %collective-permute-start.4 = (bf16[400,256]{1,0:T(8,128)(2,1)S(1)}, bf16[400,256]{1,0:T(8,128)(2,1)S(1)}, u32[]{:S(2)}, u32[]{:S(2)}) collective-permute-start(bf16[400,256]{1,0:T(8,128)(2,1)S(1)} %get-tuple-element.40), channel_id=1, source_target_pairs={{0,1},{1,0},{2,3},{3,2},{4,5},{5,4},{6,7},{7,6},{8,9},{9,8},{10,11... | collective-permute-start | bytes 614408 | tf_op jit(solution)/shard_map/ppermute | solution.py:446
  43.3 12.3 %collective-permute-start.5 = (bf16[400,256]{1,0:T(8,128)(2,1)S(1)}, bf16[400,256]{1,0:T(8,128)(2,1)S(1)}, u32[]{:S(2)}, u32[]{:S(2)}) collective-permute-start(bf16[400,256]{1,0:T(8,128)(2,1)S(1)} %get-tuple-element.41), channel_id=1, source_target_pairs={{0,8},{1,9},{2,10},{3,11},{4,12},{5,13},{6,14},{7,15},{8,0},{9,1},... | collective-permute-start | bytes 614408 | tf_op jit(solution)/shard_map/ppermute | solution.py:446
  43.3 12.3 %collective-permute-start.6 = (bf16[400,256]{1,0:T(8,128)(2,1)S(1)}, bf16[400,256]{1,0:T(8,128)(2,1)S(1)}, u32[]{:S(2)}, u32[]{:S(2)}) collective-permute-start(bf16[400,256]{1,0:T(8,128)(2,1)S(1)} %get-tuple-element.43), channel_id=1, source_target_pairs={{0,8},{1,9},{2,10},{3,11},{4,12},{5,13},{6,14},{7,15},{8,16},{9,17... | collective-permute-start | bytes 614408 | tf_op jit(solution)/shard_map/ppermute | solution.py:446

commit v5 on v4

--- a/solution.py
+++ b/solution.py
@@ -286,7 +286,7 @@
 
 def cut_kernel(*refs):
     page_hbm, lengths_hbm, targets_hbm, source, cos_hbm, sin_hbm = refs[:6]
-    slab, plan, cos_ref, sin_ref, sem, page_table, lengths, targets, int_sem = refs[6:]
+    slab, plan_out, cos_ref, sin_ref, sem, page_table, lengths, targets, int_sem, plan = refs[6:]
     ints = [
         pltpu.make_async_copy(page_hbm, page_table, int_sem.at[0]),
         pltpu.make_async_copy(lengths_hbm, lengths, int_sem.at[1]),
@@ -305,6 +305,8 @@
         plan[LENGTHS_AT + r] = lengths[r]
         plan[TARGETS_AT + r] = targets[r]
     plan[PLACE_AT] = lax.rem(lax.axis_index("grp"), 2) * 2 + lax.rem(lax.axis_index("tp"), 2)
+    copies.append(pltpu.make_async_copy(plan, plan_out, int_sem.at[3]))
+    copies[-1].start()
     halves = [plan[LENGTHS_AT + r] // 2 for r in range(PROMPTS_DEV)]
     numbers = [plan[r] for r in range(LENGTHS_AT)] + halves
     numbers += [plan[LENGTHS_AT + r] - 2 * halves[r] for r in range(PROMPTS_DEV)]
@@ -323,13 +325,14 @@
     return pl.pallas_call(
         cut_kernel,
         in_specs=[HBM] * 6,
-        out_specs=[VMEM, SMEM, VMEM, VMEM],
+        out_specs=[VMEM, HBM, VMEM, VMEM],
         scratch_shapes=[
             pltpu.SemaphoreType.DMA((CUTS + 2,)),
             pltpu.SMEM((PROMPTS_DEV, PAGES_P), jnp.int32),
             pltpu.SMEM((PROMPTS_DEV,), jnp.int32),
             pltpu.SMEM((PROMPTS_DEV,), jnp.int32),
-            pltpu.SemaphoreType.DMA((3,)),
+            pltpu.SemaphoreType.DMA((4,)),
+            pltpu.SMEM((16,), jnp.int32),
         ],
         out_shape=[
             jax.ShapeDtypeStruct((POOL + PLAN_ROWS, 2 * HD), jnp.bfloat16),

time: 58 us -> 57.6 us (level)
  transfers between devices with their start and end apart: 12 -> 12, of which waited for: 4 -> 4; matrix products, arithmetic and copies ran while one was open for 0% -> 0% of each run, Pallas kernels for 41% -> 42%
where the time goes in v5:
time: 57.6 us; the launch traced here: 57.5 us
  Pallas kernels  27.7 us (48%)
  starting transfers between devices  14.8 us (26%)
  waiting for transfers between devices  14.1 us (24%)
  between operations  0.87 us (2%)
    pallas_call x2, Pallas kernels, attend(): pl.pallas_call(functools.partial(attend_kernel, first=first, count=count,...  20.3 us
    ppermute x12, starting transfers between devices, moved(): return lax.ppermute(value, ('grp', 'tp'), pairs)  14.8 us
    ppermute x12, waiting for transfers between devices, moved(): return lax.ppermute(value, ('grp', 'tp'), pairs)  14.1 us
    pallas_call x2, Pallas kernels, settle(): pl.pallas_call(functools.partial(settle_kernel, layer=layer), in_specs=in...  3.71 us
    pallas_call x2, Pallas kernels, pack(): pl.pallas_call(pack_kernel, in_specs=[ANY, VMEM, VMEM, VMEM, VMEM, ANY] +...  2.11 us
    pallas_call x1, Pallas kernels, cut(): pl.pallas_call(cut_kernel, in_specs=[HBM] * 6, out_specs=[VMEM, HBM, VMEM...  1.56 us
  transfers between devices with their start and end apart: 12, of which 4 were waited for; matrix products, arithmetic and copies ran while one was open for 0% of the time, Pallas kernels for 42%

profile of v5, /device:TPU:1, one launch (start us, length us, event | category | flops | bytes accessed | tf_op | source)
XLA Modules:
  0.0 57.5 jit_solution(4987205092167843148)
XLA Ops:
  0.6 1.6 %cut.1 = (bf16[1184,256]{1,0:T(8,128)(2,1)S(1)}, s32[16]{0:T(128)S(1)}, f32[392,128]{1,0:T(8,128)S(1)}, f32[392,128]{1,0:T(8,128)S(1)}) custom-call(s32[3,3]{1,0:T(4,128)} %refs_0_.1, s32[3]{0:T(128)} %refs_1_.1, s32[3]{0:T(128)} %bitcast.1, bf16[2,1152,256]{2,1,0:T(8,128)(2,1)} %refs_3_.3, f32[392,128]{1,0:T(8,128)} %constant.4.clone.refs_4_, ...), custom_call_target="tpu_custom_call" | custom-call | flops 1 | bytes 1 | tf_op jit(solution)/shard_map/cut/pallas_call | solution.py:325
  2.2 2.5 %collective-permute-start = (bf16[1184,256]{1,0:T(8,128)(2,1)S(1)}, bf16[1184,256]{1,0:T(8,128)(2,1)S(1)}, u32[]{:S(2)}, u32[]{:S(2)}) collective-permute-start(bf16[1184,256]{1,0:T(8,128)(2,1)S(1)} %get-tuple-element.29.refs_0_.own_ref), channel_id=1, source_target_pairs={{0,16},{1,17},{2,18},{3,19},{4,20},{5,21},{6,22},{7,23},{8,24},{9,... | collective-permute-start | bytes 1818632 | tf_op jit(solution)/shard_map/ppermute | solution.py:449
  4.7 12.8 %attend.2 = (bf16[2,1152,1024]{2,1,0:T(8,128)(2,1)}, bf16[1184,256]{1,0:T(8,128)(2,1)S(1)}) custom-call(s32[16]{0:T(128)S(1)} %get-tuple-element.28.plan.plan_any, bf16[2,1152,1024]{2,1,0:T(8,128)(2,1)} %q_hbm.3, bf16[1184,256]{1,0:T(8,128)(2,1)S(1)} %get-tuple-element.29.refs_0_.own_ref, f32[392,128]{1,0:T(8,128)S(1)} %get-tuple-element.30.refs_1_.cos_ref.refs_8_, ...), custom_call_target="tpu_custom_call" | custom-call | flops 1 | bytes 1 | tf_op jit(solution)/shard_map/attend/pallas_call | solution.py:191
  17.6 1.7 %collective-permute-start.1 = (bf16[1184,256]{1,0:T(8,128)(2,1)S(1)}, bf16[1184,256]{1,0:T(8,128)(2,1)S(1)}, u32[]{:S(2)}, u32[]{:S(2)}) collective-permute-start(bf16[1184,256]{1,0:T(8,128)(2,1)S(1)} %get-tuple-element.32.after.refs_0_.own_ref), channel_id=1, source_target_pairs={{0,16},{1,17},{2,18},{3,19},{4,20},{5,21},{6,22},{7,23},{8,24},{9,... | collective-permute-start | bytes 1818632 | tf_op jit(solution)/shard_map/ppermute | solution.py:449
  19.3 3.8 %collective-permute-done.got_ref = bf16[1184,256]{1,0:T(8,128)(2,1)S(1)} collective-permute-done((bf16[1184,256]{1,0:T(8,128)(2,1)S(1)}, bf16[1184,256]{1,0:T(8,128)(2,1)S(1)}, u32[]{:S(2)}, u32[]{:S(2)}) %collective-permute-start) | collective-permute-done | bytes 606240 | tf_op jit(solution)/shard_map/ppermute | solution.py:449
  23.1 1.0 %pack.2 = (bf16[400,256]{1,0:T(8,128)(2,1)S(1)}, bf16[400,256]{1,0:T(8,128)(2,1)S(1)}, bf16[400,256]{1,0:T(8,128)(2,1)S(1)}, bf16[400,256]{1,0:T(8,128)(2,1)S(1)...) custom-call(s32[16]{0:T(128)S(1)} %get-tuple-element.28.plan.plan_any, ...), custom_call_target="tpu_custom_call" | custom-call | flops 1 | bytes 1 | tf_op jit(solution)/shard_map/pack/pallas_call | solution.py:270
  24.1 0.1 collective-permute-start.7
  24.2 2.4 %collective-permute-start.8 = (bf16[400,256]{1,0:T(8,128)(2,1)S(1)}, bf16[400,256]{1,0:T(8,128)(2,1)S(1)}, u32[]{:S(2)}, u32[]{:S(2)}) collective-permute-start(bf16[400,256]{1,0:T(8,128)(2,1)S(1)} %get-tuple-element.45), channel_id=1, source_target_pairs={{0,9},{1,8},{2,11},{3,10},{4,13},{5,12},{6,15},{7,14},{8,1},{9,0},... | collective-permute-start | bytes 614408 | tf_op jit(solution)/shard_map/ppermute | solution.py:449
  26.6 0.5 collective-permute-start.9
  27.2 1.8 %collective-permute-start.11 = (bf16[400,256]{1,0:T(8,128)(2,1)S(1)}, bf16[400,256]{1,0:T(8,128)(2,1)S(1)}, u32[]{:S(2)}, u32[]{:S(2)}) collective-permute-start(bf16[400,256]{1,0:T(8,128)(2,1)S(1)} %get-tuple-element.48), channel_id=1, source_target_pairs={{0,8},{1,9},{2,10},{3,11},{4,12},{5,13},{6,14},{7,15},{8,16},{9,17... | collective-permute-start | bytes 614408 | tf_op jit(solution)/shard_map/ppermute | solution.py:449
  29.0 0.0 copy-start
  29.0 0.0 copy-start.1
  29.0 7.5 %attend.3 = (bf16[2,1152,1024]{2,1,0:T(8,128)(2,1)}, s32[8,128]{1,0:T(8,128)S(1)}) custom-call(s32[16]{0:T(128)S(1)} %get-tuple-element.28.plan.plan_any, bf16[2,1152,1024]{2,1,0:T(8,128)(2,1)} %q_hbm.3, bf16[1184,256]{1,0:T(8,128)(2,1)S(1)} %get-tuple-element.32.after.refs_0_.own_ref, ...), custom_call_target="tpu_custom_call", output_to_operand_aliasing={{0}: (6, {})} | custom-call | flops 1 | bytes 1 | tf_op jit(solution)/shard_map/attend/pallas_call | solution.py:191
  36.5 0.0 collective-permute-done.1.got_ref
  36.5 1.1 %pack.3 = (bf16[400,256]{1,0:T(8,128)(2,1)S(1)}, bf16[400,256]{1,0:T(8,128)(2,1)S(1)}, bf16[400,256]{1,0:T(8,128)(2,1)S(1)}, bf16[400,256]{1,0:T(8,128)(2,1)S(1)...) custom-call(s32[16]{0:T(128)S(1)} %get-tuple-element.28.plan.plan_any, ...), custom_call_target="tpu_custom_call" | custom-call | flops 1 | bytes 1 | tf_op jit(solution)/shard_map/pack/pallas_call | solution.py:270
  37.6 1.7 %collective-permute-start.10 = (bf16[400,256]{1,0:T(8,128)(2,1)S(1)}, bf16[400,256]{1,0:T(8,128)(2,1)S(1)}, u32[]{:S(2)}, u32[]{:S(2)}) collective-permute-start(bf16[400,256]{1,0:T(8,128)(2,1)S(1)} %get-tuple-element.47), channel_id=1, source_target_pairs={{0,8},{1,9},{2,10},{3,11},{4,12},{5,13},{6,14},{7,15},{8,0},{9,1},... | collective-permute-start | bytes 614408 | tf_op jit(solution)/shard_map/ppermute | solution.py:449
  39.3 0.0 collective-permute-done.7.refs_0_
  39.3 0.0 collective-permute-start.2
  39.3 0.0 collective-permute-done.8.refs_1_
  39.3 1.7 %collective-permute-start.3 = (bf16[400,256]{1,0:T(8,128)(2,1)S(1)}, bf16[400,256]{1,0:T(8,128)(2,1)S(1)}, u32[]{:S(2)}, u32[]{:S(2)}) collective-permute-start(bf16[400,256]{1,0:T(8,128)(2,1)S(1)} %get-tuple-element.39), channel_id=1, source_target_pairs={{0,9},{1,8},{2,11},{3,10},{4,13},{5,12},{6,15},{7,14},{8,1},{9,0},... | collective-permute-start | bytes 614408 | tf_op jit(solution)/shard_map/ppermute | solution.py:449
  41.0 0.0 collective-permute-done.9.refs_2_
  41.0 1.9 %collective-permute-start.4 = (bf16[400,256]{1,0:T(8,128)(2,1)S(1)}, bf16[400,256]{1,0:T(8,128)(2,1)S(1)}, u32[]{:S(2)}, u32[]{:S(2)}) collective-permute-start(bf16[400,256]{1,0:T(8,128)(2,1)S(1)} %get-tuple-element.40), channel_id=1, source_target_pairs={{0,1},{1,0},{2,3},{3,2},{4,5},{5,4},{6,7},{7,6},{8,9},{9,8},{10,11... | collective-permute-start | bytes 614408 | tf_op jit(solution)/shard_map/ppermute | solution.py:449
  42.9 0.0 collective-permute-done.11.refs_5_
  42.9 0.0 collective-permute-start.5
  42.9 0.0 collective-permute-done.10.refs_3_
  42.9 0.4 collective-permute-start.6
  43.3 0.0 copy-done
  43.3 0.0 copy-done.1
  43.3 1.5 %settle.2 = (bf16[3,2,384,512]{3,2,1,0:T(8,128)(2,1)}, f32[3,2,1024]{2,1,0:T(2,128)S(1)}) custom-call(bf16[400,256]{1,0:T(8,128)(2,1)S(1)} %collective-permute-done.7.refs_0_, bf16[400,256]{1,0:T(8,128)(2,1)S(1)} %collective-permute-done.8.refs_1_, bf16[400,256]{1,0:T(8,128)(2,1)S(1)} %collective-permute-done.9.refs_2_, ...), custom_call_target="tpu_custom_call" | custom-call | flops 1 | bytes 1 | tf_op jit(solution)/shard_map/settle/pallas_call | solution.py:430
  44.9 0.4 collective-permute-done.2.refs_0_
  45.3 6.3 %collective-permute-done.3.refs_1_ = bf16[400,256]{1,0:T(8,128)(2,1)S(1)} collective-permute-done((bf16[400,256]{1,0:T(8,128)(2,1)S(1)}, bf16[400,256]{1,0:T(8,128)(2,1)S(1)}, u32[]{:S(2)}, u32[]{:S(2)}) %collective-permute-start.3) | collective-permute-done | bytes 204832 | tf_op jit(solution)/shard_map/ppermute | solution.py:449
  51.6 3.6 %collective-permute-done.4.refs_2_ = bf16[400,256]{1,0:T(8,128)(2,1)S(1)} collective-permute-done((bf16[400,256]{1,0:T(8,128)(2,1)S(1)}, bf16[400,256]{1,0:T(8,128)(2,1)S(1)}, u32[]{:S(2)}, u32[]{:S(2)}) %collective-permute-start.4) | collective-permute-done | bytes 204832 | tf_op jit(solution)/shard_map/ppermute | solution.py:449
  55.2 0.0 collective-permute-done.5.refs_3_
  55.2 0.0 collective-permute-done.6.refs_5_
  55.2 2.2 %settle.3 = (bf16[3,2,384,512]{3,2,1,0:T(8,128)(2,1)}, bf16[3,2,2,1024]{3,2,1,0:T(2,128)(2,1)}) custom-call(bf16[400,256]{1,0:T(8,128)(2,1)S(1)} %collective-permute-done.2.refs_0_, bf16[400,256]{1,0:T(8,128)(2,1)S(1)} %collective-permute-done.3.refs_1_, bf16[400,256]{1,0:T(8,128)(2,1)S(1)} %collective-permute-done.4.refs_2_, ...), custom_call_target="tpu_custom_call", output_to_operand_aliasing={{0}: (11, {})} | custom-call | flops 1 | bytes 1 | tf_op jit(solution)/shard_map/settle/pallas_call | solution.py:430
Async XLA Ops:
  2.2 20.9 %collective-permute-start = (bf16[1184,256]{1,0:T(8,128)(2,1)S(1)}, bf16[1184,256]{1,0:T(8,128)(2,1)S(1)}, u32[]{:S(2)}, u32[]{:S(2)}) collective-permute-start(bf16[1184,256]{1,0:T(8,128)(2,1)S(1)} %get-tuple-element.29.refs_0_.own_ref), channel_id=1, source_target_pairs={{0,16},{1,17},{2,18},{3,19},{4,20},{5,21},{6,22},{7,23},{8,24},{9,... | collective-permute-start | bytes 1818632 | tf_op jit(solution)/shard_map/ppermute | solution.py:449
  17.6 18.9 %collective-permute-start.1 = (bf16[1184,256]{1,0:T(8,128)(2,1)S(1)}, bf16[1184,256]{1,0:T(8,128)(2,1)S(1)}, u32[]{:S(2)}, u32[]{:S(2)}) collective-permute-start(bf16[1184,256]{1,0:T(8,128)(2,1)S(1)} %get-tuple-element.32.after.refs_0_.own_ref), channel_id=1, source_target_pairs={{0,16},{1,17},{2,18},{3,19},{4,20},{5,21},{6,22},{7,23},{8,24},{9,... | collective-permute-start | bytes 1818632 | tf_op jit(solution)/shard_map/ppermute | solution.py:449
  24.1 15.1 %collective-permute-start.7 = (bf16[400,256]{1,0:T(8,128)(2,1)S(1)}, bf16[400,256]{1,0:T(8,128)(2,1)S(1)}, u32[]{:S(2)}, u32[]{:S(2)}) collective-permute-start(bf16[400,256]{1,0:T(8,128)(2,1)S(1)} %get-tuple-element.44), channel_id=1, source_target_pairs={{0,9},{1,8},{2,11},{3,10},{4,13},{5,12},{6,15},{7,14},{8,17},{9,16... | collective-permute-start | bytes 614408 | tf_op jit(solution)/shard_map/ppermute | solution.py:449
  24.2 15.0 %collective-permute-start.8 = (bf16[400,256]{1,0:T(8,128)(2,1)S(1)}, bf16[400,256]{1,0:T(8,128)(2,1)S(1)}, u32[]{:S(2)}, u32[]{:S(2)}) collective-permute-start(bf16[400,256]{1,0:T(8,128)(2,1)S(1)} %get-tuple-element.45), channel_id=1, source_target_pairs={{0,9},{1,8},{2,11},{3,10},{4,13},{5,12},{6,15},{7,14},{8,1},{9,0},... | collective-permute-start | bytes 614408 | tf_op jit(solution)/shard_map/ppermute | solution.py:449
  26.6 14.4 %collective-permute-start.9 = (bf16[400,256]{1,0:T(8,128)(2,1)S(1)}, bf16[400,256]{1,0:T(8,128)(2,1)S(1)}, u32[]{:S(2)}, u32[]{:S(2)}) collective-permute-start(bf16[400,256]{1,0:T(8,128)(2,1)S(1)} %get-tuple-element.46), channel_id=1, source_target_pairs={{0,1},{1,0},{2,3},{3,2},{4,5},{5,4},{6,7},{7,6},{8,9},{9,8},{10,11... | collective-permute-start | bytes 614408 | tf_op jit(solution)/shard_map/ppermute | solution.py:449
  27.2 15.7 %collective-permute-start.11 = (bf16[400,256]{1,0:T(8,128)(2,1)S(1)}, bf16[400,256]{1,0:T(8,128)(2,1)S(1)}, u32[]{:S(2)}, u32[]{:S(2)}) collective-permute-start(bf16[400,256]{1,0:T(8,128)(2,1)S(1)} %get-tuple-element.48), channel_id=1, source_target_pairs={{0,8},{1,9},{2,10},{3,11},{4,12},{5,13},{6,14},{7,15},{8,16},{9,17... | collective-permute-start | bytes 614408 | tf_op jit(solution)/shard_map/ppermute | solution.py:449
  29.0 14.4 %copy-start = (bf16[3,2,2,1024]{3,2,1,0:T(2,128)(2,1)S(1)}, bf16[3,2,2,1024]{3,2,1,0:T(2,128)(2,1)}, u32[]{:S(2)}) copy-start(bf16[3,2,2,1024]{3,2,1,0:T(2,128)(2,1)} %refs_6_.3) | copy-start | bytes 73732
  29.0 14.4 %copy-start.1 = (bf16[3,2,2,256]{3,2,1,0:T(2,128)(2,1)S(1)}, bf16[3,2,2,256]{3,2,1,0:T(2,128)(2,1)}, u32[]{:S(2)}) copy-start(bf16[3,2,2,256]{3,2,1,0:T(2,128)(2,1)} %refs_7_.3) | copy-start | bytes 18436
  37.6 5.3 %collective-permute-start.10 = (bf16[400,256]{1,0:T(8,128)(2,1)S(1)}, bf16[400,256]{1,0:T(8,128)(2,1)S(1)}, u32[]{:S(2)}, u32[]{:S(2)}) collective-permute-start(bf16[400,256]{1,0:T(8,128)(2,1)S(1)} %get-tuple-element.47), channel_id=1, source_target_pairs={{0,8},{1,9},{2,10},{3,11},{4,12},{5,13},{6,14},{7,15},{8,0},{9,1},... | collective-permute-start | bytes 614408 | tf_op jit(solution)/shard_map/ppermute | solution.py:449
  39.3 6.0 %collective-permute-start.2 = (bf16[400,256]{1,0:T(8,128)(2,1)S(1)}, bf16[400,256]{1,0:T(8,128)(2,1)S(1)}, u32[]{:S(2)}, u32[]{:S(2)}) collective-permute-start(bf16[400,256]{1,0:T(8,128)(2,1)S(1)} %get-tuple-element.38), channel_id=1, source_target_pairs={{0,9},{1,8},{2,11},{3,10},{4,13},{5,12},{6,15},{7,14},{8,17},{9,16... | collective-permute-start | bytes 614408 | tf_op jit(solution)/shard_map/ppermute | solution.py:449
  39.3 12.3 %collective-permute-start.3 = (bf16[400,256]{1,0:T(8,128)(2,1)S(1)}, bf16[400,256]{1,0:T(8,128)(2,1)S(1)}, u32[]{:S(2)}, u32[]{:S(2)}) collective-permute-start(bf16[400,256]{1,0:T(8,128)(2,1)S(1)} %get-tuple-element.39), channel_id=1, source_target_pairs={{0,9},{1,8},{2,11},{3,10},{4,13},{5,12},{6,15},{7,14},{8,1},{9,0},... | collective-permute-start | bytes 614408 | tf_op jit(solution)/shard_map/ppermute | solution.py:449
  41.0 14.1 %collective-permute-start.4 = (bf16[400,256]{1,0:T(8,128)(2,1)S(1)}, bf16[400,256]{1,0:T(8,128)(2,1)S(1)}, u32[]{:S(2)}, u32[]{:S(2)}) collective-permute-start(bf16[400,256]{1,0:T(8,128)(2,1)S(1)} %get-tuple-element.40), channel_id=1, source_target_pairs={{0,1},{1,0},{2,3},{3,2},{4,5},{5,4},{6,7},{7,6},{8,9},{9,8},{10,11... | collective-permute-start | bytes 614408 | tf_op jit(solution)/shard_map/ppermute | solution.py:449
  42.9 12.3 %collective-permute-start.5 = (bf16[400,256]{1,0:T(8,128)(2,1)S(1)}, bf16[400,256]{1,0:T(8,128)(2,1)S(1)}, u32[]{:S(2)}, u32[]{:S(2)}) collective-permute-start(bf16[400,256]{1,0:T(8,128)(2,1)S(1)} %get-tuple-element.41), channel_id=1, source_target_pairs={{0,8},{1,9},{2,10},{3,11},{4,12},{5,13},{6,14},{7,15},{8,0},{9,1},... | collective-permute-start | bytes 614408 | tf_op jit(solution)/shard_map/ppermute | solution.py:449
  42.9 12.3 %collective-permute-start.6 = (bf16[400,256]{1,0:T(8,128)(2,1)S(1)}, bf16[400,256]{1,0:T(8,128)(2,1)S(1)}, u32[]{:S(2)}, u32[]{:S(2)}) collective-permute-start(bf16[400,256]{1,0:T(8,128)(2,1)S(1)} %get-tuple-element.43), channel_id=1, source_target_pairs={{0,8},{1,9},{2,10},{3,11},{4,12},{5,13},{6,14},{7,15},{8,16},{9,17... | collective-permute-start | bytes 614408 | tf_op jit(solution)/shard_map/ppermute | solution.py:449
